TPU v7x, 32 devices: a whole 2x2x4 slice. The times are simulated.
32 devices in a mesh: narrow: 4 (over y, x), wide: 8 (over z, core).
Axes of the slice: x: 2, y: 2, z: 4, core: 2. Of those that a mesh axis runs over, the one named last changes fastest.
Arguments:
- tokens: float32 [32768, 1152], P(('narrow', 'wide')), may hold values from -6 to 6
- conditioning: bfloat16 [128, 1152], P(('narrow', 'wide')), may hold values from -6 to 6
- row_items: int32 [32], P(('narrow', 'wide')), may hold values from 1 to 4, as said below
- head_mask: int32 [128, 16], P(('narrow', 'wide')), may hold values 0 or 1
- chan_mask: int32 [128, 32], P(('narrow', 'wide')), may hold values 0 or 1
- skip_mask: int32 [32768], P(('narrow', 'wide')), may hold values 0 or 1
- ada_weight: bfloat16 [1152, 6912], P(None, ('narrow', 'wide')), may hold values from -0.25 to 0.25
- ada_bias: bfloat16 [6912], P(('narrow', 'wide')), may hold values from -3 to 3
- qkv_weight: bfloat16 [1152, 3456], P(('narrow', 'wide')), may hold values from -0.1875 to 0.1875
- query_bias: bfloat16 [1152], replicated, may hold values from -3 to 3
- value_bias: bfloat16 [1152], replicated, may hold values from -3 to 3
- proj_weight: bfloat16 [1152, 1152], P(('narrow', 'wide')), may hold values from -3.5 to 3.5
- proj_bias: bfloat16 [1152], replicated, may hold values from -3 to 3
- fc1_weight: bfloat16 [4608, 1152], P('wide', 'narrow'), may hold values from -0.1875 to 0.1875
- fc1_bias: bfloat16 [4608], replicated, may hold values from -3 to 3
- fc2_weight: bfloat16 [4608, 1152], P('wide', 'narrow'), may hold values from -0.5 to 0.5
- fc2_bias: bfloat16 [1152], replicated, may hold values from -3 to 3
- head_router: bfloat16 [1152, 16], replicated, may hold values from -0.375 to 0.375
- head_router_bias: bfloat16 [16], replicated, may hold values from -3 to 3
- chan_router: bfloat16 [1152, 32], replicated, may hold values from -0.375 to 0.375
- chan_router_bias: bfloat16 [32], replicated, may hold values from -3 to 3
- token_router: bfloat16 [1152], replicated, may hold values from -0.1875 to 0.1875
- cotangent: float32 [32768, 1152], P(('narrow', 'wide')), may hold values from -6 to 6
Outputs:
- output: float32 [32768, 1152], P(('narrow', 'wide'))
- grad_tokens: float32 [32768, 1152], P(('narrow', 'wide'))
- grad_ada_weight: float32 [1152, 6912], P(None, ('narrow', 'wide'))
- grad_ada_bias: float32 [6912], P(('narrow', 'wide'))
- grad_qkv_weight: float32 [1152, 3456], P(('narrow', 'wide'))
- grad_query_bias: float32 [1152], replicated
- grad_value_bias: float32 [1152], replicated
- grad_proj_weight: float32 [1152, 1152], P(('narrow', 'wide'))
- grad_proj_bias: float32 [1152], replicated
- grad_fc1_weight: float32 [4608, 1152], P('wide', 'narrow')
- grad_fc1_bias: float32 [4608], replicated
- grad_fc2_weight: float32 [4608, 1152], P('wide', 'narrow')
- grad_fc2_bias: float32 [1152], replicated
- grad_head_router: float32 [1152, 16], replicated
- grad_head_router_bias: float32 [16], replicated
- grad_chan_router: float32 [1152, 32], replicated
- grad_chan_router_bias: float32 [32], replicated
- grad_token_router: float32 [1152], replicated
Inputs may be any that keep to these rules, and one draw needn't show every extreme that they name: `row_items`: each row holds 1 or 4 items of equal length; exactly half of the rows hold one item. Slots of a one-item row beyond the first are not read.
All inputs are finite; a program needn't handle non-finite values. No bound on the sum of `head_mask` or of `chan_mask` or of `skip_mask` on one device may be relied on, other than what follows from the above.
Results may differ from a plain program's by a relative error of at most 0.018.
The roundings to bfloat16 on the way count: a program that leaves them out, or rounds other values in their place, can miss the bound.
Values may be sent and summed in bfloat16 or wider, within the bound.
A program may use at most 448 MiB of HBM per device.

v0:
```python
import jax
import jax.numpy as jnp
from jax import lax
from jax.sharding import PartitionSpec as P

HIGHEST = lax.Precision.HIGHEST
EPSILON = 1e-06
MASKED = -1e30


def layer_norm(values):
    centered = values - jnp.mean(values, axis=-1, keepdims=True)
    variance = jnp.mean(centered * centered, axis=-1, keepdims=True)
    return centered * lax.rsqrt(variance + EPSILON)


def contract_rows(former, latter):
    return lax.dot_general(
        former, latter, (((0,), (0,)), ((), ())), preferred_element_type=jnp.float32
    )


def contract_last(former, latter):
    return lax.dot_general(
        former, latter, (((1,), (1,)), ((), ())), preferred_element_type=jnp.float32
    )


def group_table(length, unit_total, group_total):
    unit_group = jnp.arange(length, dtype=jnp.int32) // (unit_total // group_total)
    return (jnp.arange(group_total, dtype=jnp.int32)[:, None] == unit_group[None, :]).astype(
        jnp.float32
    )


def to_heads(matrix, row_total, head_count):
    token_total, model_width = matrix.shape
    seq_length = token_total // row_total
    head_size = model_width // head_count
    shaped = matrix.reshape(row_total, seq_length, head_count, head_size).transpose(0, 2, 1, 3)
    return shaped.reshape(row_total * head_count, seq_length, head_size)


def from_heads(stacked, row_total, head_count):
    seq_length, head_size = (stacked.shape[1], stacked.shape[2])
    shaped = stacked.reshape(row_total, head_count, seq_length, head_size).transpose(0, 2, 1, 3)
    return shaped.reshape(row_total * seq_length, head_count * head_size)


def masked_scores(query_rows, key_rows, segment):
    scores = contract_last(query_rows, key_rows) * query_rows.shape[1] ** (-0.5)
    same_item = segment[:, None] == segment[None, :]
    return jnp.where(same_item, scores, MASKED)


def attend_forward(inputs):
    query_rows, key_rows, value_rows, segment = inputs
    scores = masked_scores(query_rows, key_rows, segment)
    largest = jnp.max(scores, axis=-1, keepdims=True)
    weights = jnp.exp(scores - largest)
    totals = jnp.sum(weights, axis=-1, keepdims=True)
    probabilities = (weights / totals).astype(jnp.bfloat16)
    attended = jnp.dot(probabilities, value_rows, preferred_element_type=jnp.float32)
    return (attended, (largest + jnp.log(totals))[:, 0])


def attend_backward(inputs):
    query_rows, key_rows, value_rows, segment, log_total, grad_rows = inputs
    score_scale = query_rows.shape[1] ** (-0.5)
    scores = masked_scores(query_rows, key_rows, segment)
    probabilities = jnp.exp(scores - log_total[:, None])
    grad_probs = contract_last(grad_rows, value_rows)
    weighted_sum = jnp.sum(probabilities * grad_probs, axis=-1, keepdims=True)
    grad_scores = (probabilities * (grad_probs - weighted_sum)).astype(jnp.bfloat16)
    grad_query = jnp.dot(grad_scores, key_rows, preferred_element_type=jnp.float32) * score_scale
    grad_key = contract_rows(grad_scores, query_rows) * score_scale
    grad_value = contract_rows(probabilities.astype(jnp.bfloat16), grad_rows)
    return (grad_query, grad_key, grad_value)


def on_device(
    tokens,
    conditioning,
    row_items,
    head_mask,
    chan_mask,
    skip_mask,
    ada_weight,
    ada_bias,
    qkv_weight,
    query_bias,
    value_bias,
    proj_weight,
    proj_bias,
    fc1_weight,
    fc1_bias,
    fc2_weight,
    fc2_bias,
    head_router,
    head_router_bias,
    chan_router,
    chan_router_bias,
    token_router,
    cotangent,
):
    row_total = row_items.shape[0]
    token_total, model_width = tokens.shape
    seq_length = token_total // row_total
    slot_count = conditioning.shape[0]
    item_slots = slot_count // row_total
    head_count = head_mask.shape[1]
    group_count = chan_mask.shape[1]
    hidden_total = fc1_bias.shape[0]
    silu_cond = jax.nn.silu(conditioning.astype(jnp.float32)).astype(jnp.bfloat16)
    every_cond = lax.all_gather(silu_cond, ("narrow", "wide"), axis=0, tiled=True)
    mod_columns = jnp.dot(
        every_cond, ada_weight, preferred_element_type=jnp.float32
    ) + ada_bias.astype(jnp.float32)
    modulation = lax.all_to_all(
        mod_columns.astype(jnp.bfloat16),
        ("narrow", "wide"),
        split_axis=0,
        concat_axis=1,
        tiled=True,
    )
    cond_float = silu_cond.astype(jnp.float32)

    def router_gates(head_weight, head_offset, chan_weight, chan_offset):
        head_gate = head_mask.astype(jnp.float32) * jax.nn.sigmoid(
            jnp.dot(cond_float, head_weight, precision=HIGHEST) + head_offset
        )
        chan_gate = chan_mask.astype(jnp.float32) * jax.nn.sigmoid(
            jnp.dot(cond_float, chan_weight, precision=HIGHEST) + chan_offset
        )
        return (head_gate, chan_gate)

    (head_gate, chan_gate), router_pull = jax.vjp(
        router_gates,
        head_router.astype(jnp.float32),
        head_router_bias.astype(jnp.float32),
        chan_router.astype(jnp.float32),
        chan_router_bias.astype(jnp.float32),
    )
    position = jnp.arange(seq_length, dtype=jnp.int32)
    segment = jnp.where(row_items[:, None] == 1, 0, position[None, :] // (seq_length // item_slots))
    slot_index = (jnp.arange(row_total, dtype=jnp.int32)[:, None] * item_slots + segment).reshape(
        token_total
    )
    slot_match = slot_index[:, None] == jnp.arange(slot_count, dtype=jnp.int32)[None, :]
    slot_float = slot_match.astype(jnp.float32)
    token_mod = jnp.dot(
        slot_match.astype(jnp.bfloat16), modulation, preferred_element_type=jnp.float32
    )
    token_head = jnp.dot(slot_float, head_gate, precision=HIGHEST)
    token_chan = jnp.dot(slot_float, chan_gate, precision=HIGHEST)
    keep_scale = 1.0 - skip_mask.astype(jnp.float32)

    def first_norm(tokens_in, mod_in):
        spans = jnp.split(mod_in, 6, axis=1)
        return layer_norm(tokens_in) * (1.0 + spans[1]) + spans[0]

    normed_one, first_pull = jax.vjp(first_norm, tokens, token_mod)
    normed_low = normed_one.astype(jnp.bfloat16)
    full_qkv, full_proj = (
        lax.all_gather(qkv_weight, ("narrow", "wide"), axis=0, tiled=True),
        lax.all_gather(proj_weight, ("narrow", "wide"), axis=0, tiled=True),
    )
    qkv_bias = jnp.concatenate([query_bias, jnp.zeros_like(query_bias), value_bias]).astype(
        jnp.float32
    )
    qkv_low = (jnp.dot(normed_low, full_qkv, preferred_element_type=jnp.float32) + qkv_bias).astype(
        jnp.bfloat16
    )
    thirds = jnp.split(qkv_low, 3, axis=1)
    head_query = to_heads(thirds[0], row_total, head_count)
    head_key = to_heads(thirds[1], row_total, head_count)
    head_value = to_heads(thirds[2], row_total, head_count)
    head_segment = jnp.repeat(segment, head_count, axis=0)
    attended_heads, log_totals = lax.map(
        attend_forward, (head_query, head_key, head_value, head_segment)
    )
    attended = from_heads(attended_heads, row_total, head_count)
    head_scale = jnp.repeat(token_head, model_width // head_count, axis=1)
    gated_low = (attended * head_scale).astype(jnp.bfloat16)
    attn_out = jnp.dot(gated_low, full_proj, preferred_element_type=jnp.float32) + proj_bias.astype(
        jnp.float32
    )

    def middle(tokens_in, mod_in, attn_in, router_in):
        spans = jnp.split(mod_in, 6, axis=1)
        after_attn = tokens_in + spans[2] * attn_in
        normed = layer_norm(after_attn) * (1.0 + spans[4]) + spans[3]
        token_gate = jax.nn.sigmoid(jnp.dot(normed, router_in, precision=HIGHEST))
        return (after_attn, normed, token_gate)

    (after_attn, normed_two, token_gate), middle_pull = jax.vjp(
        middle, tokens, token_mod, attn_out, token_router.astype(jnp.float32)
    )
    normed_two_low = normed_two.astype(jnp.bfloat16)
    hidden_bias = fc1_bias.astype(jnp.float32)
    up_local, down_local = (
        lax.all_gather(fc1_weight, "narrow", axis=1, tiled=True),
        lax.all_gather(fc2_weight, "narrow", axis=1, tiled=True),
    )
    up_rows = lax.all_gather(up_local, "wide", axis=0, tiled=True)
    down_rows = lax.all_gather(down_local, "wide", axis=0, tiled=True)
    length = up_rows.shape[0]
    pre_act = contract_last(normed_two_low, up_rows) + hidden_bias
    chan_scale = jnp.dot(
        token_chan, group_table(length, hidden_total, group_count), precision=HIGHEST
    )
    scaled_low = (jax.nn.gelu(pre_act, approximate=True) * chan_scale).astype(jnp.bfloat16)
    mixed_sum = jnp.dot(scaled_low, down_rows, preferred_element_type=jnp.float32)
    mlp_out = mixed_sum + fc2_bias.astype(jnp.float32)
    spans = jnp.split(token_mod, 6, axis=1)
    branch_scale = spans[5] * (keep_scale * token_gate)[:, None]
    output = after_attn + branch_scale * mlp_out
    grad_mlp_low = (cotangent * branch_scale).astype(jnp.bfloat16)
    mlp_weighted = cotangent * mlp_out
    grad_gate_two = mlp_weighted * (keep_scale * token_gate)[:, None]
    grad_token_gate = jnp.sum(mlp_weighted * spans[5], axis=1) * keep_scale

    def mlp_backward(pieces):
        up_rows, down_rows = pieces
        length = up_rows.shape[0]
        unit_table = group_table(length, hidden_total, group_count)
        chan_scale = jnp.dot(token_chan, unit_table, precision=HIGHEST)
        active, gelu_pull = jax.vjp(
            lambda pre_value: jax.nn.gelu(pre_value, approximate=True), pre_act
        )
        scaled_low = (active * chan_scale).astype(jnp.bfloat16)
        grad_scaled = contract_last(grad_mlp_low, down_rows)
        grad_chan = jnp.dot(grad_scaled * active, unit_table.T, precision=HIGHEST)
        grad_pre_low = gelu_pull(grad_scaled * chan_scale)[0].astype(jnp.bfloat16)
        grad_normed = jnp.dot(grad_pre_low, up_rows, preferred_element_type=jnp.float32)
        return (grad_normed, grad_pre_low, scaled_low, grad_chan)

    up_again, down_again = (
        lax.all_gather(fc1_weight, "narrow", axis=1, tiled=True),
        lax.all_gather(fc2_weight, "narrow", axis=1, tiled=True),
    )
    mlp_back = mlp_backward(
        (
            lax.all_gather(up_again, "wide", axis=0, tiled=True),
            lax.all_gather(down_again, "wide", axis=0, tiled=True),
        )
    )
    grad_normed_two, grad_pre_all, scaled_all, grad_chan_tok = mlp_back
    mlp_partial = lax.psum_scatter(
        jnp.stack(
            [contract_rows(grad_pre_all, normed_two_low), contract_rows(scaled_all, grad_mlp_low)],
            axis=1,
        ).astype(jnp.bfloat16),
        "wide",
        scatter_dimension=0,
        tiled=True,
    )
    mlp_grads = lax.psum_scatter(mlp_partial, "narrow", scatter_dimension=2, tiled=True).astype(
        jnp.float32
    )
    grad_fc1_weight = mlp_grads[:, 0]
    grad_fc2_weight = mlp_grads[:, 1]
    grad_fc1_bias = jnp.sum(grad_pre_all.astype(jnp.float32), axis=0)
    grad_fc2_bias = jnp.sum(grad_mlp_low.astype(jnp.float32), axis=0)
    grad_chan_gate = jnp.dot(slot_float.T, grad_chan_tok, precision=HIGHEST)
    grad_tokens_mid, grad_mod_mid, grad_attn, grad_router_vector = middle_pull(
        (cotangent, grad_normed_two, grad_token_gate)
    )
    grad_attn_low = grad_attn.astype(jnp.bfloat16)
    qkv_back, proj_back = (
        lax.all_gather(qkv_weight, ("narrow", "wide"), axis=0, tiled=True),
        lax.all_gather(proj_weight, ("narrow", "wide"), axis=0, tiled=True),
    )
    grad_gated = contract_last(grad_attn_low, proj_back)
    grad_head_scale = jnp.sum(
        (grad_gated * attended).reshape(token_total, head_count, model_width // head_count), axis=2
    )
    grad_attended_low = (grad_gated * head_scale).astype(jnp.bfloat16)
    grad_query, grad_key, grad_value = lax.map(
        attend_backward,
        (
            head_query,
            head_key,
            head_value,
            head_segment,
            log_totals,
            to_heads(grad_attended_low, row_total, head_count),
        ),
    )
    grad_qkv_low = jnp.concatenate(
        [
            from_heads(grad_query, row_total, head_count),
            from_heads(grad_key, row_total, head_count),
            from_heads(grad_value, row_total, head_count),
        ],
        axis=1,
    ).astype(jnp.bfloat16)
    grad_normed_one = contract_last(grad_qkv_low, qkv_back)
    grad_tokens_first, grad_mod_first = first_pull(grad_normed_one)
    attn_grads = lax.psum_scatter(
        jnp.concatenate(
            [contract_rows(normed_low, grad_qkv_low), contract_rows(gated_low, grad_attn_low)],
            axis=1,
        ),
        ("narrow", "wide"),
        scatter_dimension=0,
        tiled=True,
    )
    grad_qkv_float = grad_qkv_low.astype(jnp.float32)
    grad_query_bias = jnp.sum(grad_qkv_float[:, :model_width], axis=0)
    grad_value_bias = jnp.sum(grad_qkv_float[:, 2 * model_width :], axis=0)
    grad_proj_bias = jnp.sum(grad_attn_low.astype(jnp.float32), axis=0)
    grad_token_mod = (grad_mod_mid + grad_mod_first).at[:, 5 * model_width :].add(grad_gate_two)
    grad_slot_mod = jnp.dot(slot_float.T, grad_token_mod, precision=HIGHEST).astype(jnp.bfloat16)
    grad_mod_columns = lax.all_to_all(
        grad_slot_mod, ("narrow", "wide"), split_axis=1, concat_axis=0, tiled=True
    )
    grad_ada_weight = contract_rows(every_cond, grad_mod_columns)
    grad_ada_bias = jnp.sum(grad_mod_columns.astype(jnp.float32), axis=0)
    grad_head_gate = jnp.dot(slot_float.T, grad_head_scale, precision=HIGHEST)
    grad_head_weight, grad_head_offset, grad_chan_weight, grad_chan_offset = router_pull(
        (grad_head_gate, grad_chan_gate)
    )
    small_sums = lax.psum(
        (
            grad_query_bias,
            grad_value_bias,
            grad_proj_bias,
            grad_fc1_bias,
            grad_fc2_bias,
            grad_head_weight,
            grad_head_offset,
            grad_chan_weight,
            grad_chan_offset,
            grad_router_vector,
        ),
        ("narrow", "wide"),
    )
    return (
        output,
        grad_tokens_mid + grad_tokens_first,
        grad_ada_weight,
        grad_ada_bias,
        attn_grads[:, : 3 * model_width],
        small_sums[0],
        small_sums[1],
        attn_grads[:, 3 * model_width :],
        small_sums[2],
        grad_fc1_weight,
        small_sums[3],
        grad_fc2_weight,
        small_sums[4],
        small_sums[5],
        small_sums[6],
        small_sums[7],
        small_sums[8],
        small_sums[9],
    )


def solution(mesh):
    return jax.shard_map(
        on_device,
        mesh=mesh,
        in_specs=(
            P(("narrow", "wide"), None),
            P(("narrow", "wide"), None),
            P(("narrow", "wide")),
            P(("narrow", "wide"), None),
            P(("narrow", "wide"), None),
            P(("narrow", "wide")),
            P(None, ("narrow", "wide")),
            P(("narrow", "wide")),
            P(("narrow", "wide"), None),
            P(),
            P(),
            P(("narrow", "wide"), None),
            P(),
            P("wide", "narrow"),
            P(),
            P("wide", "narrow"),
            P(),
            P(),
            P(),
            P(),
            P(),
            P(),
            P(("narrow", "wide"), None),
        ),
        out_specs=(
            P(("narrow", "wide"), None),
            P(("narrow", "wide"), None),
            P(None, ("narrow", "wide")),
            P(("narrow", "wide")),
            P(("narrow", "wide"), None),
            P(),
            P(),
            P(("narrow", "wide"), None),
            P(),
            P("wide", "narrow"),
            P(),
            P("wide", "narrow"),
            P(),
            P(),
            P(),
            P(),
            P(),
            P(),
        ),
        check_vma=False,
    )
```

profile of v0, /device:TPU:0, one launch (start us, length us, event | category | flops | bytes accessed | tf_op | source)
XLA Modules:
  0.0 1385.1 jit_solution(5568235661886437054)
XLA Ops:
  10.1 32.7 %all-gather.14.cloned.1.call-done = bf16[576,1152]{0,1:T(8,128)(2,1)} async-done(((bf16[576,288]{0,1:T(8,128)(2,1)}), bf16[576,1152]{0,1:T(8,128)(2,1)}) %all-gather.14.cloned.1.call-update) | async-done | bytes 1327120 | tf_op jit(solution)/shard_map/all_gather | solution.py:203
  45.5 42.0 %all-gather = bf16[32,4,1152]{2,1,0:T(4,128)(2,1)S(1)} all-gather(bf16[1,4,1152]{2,1,0:T(4,128)(2,1)S(1)} %fusion.120), channel_id=1, replica_groups=mesh['narrow'=4,'wide'=8] {'narrow','wide'}, dimensions={0}, use_global_device_ids=true | all-gather | bytes 304128 | tf_op jit(solution)/shard_map/all_gather | solution.py:115
  155.7 62.7 %all-gather.18.cloned.1.call-done = bf16[32,36,3456]{2,1,0:T(8,128)(2,1)} async-done(((bf16[1,36,3456]{2,1,0:T(8,128)(2,1)}), bf16[32,36,3456]{2,1,0:T(8,128)(2,1)}) %all-gather.18.cloned.1.call-update) | async-done | bytes 7962640 | tf_op jit(solution)/shard_map/all_gather | solution.py:165
  218.4 12.7 reshape.323
  231.1 12.1 add_convert_fusion
  274.3 168.6 %while.29 = (s32[]{:T(128)}, f32[16,1024,72]{1,2,0:T(8,128)}, f32[16,1024]{1,0:T(8,128)}, s32[16,1024]{1,0:T(8,128)S(1)}, bf16[16,1024,72]{2,1,0:T(8,128)(2,1)},...) while((s32[]{:T(128)}, f32[16,1024,72]{1,2,0:T(8,128)}, f32[16,1024]{1,0:T(8,128)}, ...), condition=%wide.region_5.6_spmd.clone, body=%wide.region_2.5_spmd.sunk.clone | while | flops 317717504 | bytes 30513272 | solution.py:179
  474.7 18.7 %fusion.135 = f32[1024,4608]{1,0:T(8,128)} fusion(bf16[1024,1152]{1,0:T(8,128)(2,1)S(1)} %get-tuple-element.262, bf16[4608,1152]{1,0:T(8,128)(2,1)} %all-gather.16.cloned.1.call-done), kind=kOutput, calls=%fused_computation.220 | convolution fusion | flops 10871635968 | bytes 31850496 | tf_op jit(solution)/shard_map/dot_general | solution.py:24
  493.5 39.4 %convert_reduce_fusion = (f32[4608]{0:T(1024)}, bf16[1024,4608]{1,0:T(8,128)(2,1)}, bf16[1024,4608]{1,0:T(8,128)(2,1)}, f32[1024,4608]{1,0:T(8,128)}) fusion(f32[4608]{0:T(1024)S(1)} %copy-done.39, f32[1024,4608]{1,0:T(8,128)} %fusion.135, f32[1024,4608]{1,0:T(8,128)} %fusion.77, bf16[4608,1152]{1,0:T(8,128)(2,1)} %all-gather.12.cloned.1.call-done, ...), kind=kOutput, calls=%fused_computation.72 | convolution fusion | flops 11000213504 | bytes 90869760 | tf_op jit(solution)/shard_map/dot_general | solution.py:24
  532.9 18.3 %fusion.58 = bf16[4608,1,1152]{2,0,1:T(8,128)(2,1)} fusion(bf16[1024,4608]{1,0:T(8,128)(2,1)} %get-tuple-element.278, bf16[1024,1152]{1,0:T(8,128)(2,1)S(1)} %get-tuple-element.262), kind=kOutput, calls=%fused_computation.76 | convolution fusion | flops 10876944384 | bytes 22413312 | tf_op jit(solution)/shard_map/dot_general | solution.py:18
  551.3 21.8 %multiply_reduce_fusion.3 = (f32[1024]{0:T(1024)S(1)}, f32[1024,1152]{1,0:T(8,128)}) fusion(f32[1024,6912]{1,0:T(8,128)} %fusion.81, f32[1024,1152]{1,0:T(8,128)} %param.51, f32[1152]{0:T(1024)S(1)} %copy-done.48, bf16[1024,4608]{1,0:T(8,128)(2,1)} %get-tuple-element.278, bf16[4608,1152]{1,0:T(8,128)(2,1)} %all-gather.16.cloned.1.call-done), kind=kOutput, calls=%fused_computation.104 | convolution fusion | flops 10876353536 | bytes 34218496 | tf_op jit(solution)/shard_map/dot_general | solution.py:213
  573.1 18.3 %fusion.57 = bf16[4608,1,1152]{2,0,1:T(8,128)(2,1)} fusion(bf16[1024,4608]{1,0:T(8,128)(2,1)} %get-tuple-element.264, f32[1024,1152]{1,0:T(8,128)S(1)} %bitcast.232), kind=kOutput, calls=%fused_computation.75 | convolution fusion | flops 10878124032 | bytes 24772608 | tf_op jit(solution)/shard_map/dot_general | solution.py:18
  591.5 20.9 %multiply_reduce_fusion.2 = (f32[1024]{0:T(1024)S(1)}, f32[1024,1152]{1,0:T(8,128)}) fusion(f32[1024,1152]{1,0:T(8,128)S(1)} %bitcast.222, f32[1024]{0:T(1024)S(1)} %broadcast_multiply_fusion, f32[1024,6912]{1,0:T(8,128)} %fusion.81, f32[1152]{0:T(1024)S(1)} %copy-done.47, f32[1024]{0:T(1024)S(1)} %fusion.99, bf16[1024,4608]{1,0:T(8,128)(2,1)} %get-tuple-element.264, ...), kind=kOutput, calls=%fused_computation.103 | convolution fusion | flops 10879892480 | bytes 34226688 | tf_op jit(solution)/shard_map/dot_general | solution.py:235
  612.4 21.3 %fusion.55 = f32[1024,32]{0,1:T(8,128)S(1)} fusion(f32[1024,4608]{1,0:T(8,128)} %fusion.135, f32[1024,4608]{1,0:T(8,128)} %get-tuple-element.294, f32[4608]{0:T(1024)S(1)} %copy-done.39, s32[4608]{0:T(1024)S(1)} %copy-done.21), kind=kOutput, calls=%fused_computation.70 | convolution fusion | flops 1859272704 | bytes 37916672 | tf_op jit(solution)/shard_map/dot_general | solution.py:233
  633.8 13.0 pad_maximum_fusion.1
  647.5 12.3 fusion.126
  697.7 211.0 %while.30 = (s32[]{:T(128)}, bf16[16,1024,72]{1,2,0:T(8,128)(2,1)S(1)}, bf16[16,1024,72]{1,2,0:T(8,128)(2,1)}, bf16[16,1024,72]{1,2,0:T(8,128)(2,1)}, s32[16,102...) while((s32[]{:T(128)}, ...), condition=%wide.region_13.14_spmd.clone, body=%wide.region_11.13_spmd.sunk.clone | while | flops 765606912 | bytes 33989748 | solution.py:279
  908.7 15.0 %fusion.122 = f32[1152,3456]{1,0:T(8,128)} fusion(bf16[1024,1152]{1,0:T(8,128)(2,1)} %copy-done.13, bf16[1024,1152]{0,1:T(8,128)(2,1)} %bitcast.252, bf16[1024,1152]{0,1:T(8,128)(2,1)} %bitcast.255, bf16[1024,1152]{0,1:T(8,128)(2,1)S(1)} %bitcast.235), kind=kOutput, calls=%fused_computation.208 | convolution fusion | flops 8174960640 | bytes 25362432 | tf_op jit(solution)/shard_map/dot_general | solution.py:18
  923.7 14.0 %pad_maximum_fusion = f32[1152,4608]{1,0:T(8,128)} fusion(f32[1152,1152]{1,0:T(8,128)S(1)} %copy-done.10, f32[1152,3456]{1,0:T(8,128)} %fusion.122), kind=kLoop, calls=%fused_computation.59 | loop fusion | flops 5308416 | bytes 42467328 | tf_op jit(solution)/shard_map/concatenate | solution.py:301
  938.5 18.6 %multiply_reduce_fusion.1 = (f32[1024]{0:T(1024)S(1)}, f32[1024,1152]{1,0:T(8,128)}) fusion(f32[1024,1152]{1,0:T(8,128)} %param.29, f32[1024]{0:T(1024)S(1)} %copy-done.24, f32[1024,6912]{1,0:T(8,128)} %fusion.81, bf16[1152,3456]{1,0:T(8,128)(2,1)} %reshape.323, bf16[1024,1152]{0,1:T(8,128)(2,1)} %bitcast.253, bf16[1024,1152]{0,1:T(8,128)(2,1)} %bitcast.256, ...), kind=kOutput, calls=%fused_computation.99 | convolution fusion | flops 8180857856 | bytes 29204480 | tf_op jit(solution)/shard_map/dot_general | solution.py:24
  990.5 21.6 %maximum_add_fusion = f32[1024,6912]{1,0:T(8,128)} fusion(f32[1024,6912]{1,0:T(8,128)} %broadcast_dynamic-update-slice_fusion.1, f32[1024,1152]{1,0:T(8,128)S(1)} %bitcast.241, f32[1024,1152]{1,0:T(8,128)S(1)} %bitcast.239, f32[6912]{0:T(1024)S(1)} %copy-done.19), kind=kLoop, calls=%fused_computation.56 | loop fusion | flops 21233664 | bytes 66087936 | tf_op jit(solution)/shard_map/add | solution.py:313
  1028.4 14.0 %convolution_convert_fusion.2 = bf16[4,6912]{1,0:T(4,128)(2,1)S(1)} fusion(f32[1024,6912]{1,0:T(8,128)} %fusion.59, s32[1024]{0:T(1024)S(1)} %copy-done.16), kind=kOutput, calls=%fused_computation.78 | convolution fusion | flops 339770368 | bytes 28370944 | tf_op jit(solution)/shard_map/dot_general | solution.py:314
  1054.3 43.5 %all-reduce.2 = (f32[1152]{0:T(1024)}, f32[1152]{0:T(1024)}, f32[1152]{0:T(1024)}, f32[4608]{0:T(1024)}, f32[1152]{0:T(1024)}, /*index=5*/f32[16]{0:T(128)}, f32[32]{0:T(128)}, f32[1152]{0:T(1024)}) all-reduce(f32[1152]{0:T(1024)S(1)} %get-tuple-element.215, ...), channel_id=1, replica_groups=mesh['narrow'=4,'wide'=8] {'narrow','wide'}, use_global_device_ids=true, to_apply=%region_19.20 | all-reduce | flops 10416 | bytes 83328 | tf_op jit(solution)/shard_map/psum | solution.py:324
  1099.8 186.8 %all-reduce.9.cloned.1.call-done = (f32[1152,4608]{1,0:T(8,128)}, f32[1152,16]{0,1:T(8,128)}, f32[1152,32]{0,1:T(8,128)}) async-done(((f32[1152,4608]{1,0:T(8,128)}, f32[1152,16]{0,1:T(8,128)}, f32[1152,32]{0,1:T(8,128)}), (f32[1152,4608]{1,0:T(8,128)}, f32[1152,16]{0,1:T(8,128)}, f32[1152,32]{0,1:T(8,128)})) %all-reduce.9.cloned.1.call-update) | async-done | bytes 21454864
  1290.4 82.4 %all-reduce.7.cloned.1.call-done = bf16[576,2,1152]{0,1,2:T(2,128)(2,1)} async-done(((bf16[576,2,1152]{0,1,2:T(2,128)(2,1)}), bf16[576,2,1152]{0,1,2:T(2,128)(2,1)}) %all-reduce.7.cloned.1.call-update) | async-done | bytes 2654224
  (580 shorter events, 624.4 us)
Async XLA Ops:
  7.2 80.4 %copy-start = (bf16[1152,216]{0,1:T(8,128)(2,1)S(1)}, bf16[1152,216]{0,1:T(8,128)(2,1)}, u32[]{:S(2)}) copy-start(bf16[1152,216]{0,1:T(8,128)(2,1)} %param.35) | copy-start | bytes 1492996
  7.2 84.1 %copy-start.40 = (bf16[1152]{0:T(1024)(128)(2,1)S(1)}, bf16[1152]{0:T(1024)(128)(2,1)}, u32[]{:S(2)}) copy-start(bf16[1152]{0:T(1024)(128)(2,1)} %param.50) | copy-start | bytes 6916
  7.2 35.6 %all-gather.14.cloned.1.call-start = ((), (), s32[]{:S(2)}) async-start(), calls=%async_computation.5 | async-start | bytes 1843200 | tf_op jit(solution)/shard_map/all_gather | solution.py:203
  8.0 138.9 %all-gather.10.cloned.1.call-start = ((), (), s32[]{:S(2)}) async-start(), calls=%async_computation.3 | async-start | bytes 1843200 | tf_op jit(solution)/shard_map/all_gather | solution.py:202
  8.7 141.8 %all-gather.20.cloned.1.call-start = ((), (), s32[]{:S(2)}) async-start(), calls=%async_computation.9 | async-start | bytes 3041280 | tf_op jit(solution)/shard_map/all_gather | solution.py:166
  9.5 209.0 %all-gather.18.cloned.1.call-start = ((), (), s32[]{:S(2)}) async-start(), calls=%async_computation.8 | async-start | bytes 9123840 | tf_op jit(solution)/shard_map/all_gather | solution.py:165
  10.0 464.7 %all-gather.16.cloned.1.call-start = ((), (), s32[]{:S(2)}) async-start(), calls=%async_computation.6 | async-start | bytes 11943936 | tf_op jit(solution)/shard_map/all_gather | solution.py:206
  88.7 42.1 %all-to-all-start = ((bf16[32,4,216]{2,1,0:T(4,128)(2,1)}), bf16[32,4,216]{2,1,0:T(4,128)(2,1)S(1)}, u32[]{:S(2)}, u32[]{:S(2)}) async-start(bf16[32,4,216]{2,1,0:T(4,128)(2,1)} %all_to_all.28), calls=%async_computation | async-start | bytes 131072 | tf_op jit(solution)/shard_map/all_to_all | solution.py:119
  91.3 402.2 %all-gather.12.cloned.1.call-start = ((), (), s32[]{:S(2)}) async-start(), calls=%async_computation.4 | async-start | bytes 11943936 | tf_op jit(solution)/shard_map/all_gather | solution.py:205
  98.5 175.8 %copy-start.14 = (s32[1024]{0:T(1024)}, s32[1024]{0:T(1024)S(1)}, u32[]{:S(2)}) copy-start(s32[1024]{0:T(1024)S(1)} %fusion.98) | copy-start | bytes 12292
  146.9 84.3 %copy-start.13 = (bf16[1024,1152]{1,0:T(8,128)(2,1)}, bf16[1024,1152]{1,0:T(8,128)(2,1)S(1)}, u32[]{:S(2)}) copy-start(bf16[1024,1152]{1,0:T(8,128)(2,1)S(1)} %fusion.60) | copy-start | bytes 7077892
  150.3 867.8 %reduce-scatter.2.cloned.1.call-start = ((), (), s32[]{:S(2)}) async-start(), calls=%async_computation.7 | async-start | bytes 23887872 | tf_op jit(solution)/shard_map/reduce_scatter | solution.py:249
  532.9 40.1 %slice-start.12 = ((s8[4718592]{0:T(1024)(128)(4,1)}), s8[4194304]{0:T(1024)(128)(4,1)S(1)}, s32[]{:S(2)}) async-start(s8[4718592]{0:T(1024)(128)(4,1)} %bitcast.231), calls=%async_computation.24 | async-start | bytes 8388608
  532.9 58.5 %slice-start.2 = ((s8[4718592]{0:T(1024)(128)(4,1)}), s8[4194304]{0:T(1024)(128)(4,1)S(1)}, s32[]{:S(2)}) async-start(s8[4718592]{0:T(1024)(128)(4,1)} %bitcast.221), calls=%async_computation.14 | async-start | bytes 8388608
  551.3 40.2 %slice-start.3 = ((s8[4718592]{0:T(1024)(128)(4,1)}), s8[524288]{0:T(1024)(128)(4,1)S(1)}, s32[]{:S(2)}) async-start(s8[4718592]{0:T(1024)(128)(4,1)} %bitcast.221), calls=%async_computation.15 | async-start | bytes 1048576
  591.5 42.3 %slice-start.22 = ((s8[10616832]{0:T(1024)(128)(4,1)}), s8[2228224]{0:T(1024)(128)(4,1)S(1)}, s32[]{:S(2)}) async-start(s8[10616832]{0:T(1024)(128)(4,1)} %bitcast.247), calls=%async_computation.34 | async-start | bytes 4456448
  591.5 42.3 %slice-start.23 = ((s8[10616832]{0:T(1024)(128)(4,1)}), s8[4194304]{0:T(1024)(128)(4,1)S(1)}, s32[]{:S(2)}) async-start(s8[10616832]{0:T(1024)(128)(4,1)} %bitcast.247), calls=%async_computation.35 | async-start | bytes 8388608
  646.8 639.9 %all-reduce.9.cloned.1.call-start = ((), (), s32[]{:S(2)}) async-start(), calls=%async_computation.11 | async-start | bytes 42909696
  937.8 435.0 %all-reduce.7.cloned.1.call-start = ((), (), s32[]{:S(2)}) async-start(), calls=%async_computation.10 | async-start | bytes 5898240
  1043.3 54.5 %all-to-all-start.1 = ((bf16[4,32,216]{2,0,1:T(4,128)(2,1)}), bf16[4,32,216]{2,0,1:T(4,128)(2,1)S(1)}, u32[]{:S(2)}, u32[]{:S(2)}) async-start(bf16[4,32,216]{2,0,1:T(4,128)(2,1)} %copy.107), calls=%async_computation.1 | async-start | bytes 131072 | tf_op jit(solution)/shard_map/all_to_all | solution.py:315
  1051.8 46.7 %copy-start.12 = (bf16[128,1152]{1,0:T(8,128)(2,1)S(1)}, bf16[128,1152]{1,0:T(8,128)(2,1)}, u32[]{:S(2)}) copy-start(bf16[128,1152]{1,0:T(8,128)(2,1)} %copy-done.11) | copy-start | bytes 884740
  1286.7 90.2 %copy-start.22 = (f32[1152,16]{0,1:T(8,128)S(1)}, f32[1152,16]{0,1:T(8,128)}, u32[]{:S(2)}) copy-start(f32[1152,16]{0,1:T(8,128)} %get-tuple-element.526) | copy-start | bytes 221188
  1286.7 91.4 %copy-start.1 = (bf16[1152,216]{0,1:T(8,128)(2,1)S(1)}, bf16[1152,216]{0,1:T(8,128)(2,1)}, u32[]{:S(2)}) copy-start(bf16[1152,216]{0,1:T(8,128)(2,1)} %param.35) | copy-start | bytes 1492996
  1288.5 89.0 %copy-start.18 = (f32[1152,32]{0,1:T(8,128)S(1)}, f32[1152,32]{0,1:T(8,128)}, u32[]{:S(2)}) copy-start(f32[1152,32]{0,1:T(8,128)} %get-tuple-element.528) | copy-start | bytes 442372
  (96 other events, 962.9 us)
Sparse Core Ops, SparseCore 0:
  9.9 32.8 all-gather.13
  44.6 30.6 all-gather.9
  78.2 59.2 all-gather.19
  140.2 78.1 all-gather.17
  219.9 99.0 all-gather.15
  320.5 98.8 all-gather.11
  646.9 209.1 reduce-scatter.1
  937.9 348.6 all-reduce.8
  1290.2 82.6 all-reduce.6
where the time goes:
time: 1400 us; the launch traced here: 1390 us
  matrix products  543 us (39%)
  waiting for transfers between devices  367 us (26%)
  local copies, waits for them, and re-layouts  197 us (14%)
  other arithmetic  166 us (12%)
  blocking collectives  85.5 us (6%)
  between operations  16.8 us (1%)
    unnamed x11, waiting for transfers between devices  272 us
    dot_general x52, matrix products, contract_last(): lax.dot_general(former, latter, (((1,), (1,)), ((), ())), preferred_eleme...  183 us
    dot_general x37, matrix products, contract_rows(): lax.dot_general(former, latter, (((0,), (0,)), ((), ())), preferred_eleme...  137 us
    dot_general x16, matrix products, attend_forward(): jnp.dot(probabilities, value_rows, preferred_element_type=jnp.float32)  68.3 us
    all_gather x1, waiting for transfers between devices, on_device(): lax.all_gather(qkv_weight, ('narrow', 'wide'), axis=0, tiled=True)  62.7 us
    psum x1, blocking collectives, on_device(): lax.psum((grad_query_bias, grad_value_bias, grad_proj_bias, grad_fc1_bias...  43.5 us
    all_gather x1, blocking collectives, on_device(): lax.all_gather(silu_cond, ('narrow', 'wide'), axis=0, tiled=True)  42 us
    unnamed x198, local copies, waits for them, and re-layouts  36.4 us
  transfers between devices with their start and end apart: 11, of which 4 were waited for; matrix products, arithmetic and copies ran while one was open for 51% of the time, Pallas kernels for 0%

commit v1 on v0

v1 whole, which is shorter than its diff:
```python
import functools

import jax
import jax.numpy as jnp
from jax import lax
from jax.experimental import pallas as pl
from jax.experimental.pallas import tpu as pltpu
from jax.sharding import PartitionSpec as P

HIGHEST = lax.Precision.HIGHEST
F32 = jnp.float32
BF = jnp.bfloat16
EPSILON = 1e-06
MASKED = -1e30
LOG2E = 1.4426950408889634
WINDOW = 256
NN = (((1,), (0,)), ((), ()))
NT = (((1,), (1,)), ((), ()))
TN = (((0,), (0,)), ((), ()))
VMEM_SPEC = pl.BlockSpec(memory_space=pltpu.VMEM)
SMEM_SPEC = pl.BlockSpec(memory_space=pltpu.SMEM)


def dg(a, b, dims):
    return lax.dot_general(a, b, dims, preferred_element_type=F32)


def params(mib=60):
    return pltpu.CompilerParams(vmem_limit_bytes=mib << 20)


def shape(dims, dtype=F32):
    return jax.ShapeDtypeStruct(dims, dtype)


def whole(*dims):
    return pl.BlockSpec(dims, lambda i: (0,) * len(dims))


def rows_of(block, width):
    return pl.BlockSpec((block, width), lambda i: (i, 0))


def row_vec(width):
    return pl.BlockSpec((1, 1, width), lambda i: (i, 0, 0))


def ln_parts(x):
    centered = x - jnp.mean(x, axis=-1, keepdims=True)
    rstd = lax.rsqrt(jnp.mean(centered * centered, axis=-1, keepdims=True) + EPSILON)
    return centered * rstd, rstd


def ln_back(grad_y, normed, rstd, scale):
    m = grad_y * (1.0 + scale)
    mean_m = jnp.mean(m, axis=-1, keepdims=True)
    mean_mn = jnp.mean(m * normed, axis=-1, keepdims=True)
    return (m - mean_m - normed * mean_mn) * rstd


def col_sum(x):
    return jnp.sum(x, axis=0, keepdims=True)


def gelu_parts(x):
    k0 = 0.7978845608028654
    k1 = 0.044715
    x2 = x * x
    t = jnp.tanh(k0 * x * (1.0 + k1 * x2))
    half = 0.5 * (1.0 + t)
    return x * half, half + 0.5 * x * (1.0 - t * t) * (k0 * (1.0 + 3.0 * k1 * x2))


def qkv_kernel(tokens_ref, shift_ref, scale_ref, w_ref, bias_ref, n1_ref, qkv_ref):
    normed, _ = ln_parts(tokens_ref[...])
    low = (normed * (1.0 + scale_ref[0]) + shift_ref[0]).astype(BF)
    n1_ref[...] = low
    qkv_ref[...] = (dg(low, w_ref[...], NN) + bias_ref[...]).astype(BF)


def qkv_call(tokens, shift, scale, w, bias, blk):
    t, d = tokens.shape
    n = w.shape[1]
    return pl.pallas_call(
        qkv_kernel,
        grid=(t // blk,),
        out_shape=(shape((t, d), BF), shape((t, n), BF)),
        in_specs=[rows_of(blk, d), row_vec(d), row_vec(d), whole(d, n), whole(1, n)],
        out_specs=(rows_of(blk, d), rows_of(blk, n)),
        compiler_params=params(),
        name="qkv_forward",
    )(tokens, shift, scale, w, bias)


def head_window(h, hd, width):
    a = pl.multiple_of(jnp.minimum((h * hd) // 128, (width - WINDOW) // 128) * 128, 128)
    lane = lax.broadcasted_iota(jnp.int32, (1, WINDOW), 1) + a
    return a, (lane >= h * hd) & (lane < h * hd + hd)


def attn_fwd_kernel(off_ref, gate_ref, qkv_ref, att_ref, gated_ref, lse_ref, lse_sc, *, heads, blk):
    t, d = att_ref.shape
    hd = d // heads
    nb = t // blk
    c = hd**-0.5 * LOG2E
    off = off_ref[0]
    lane128 = lax.broadcasted_iota(jnp.int32, (1, 128), 1)

    def body(h, carry):
        a, mask = head_window(h, hd, d)
        keys = qkv_ref[:, pl.ds(pl.multiple_of(d + a, 128), WINDOW)]
        values = qkv_ref[:, pl.ds(pl.multiple_of(2 * d + a, 128), WINDOW)]
        cols = pl.ds(a, WINDOW)
        for i in range(nb):
            rows = pl.ds(i * blk, blk)
            q = qkv_ref[rows, cols]
            q = jnp.where(mask, q, jnp.zeros_like(q))
            s = dg(q, keys, NT)
            parts = [s[:, j * blk : (j + 1) * blk] for j in range(nb)]
            own = jnp.max(parts[i], axis=1, keepdims=True) * c
            others = functools.reduce(jnp.maximum, [parts[j] for j in range(nb) if j != i])
            m = jnp.maximum(own, jnp.max(others, axis=1, keepdims=True) * c + off)
            m_off = m - off
            ps = [jnp.exp2(parts[j] * c - (m if j == i else m_off)) for j in range(nb)]
            total = jnp.sum(functools.reduce(jnp.add, ps), axis=1, keepdims=True)
            p = jnp.concatenate([x.astype(BF) for x in ps], axis=1)
            o = dg(p, values, NN) * (1.0 / total)
            og = (o * gate_ref[i, :, cols]).astype(BF)
            att_ref[rows, cols] = jnp.where(mask, o, att_ref[rows, cols])
            gated_ref[rows, cols] = jnp.where(mask, og, gated_ref[rows, cols])
            lse_sc[rows, :] = jnp.where(lane128 == h, m + jnp.log2(total), lse_sc[rows, :])
        return carry

    lax.fori_loop(0, heads, body, 0)
    lse_ref[...] = lse_sc[...].T[:heads, :]


def attn_fwd(off, gate_rows, qkv, heads, blk):
    t = qkv.shape[0]
    d = qkv.shape[1] // 3
    return pl.pallas_call(
        functools.partial(attn_fwd_kernel, heads=heads, blk=blk),
        out_shape=(shape((t, d)), shape((t, d), BF), shape((heads, t))),
        in_specs=[SMEM_SPEC, VMEM_SPEC, VMEM_SPEC],
        out_specs=(VMEM_SPEC,) * 3,
        scratch_shapes=[pltpu.VMEM((t, 128), F32)],
        compiler_params=params(),
        name="attention_forward",
    )(off, gate_rows, qkv)


def attn_bwd_kernel(
    off_ref, qkv_ref, do_ref, lse_ref, delta_ref, dqkv_ref, kt_sc, dqt_sc, *, heads, blk
):
    t, d = do_ref.shape
    hd = d // heads
    nb = t // blk
    scale = hd**-0.5
    c = scale * LOG2E
    off = off_ref[0]
    kt_sc[...] = qkv_ref[:, d : 2 * d].T

    def body(h, carry):
        a, mask = head_window(h, hd, d)
        cols = pl.ds(a, WINDOW)
        key_cols = pl.ds(pl.multiple_of(d + a, 128), WINDOW)
        value_cols = pl.ds(pl.multiple_of(2 * d + a, 128), WINDOW)
        keys = qkv_ref[:, key_cols]
        values = qkv_ref[:, value_cols]
        keys_t = kt_sc[cols, :]
        dk_sum = None
        dv_sum = None
        for i in range(nb):
            rows = pl.ds(i * blk, blk)
            span = slice(i * blk, (i + 1) * blk)
            q = qkv_ref[rows, cols]
            q = jnp.where(mask, q, jnp.zeros_like(q))
            do = do_ref[rows, cols]
            do = jnp.where(mask, do, jnp.zeros_like(do))
            lse = lse_ref[pl.ds(h, 1), span]
            delta = delta_ref[pl.ds(h, 1), span]
            s_t = dg(keys, q, NT)
            dp_t = dg(values, do, NT)
            ps = []
            ds = []
            for j in range(nb):
                part = slice(j * blk, (j + 1) * blk)
                p = jnp.exp2(s_t[part] * c - (lse if j == i else lse - off))
                ps.append(p.astype(BF))
                ds.append((p * (dp_t[part] - delta)).astype(BF))
            p = jnp.concatenate(ps, axis=0)
            grad_s = jnp.concatenate(ds, axis=0)
            dv = dg(p, do, NN)
            dk = dg(grad_s, q, NN)
            dv_sum = dv if dv_sum is None else dv_sum + dv
            dk_sum = dk if dk_sum is None else dk_sum + dk
            dqt_sc[:, span] = (dg(keys_t, grad_s, NN) * scale).astype(BF)
        dk = (dk_sum * scale).astype(BF)
        dqkv_ref[:, key_cols] = jnp.where(mask, dk, dqkv_ref[:, key_cols])
        dqkv_ref[:, value_cols] = jnp.where(mask, dv_sum.astype(BF), dqkv_ref[:, value_cols])
        dqkv_ref[:, cols] = jnp.where(mask, dqt_sc[...].T, dqkv_ref[:, cols])
        return carry

    lax.fori_loop(0, heads, body, 0)


def attn_bwd(off, qkv, do, lse, delta, heads, blk):
    t, d = do.shape
    return pl.pallas_call(
        functools.partial(attn_bwd_kernel, heads=heads, blk=blk),
        out_shape=shape((t, 3 * d), BF),
        in_specs=[SMEM_SPEC] + [VMEM_SPEC] * 4,
        out_specs=VMEM_SPEC,
        scratch_shapes=[pltpu.VMEM((d, t), BF), pltpu.VMEM((WINDOW, t), BF)],
        compiler_params=params(),
        name="attention_backward",
    )(off, qkv, do, lse, delta)


def middle_kernel(
    gated_ref,
    w_ref,
    bias_ref,
    tokens_ref,
    cot_ref,
    keep_ref,
    router_ref,
    gate1_ref,
    shift2_ref,
    scale2_ref,
    gate2_ref,
    attn_ref,
    after_ref,
    n2_ref,
    gm_ref,
    tg_ref,
):
    attn = dg(gated_ref[...], w_ref[...], NN) + bias_ref[...]
    attn_ref[...] = attn
    after = tokens_ref[...] + gate1_ref[0] * attn
    after_ref[...] = after
    normed, _ = ln_parts(after)
    y = normed * (1.0 + scale2_ref[0]) + shift2_ref[0]
    n2_ref[...] = y.astype(BF)
    token_gate = jax.nn.sigmoid(jnp.sum(y * router_ref[...], axis=1, keepdims=True))
    tg_ref[...] = token_gate
    gm_ref[...] = (cot_ref[...] * (gate2_ref[0] * (keep_ref[...] * token_gate))).astype(BF)


def middle_call(gated, w, bias, tokens, cot, keep, router, gate1, shift2, scale2, gate2, blk):
    t, d = tokens.shape
    r, v = rows_of(blk, d), row_vec(d)
    column = rows_of(blk, 1)
    return pl.pallas_call(
        middle_kernel,
        grid=(t // blk,),
        out_shape=(shape((t, d)), shape((t, d)), shape((t, d), BF), shape((t, d), BF), shape((t, 1))),
        in_specs=[r, whole(d, d), whole(1, d), r, r, column, whole(1, d), v, v, v, v],
        out_specs=(r, r, r, r, column),
        compiler_params=params(),
        name="middle_forward",
    )(gated, w, bias, tokens, cot, keep, router, gate1, shift2, scale2, gate2)


def mlp_kernel(
    n2_ref, gm_ref, w1_ref, w2_ref, b1_ref, cs_ref, mlp_ref, gn2_ref, g1_ref, g2_ref, gb1_ref, gch_ref, sc_s, gp_s, *, blk
):
    nb = n2_ref.shape[0] // blk

    @pl.when(pl.program_id(0) == 0)
    def _():
        mlp_ref[...] = jnp.zeros_like(mlp_ref)
        gn2_ref[...] = jnp.zeros_like(gn2_ref)

    w1 = w1_ref[...]
    w2 = w2_ref[...]
    grad_bias = None
    for i in range(nb):
        rows = slice(i * blk, (i + 1) * blk)
        pre = dg(n2_ref[rows, :], w1, NT) + b1_ref[...]
        grad_scaled = dg(gm_ref[rows, :], w2, NT)
        act, slope = gelu_parts(pre)
        gate = cs_ref[i]
        scaled = (act * gate).astype(BF)
        grad_pre = (grad_scaled * gate * slope).astype(BF)
        gch_ref[i] = col_sum(grad_scaled * act)
        part = col_sum(grad_pre.astype(F32))
        grad_bias = part if grad_bias is None else grad_bias + part
        sc_s[rows, :] = scaled
        gp_s[rows, :] = grad_pre
        mlp_ref[rows, :] += dg(scaled, w2, NN)
        gn2_ref[rows, :] += dg(grad_pre, w1, NN)
    gb1_ref[...] = grad_bias
    g1_ref[...] = dg(gp_s[...], n2_ref[...], TN).astype(BF)
    g2_ref[...] = dg(sc_s[...], gm_ref[...], TN).astype(BF)


def mlp_call(n2, gm, w1, w2, b1, gates, hb, blk):
    t, d = n2.shape
    ff = w1.shape[0]
    nb = t // blk
    w_spec = pl.BlockSpec((hb, d), lambda j: (j, 0))
    b_spec = pl.BlockSpec((1, hb), lambda j: (0, j))
    c_spec = pl.BlockSpec((nb, 1, hb), lambda j: (0, 0, j))
    return pl.pallas_call(
        functools.partial(mlp_kernel, blk=blk),
        grid=(ff // hb,),
        out_shape=(
            shape((t, d)),
            shape((t, d)),
            shape((ff, d), BF),
            shape((ff, d), BF),
            shape((1, ff)),
            shape((nb, 1, ff)),
        ),
        in_specs=[whole(t, d), whole(t, d), w_spec, w_spec, b_spec, c_spec],
        out_specs=(whole(t, d), whole(t, d), w_spec, w_spec, b_spec, c_spec),
        scratch_shapes=[pltpu.VMEM((t, hb), BF), pltpu.VMEM((t, hb), BF)],
        compiler_params=params(),
        name="feed_forward",
    )(n2, gm, w1, w2, b1, gates)


def middle_back_kernel(
    mlp_ref,
    gn2_ref,
    after_ref,
    attn_ref,
    cot_ref,
    gm_ref,
    gated_ref,
    att_ref,
    tg_ref,
    keep_ref,
    w_ref,
    b2_ref,
    router_ref,
    gate1_ref,
    shift2_ref,
    scale2_ref,
    gate2_ref,
    head_ref,
    out_ref,
    ga_ref,
    do_ref,
    delta_ref,
    gw_ref,
    mod_ref,
    sums_ref,
    *,
    heads,
):
    d = after_ref.shape[1]
    hd = d // heads
    first = pl.program_id(0) == 0
    after = after_ref[...]
    cot = cot_ref[...]
    gate2 = gate2_ref[0]
    tg = tg_ref[...]
    keep = keep_ref[...]
    normed, rstd = ln_parts(after)
    scale2 = scale2_ref[0]
    y = normed * (1.0 + scale2) + shift2_ref[0]
    mlp_out = mlp_ref[...] + b2_ref[...]
    open_gate = keep * tg
    out_ref[...] = after + (gate2 * open_gate) * mlp_out
    weighted = cot * mlp_out
    grad_tg = jnp.sum(weighted * gate2, axis=1, keepdims=True) * keep
    coef = grad_tg * tg * (1.0 - tg)
    gy = gn2_ref[...] + coef * router_ref[...]
    ga = cot + ln_back(gy, normed, rstd, scale2)
    ga_ref[...] = ga
    attn = attn_ref[...]
    g_attn = (ga * gate1_ref[0]).astype(BF)
    mod_ref[0] = jnp.concatenate(
        [col_sum(ga * attn), col_sum(gy), col_sum(gy * normed), col_sum(weighted * open_gate)], axis=0
    )
    sums = jnp.concatenate(
        [
            col_sum(coef * y),
            col_sum(g_attn.astype(F32)),
            col_sum(gm_ref[...].astype(F32)),
        ],
        axis=0,
    )
    g_gated = dg(g_attn, w_ref[...], NT)
    att = att_ref[...]
    mod_ref[1] = jnp.concatenate([col_sum(g_gated * att), jnp.zeros((3, d), F32)], axis=0)
    do = (g_gated * head_ref[0]).astype(BF)
    do_ref[...] = do
    lane = lax.broadcasted_iota(jnp.int32, (heads, d), 1)
    head = lax.broadcasted_iota(jnp.int32, (heads, d), 0) * hd
    pick = jnp.where((lane >= head) & (lane < head + hd), 1.0, 0.0)
    delta_ref[...] = lax.dot_general(
        pick, do.astype(F32) * att, NT, precision=HIGHEST, preferred_element_type=F32
    )
    gw = dg(gated_ref[...], g_attn, TN)

    @pl.when(first)
    def _():
        sums_ref[...] = sums
        gw_ref[...] = gw

    @pl.when(jnp.logical_not(first))
    def _():
        sums_ref[...] += sums
        gw_ref[...] += gw


def middle_back_call(
    mlp, gn2, after, attn, cot, gm, gated, att, tg, keep, w, b2, router, gate1, shift2, scale2, gate2, head_rows, heads, blk
):
    t, d = after.shape
    nb = t // blk
    r, v, column = rows_of(blk, d), row_vec(d), rows_of(blk, 1)
    return pl.pallas_call(
        functools.partial(middle_back_kernel, heads=heads),
        grid=(nb,),
        out_shape=(
            shape((t, d)),
            shape((t, d)),
            shape((t, d), BF),
            shape((heads, t)),
            shape((d, d)),
            shape((nb * 2, 4, d)),
            shape((3, d)),
        ),
        in_specs=[r] * 8 + [column, column, whole(d, d), whole(1, d), whole(1, d), v, v, v, v, v],
        out_specs=(
            r,
            r,
            r,
            pl.BlockSpec((heads, blk), lambda i: (0, i)),
            whole(d, d),
            pl.BlockSpec((2, 4, d), lambda i: (i, 0, 0)),
            whole(3, d),
        ),
        compiler_params=params(),
        name="middle_backward",
    )(mlp, gn2, after, attn, cot, gm, gated, att, tg, keep, w, b2, router, gate1, shift2, scale2, gate2, head_rows)


def qkv_weight_kernel(n1_ref, dqkv_ref, gw_ref, bias_ref, n1t):
    @pl.when(pl.program_id(0) == 0)
    def _():
        n1t[...] = n1_ref[...].T

    dqkv = dqkv_ref[...]
    gw_ref[...] = dg(n1t[...], dqkv, NN).astype(gw_ref.dtype)
    bias_ref[...] = col_sum(dqkv.astype(F32))


def qkv_weight_call(n1, dqkv, width, dtype):
    t, d = n1.shape
    n = dqkv.shape[1]
    return pl.pallas_call(
        qkv_weight_kernel,
        grid=(n // width,),
        out_shape=(shape((d, n), dtype), shape((1, n))),
        in_specs=[whole(t, d), pl.BlockSpec((t, width), lambda j: (0, j))],
        out_specs=(
            pl.BlockSpec((d, width), lambda j: (0, j)),
            pl.BlockSpec((1, width), lambda j: (0, j)),
        ),
        scratch_shapes=[pltpu.VMEM((d, t), BF)],
        compiler_params=params(),
        name="qkv_weight_gradient",
    )(n1, dqkv)


def qkv_back_kernel(dqkv_ref, w_ref, tokens_ref, ga_ref, scale_ref, out_ref, mod_ref):
    gy = dg(dqkv_ref[...], w_ref[...], NT)
    normed, rstd = ln_parts(tokens_ref[...])
    out_ref[...] = ga_ref[...] + ln_back(gy, normed, rstd, scale_ref[0])
    mod_ref[0] = jnp.concatenate([col_sum(gy), col_sum(gy * normed)], axis=0)


def qkv_back_call(dqkv, w, tokens, ga, scale, blk):
    t, d = tokens.shape
    n = dqkv.shape[1]
    r = rows_of(blk, d)
    return pl.pallas_call(
        qkv_back_kernel,
        grid=(t // blk,),
        out_shape=(shape((t, d)), shape((t // blk, 2, d))),
        in_specs=[rows_of(blk, n), whole(d, n), r, r, row_vec(d)],
        out_specs=(r, pl.BlockSpec((1, 2, d), lambda i: (i, 0, 0))),
        compiler_params=params(),
        name="qkv_backward",
    )(dqkv, w, tokens, ga, scale)


def on_device(
    tokens,
    conditioning,
    row_items,
    head_mask,
    chan_mask,
    skip_mask,
    ada_weight,
    ada_bias,
    qkv_weight,
    query_bias,
    value_bias,
    proj_weight,
    proj_bias,
    fc1_weight,
    fc1_bias,
    fc2_weight,
    fc2_bias,
    head_router,
    head_router_bias,
    chan_router,
    chan_router_bias,
    token_router,
    cotangent,
):
    axes = ("narrow", "wide")
    t, d = tokens.shape
    slots = conditioning.shape[0]
    heads = head_mask.shape[1]
    groups = chan_mask.shape[1]
    hidden = fc1_bias.shape[0]
    hd = d // heads
    unit = hidden // groups
    blk = t // slots
    single = row_items[0] == 1
    off = jnp.where(single, 0.0, MASKED).astype(F32).reshape(1)

    def per_block(table):
        return jnp.where(single, table[:1], table)

    def per_slot(blocks):
        total = jnp.sum(blocks, axis=0, keepdims=True)
        first = (jnp.arange(slots) == 0).reshape((slots,) + (1,) * (blocks.ndim - 1))
        return jnp.where(single, jnp.where(first, total, 0.0), blocks)

    silu_cond = jax.nn.silu(conditioning.astype(F32)).astype(BF)
    every_cond = lax.all_gather(silu_cond, axes, axis=0, tiled=True)
    mod_columns = jnp.dot(every_cond, ada_weight, preferred_element_type=F32) + ada_bias.astype(F32)
    modulation = lax.all_to_all(
        mod_columns.astype(BF), axes, split_axis=0, concat_axis=1, tiled=True
    )
    mod_rows = per_block(modulation.astype(F32)).reshape(slots, 6, 1, d)
    shift1, scale1, gate1, shift2, scale2, gate2 = [mod_rows[:, k] for k in range(6)]
    cond_float = silu_cond.astype(F32)

    def router(weight, bias, mask):
        gate = jax.nn.sigmoid(
            jnp.dot(cond_float, weight.astype(F32), precision=HIGHEST) + bias.astype(F32)
        )
        mask = mask.astype(F32)
        return mask * gate, mask * gate * (1.0 - gate)

    head_gate, head_slope = router(head_router, head_router_bias, head_mask)
    chan_gate, chan_slope = router(chan_router, chan_router_bias, chan_mask)
    head_rows = jnp.repeat(per_block(head_gate), hd, axis=1)[:, None, :]
    chan_rows = jnp.repeat(per_block(chan_gate), unit, axis=1)[:, None, :]
    keep = (1.0 - skip_mask.astype(F32))[:, None]

    full_qkv = lax.all_gather(qkv_weight, axes, axis=0, tiled=True)
    full_proj = lax.all_gather(proj_weight, axes, axis=0, tiled=True)
    fc1_rows = lax.all_gather(fc1_weight, "narrow", axis=1, tiled=True)
    fc2_rows = lax.all_gather(fc2_weight, "narrow", axis=1, tiled=True)
    full_fc1 = lax.all_gather(fc1_rows, "wide", axis=0, tiled=True)
    full_fc2 = lax.all_gather(fc2_rows, "wide", axis=0, tiled=True)

    qkv_bias = jnp.concatenate([query_bias, jnp.zeros_like(query_bias), value_bias])
    n1, qkv = qkv_call(tokens, shift1, scale1, full_qkv, qkv_bias.astype(F32)[None], blk)
    att, gated, lse = attn_fwd(off, head_rows, qkv, heads, blk)
    router_row = token_router.astype(F32)[None]
    attn, after, n2, gm, tg = middle_call(
        gated,
        full_proj,
        proj_bias.astype(F32)[None],
        tokens,
        cotangent,
        keep,
        router_row,
        gate1,
        shift2,
        scale2,
        gate2,
        blk,
    )
    mlp, gn2, g_fc1, g_fc2, gb1, gch = mlp_call(
        n2, gm, full_fc1, full_fc2, fc1_bias.astype(F32)[None], chan_rows, hidden // 6, blk
    )
    output, ga, do, delta, g_proj, mods, sums = middle_back_call(
        mlp,
        gn2,
        after,
        attn,
        cotangent,
        gm,
        gated,
        att,
        tg,
        keep,
        full_proj,
        fc2_bias.astype(F32)[None],
        router_row,
        gate1,
        shift2,
        scale2,
        gate2,
        head_rows,
        heads,
        blk,
    )
    mods = mods.reshape(slots, 8, d)
    fc_sum = lax.psum_scatter(
        jnp.stack([g_fc1, g_fc2], axis=1), "wide", scatter_dimension=0, tiled=True
    )
    fc_grads = lax.psum_scatter(fc_sum, "narrow", scatter_dimension=2, tiled=True).astype(F32)
    dqkv = attn_bwd(off, qkv, do, lse, delta, heads, blk)
    g_qkv, qkv_sums = qkv_weight_call(n1, dqkv, 3 * d // 9, BF)
    attn_grads = lax.psum_scatter(
        jnp.concatenate([g_qkv, g_proj.astype(BF)], axis=1), axes, scatter_dimension=0, tiled=True
    ).astype(F32)
    grad_tokens, mods1 = qkv_back_call(dqkv, full_qkv, tokens, ga, scale1, blk)
    block_mods = jnp.concatenate(
        [mods1[:, 0], mods1[:, 1], mods[:, 0], mods[:, 1], mods[:, 2], mods[:, 3]], axis=1
    )
    grad_slot_mod = per_slot(block_mods).astype(BF)
    grad_mod_columns = lax.all_to_all(
        grad_slot_mod, axes, split_axis=1, concat_axis=0, tiled=True
    )
    grad_ada_weight = dg(every_cond, grad_mod_columns, TN)
    grad_ada_bias = jnp.sum(grad_mod_columns.astype(F32), axis=0)
    g_head = per_slot(jnp.sum(mods[:, 4].reshape(slots, heads, hd), axis=2)) * head_slope
    g_chan = per_slot(jnp.sum(gch.reshape(slots, groups, unit), axis=2)) * chan_slope
    logits = lax.all_gather(
        jnp.concatenate([g_head, g_chan], axis=1), axes, axis=0, tiled=True
    )
    router_grads = lax.dot_general(
        every_cond.astype(F32), logits, TN, precision=HIGHEST, preferred_element_type=F32
    )
    logit_sums = jnp.sum(logits, axis=0)
    small = lax.psum(
        jnp.concatenate(
            [
                qkv_sums[0, :d],
                qkv_sums[0, 2 * d :],
                sums[1],
                gb1[0],
                sums[2],
                sums[0],
            ]
        ),
        axes,
    )
    ends = [d, 2 * d, 3 * d, 3 * d + hidden, 4 * d + hidden]
    g_query, g_value, g_proj_bias, g_b1, g_b2, g_router = jnp.split(small, ends)
    return (
        output,
        grad_tokens,
        grad_ada_weight,
        grad_ada_bias,
        attn_grads[:, : 3 * d],
        g_query,
        g_value,
        attn_grads[:, 3 * d :],
        g_proj_bias,
        fc_grads[:, 0],
        g_b1,
        fc_grads[:, 1],
        g_b2,
        router_grads[:, :heads],
        logit_sums[:heads],
        router_grads[:, heads:],
        logit_sums[heads:],
        g_router,
    )


def solution(mesh):
    return jax.shard_map(
        on_device,
        mesh=mesh,
        in_specs=(
            P(("narrow", "wide"), None),
            P(("narrow", "wide"), None),
            P(("narrow", "wide")),
            P(("narrow", "wide"), None),
            P(("narrow", "wide"), None),
            P(("narrow", "wide")),
            P(None, ("narrow", "wide")),
            P(("narrow", "wide")),
            P(("narrow", "wide"), None),
            P(),
            P(),
            P(("narrow", "wide"), None),
            P(),
            P("wide", "narrow"),
            P(),
            P("wide", "narrow"),
            P(),
            P(),
            P(),
            P(),
            P(),
            P(),
            P(("narrow", "wide"), None),
        ),
        out_specs=(
            P(("narrow", "wide"), None),
            P(("narrow", "wide"), None),
            P(None, ("narrow", "wide")),
            P(("narrow", "wide")),
            P(("narrow", "wide"), None),
            P(),
            P(),
            P(("narrow", "wide"), None),
            P(),
            P("wide", "narrow"),
            P(),
            P("wide", "narrow"),
            P(),
            P(),
            P(),
            P(),
            P(),
            P(),
        ),
        check_vma=False,
    )
```

time: 1400 us -> 1000 us (0.71)
  matrix products: 543 us -> 2.24 us
  Pallas kernels: 0 us -> 278 us
  blocking collectives: 85.5 us -> 310 us
  local copies, waits for them, and re-layouts: 197 us -> 53.3 us
  other arithmetic: 166 us -> 34.3 us
  waiting for transfers between devices: 367 us -> 269 us
    dot_general x140 -> x5, matrix products: 543 us -> 2.24 us  [the longest x1 1.3 us: dg(): return lax.dot_general(a, b, dims, preferred_element_type=F32)]
    pallas_call x0 -> x8, Pallas kernels: none -> 278 us  [the longest x1 84.9 us: mlp_call(): pl.pallas_call(functools.partial(mlp_kernel, blk=blk), grid=(ff // hb,),...]
    unnamed x11 -> x13, waiting for transfers between devices: 272 us -> 8.43 us
    unnamed x0 -> x1, blocking collectives: none -> 191 us
    all_gather x6, waiting for transfers between devices: 95.5 us -> 259 us  [the longest x1 100 us: on_device(): full_fc2 = lax.all_gather(fc2_rows, 'wide', axis=0, tiled=True)]
    reduce_sum x26 -> x9, other arithmetic: 57.2 us -> 1.53 us  [the longest x5 0.69 us: per_slot(): total = jnp.sum(blocks, axis=0, keepdims=True)]
    while x35 -> x0, local copies, waits for them, and re-layouts: 49.4 us -> none
    all_gather x1 -> x2, blocking collectives: 42 us -> 79.1 us  [the longest x1 41.8 us: on_device(): every_cond = lax.all_gather(silu_cond, axes, axis=0, tiled=True)]
  transfers between devices with their start and end apart: 11 -> 14, of which waited for: 4 -> 8; matrix products, arithmetic and copies ran while one was open for 51% -> 26% of each run, Pallas kernels for 0% -> 20%
where the time goes in v1:
time: 1000 us; the launch traced here: 983 us
  blocking collectives  310 us (31%)
  Pallas kernels  278 us (28%)
  waiting for transfers between devices  269 us (27%)
  local copies, waits for them, and re-layouts  53.3 us (5%)
  other arithmetic  34.3 us (3%)
  starting transfers between devices  19.1 us (2%)
  between operations  16.7 us (2%)
    unnamed x1, blocking collectives  191 us
    all_gather x1, waiting for transfers between devices, on_device(): full_fc2 = lax.all_gather(fc2_rows, 'wide', axis=0, tiled=True)  100 us
    pallas_call x1, Pallas kernels, mlp_call(): pl.pallas_call(functools.partial(mlp_kernel, blk=blk), grid=(ff // hb,),...  84.9 us
    all_gather x1, waiting for transfers between devices, on_device(): full_qkv = lax.all_gather(qkv_weight, axes, axis=0, tiled=True)  75.9 us
    pallas_call x1, Pallas kernels, attn_bwd(): pl.pallas_call(functools.partial(attn_bwd_kernel, heads=heads, blk=blk),...  58.5 us
    pallas_call x1, Pallas kernels, attn_fwd(): pl.pallas_call(functools.partial(attn_fwd_kernel, heads=heads, blk=blk),...  42.1 us
    all_gather x1, blocking collectives, on_device(): every_cond = lax.all_gather(silu_cond, axes, axis=0, tiled=True)  41.8 us
    psum x1, blocking collectives, on_device(): lax.psum(jnp.concatenate([qkv_sums[0, :d], qkv_sums[0, 2 * d:], sums[1],...  40.3 us
  transfers between devices with their start and end apart: 14, of which 8 were waited for; matrix products, arithmetic and copies ran while one was open for 26% of the time, Pallas kernels for 20%

profile of v1, /device:TPU:0, one launch (start us, length us, event | category | flops | bytes accessed | tf_op | source)
XLA Modules:
  0.0 983.2 jit_solution(16377092446634799565)
XLA Ops:
  10.1 32.7 %all-gather.11.cloned.1.call-done = bf16[576,1152]{0,1:T(8,128)(2,1)} async-done(((bf16[576,288]{0,1:T(8,128)(2,1)}), bf16[576,1152]{0,1:T(8,128)(2,1)}) %all-gather.11.cloned.1.call-update) | async-done | bytes 1327120 | tf_op jit(solution)/shard_map/all_gather | solution.py:563
  45.5 29.4 %all-gather.15.cloned.1.call-done = bf16[576,1152]{0,1:T(8,128)(2,1)} async-done(((bf16[576,288]{0,1:T(8,128)(2,1)}), bf16[576,1152]{0,1:T(8,128)(2,1)}) %all-gather.15.cloned.1.call-update) | async-done | bytes 1327120 | tf_op jit(solution)/shard_map/all_gather | solution.py:564
  77.5 41.8 %all-gather = bf16[32,4,1152]{2,1,0:T(4,128)(2,1)S(1)} all-gather(bf16[1,4,1152]{2,1,0:T(4,128)(2,1)S(1)} %fusion.23), channel_id=1, replica_groups=mesh['narrow'=4,'wide'=8] {'narrow','wide'}, dimensions={0}, use_global_device_ids=true | all-gather | bytes 304128 | tf_op jit(solution)/shard_map/all_gather | solution.py:539
  137.1 5.2 reshape.156.w_ref
  142.3 75.9 %all-gather.19.cloned.1.call-done = bf16[32,36,3456]{2,1,0:T(8,128)(2,1)} async-done(((bf16[1,36,3456]{2,1,0:T(8,128)(2,1)}), bf16[32,36,3456]{2,1,0:T(8,128)(2,1)}) %all-gather.19.cloned.1.call-update) | async-done | bytes 7962640 | tf_op jit(solution)/shard_map/all_gather | solution.py:561
  218.2 12.8 %reshape.154.w_ref = bf16[1152,3456]{1,0:T(8,128)(2,1)} reshape(bf16[32,36,3456]{2,1,0:T(8,128)(2,1)} %all-gather.19.cloned.1.call-done) | data formatting | bytes 15925248
  230.9 16.2 %qkv_forward.1 = (bf16[1024,1152]{1,0:T(8,128)(2,1)}, bf16[1024,3456]{1,0:T(8,128)(2,1)}) custom-call(f32[1024,1152]{1,0:T(8,128)} %tokens_ref.5, f32[4,1,1152]{2,1,0:T(1,128)} %get-tuple-element.128.shift_ref, f32[4,1,1152]{2,1,0:T(1,128)} %get-tuple-element.127.scale_ref, bf16[1152,3456]{1,0:T(8,128)(2,1)} %reshape.154.w_ref, f32[1,3456]{1,0:T(1,128)} %fusion.20.bias_ref), custom_call_target="tpu_custom_call" | custom-call | tf_op jit(solution)/shard_map/qkv_forward/pallas_call | solution.py:84
  247.1 42.1 %attention_forward.1 = (f32[1024,1152]{1,0:T(8,128)}, bf16[1024,1152]{1,0:T(8,128)(2,1)}, f32[16,1024]{1,0:T(8,128)}) custom-call(f32[1]{0:T(128)} %bitcast.1.off_ref, f32[4,1,1152]{2,1,0:T(1,128)} %broadcast_in_dim_reshape.6.gate_ref.head_ref, bf16[1024,3456]{1,0:T(8,128)(2,1)} %get-tuple-element.45.qkv_ref), custom_call_target="tpu_custom_call" | custom-call | tf_op jit(solution)/shard_map/attention_forward/pallas_call | solution.py:141
  289.2 13.9 %middle_forward.1 = (f32[1024,1152]{1,0:T(8,128)}, f32[1024,1152]{1,0:T(8,128)}, bf16[1024,1152]{1,0:T(8,128)(2,1)}, bf16[1024,1152]{1,0:T(8,128)(2,1)}, f32[1024,1]{1,0:T(8,128)}) custom-call(bf16[1024,1152]{1,0:T(8,128)(2,1)} %get-tuple-element.46.gated_ref, bf16[1152,1152]{1,0:T(8,128)(2,1)} %reshape.156.w_ref, f32[1,1152]{1,0:T(1,128)} %reshape.147.bias_ref, ...), custom_call_target="tpu_custom_call" | custom-call | tf_op jit(solution)/shard_map/middle_forward/pallas_call | solution.py:254
  303.0 15.7 %all-gather.13.cloned.1.call-done.w1_ref = bf16[4608,1152]{1,0:T(8,128)(2,1)} async-done(((bf16[576,1152]{1,0:T(8,128)(2,1)}), bf16[4608,1152]{1,0:T(8,128)(2,1)}) %all-gather.13.cloned.1.call-update) | async-done | bytes 10616848 | tf_op jit(solution)/shard_map/all_gather | solution.py:565
  318.8 100.4 %all-gather.17.cloned.1.call-done.w2_ref = bf16[4608,1152]{1,0:T(8,128)(2,1)} async-done(((bf16[576,1152]{1,0:T(8,128)(2,1)}), bf16[4608,1152]{1,0:T(8,128)(2,1)}) %all-gather.17.cloned.1.call-update) | async-done | bytes 10616848 | tf_op jit(solution)/shard_map/all_gather | solution.py:566
  419.2 84.9 %feed_forward.1 = (f32[1024,1152]{1,0:T(8,128)}, f32[1024,1152]{1,0:T(8,128)}, bf16[4608,1152]{1,0:T(8,128)(2,1)}, bf16[4608,1152]{1,0:T(8,128)(2,1)}, f32[1,4608]{1,0:T(1,128)}, /*index=5*/f32[4,1,4608]{2,1,0:T(1,128)}) custom-call(bf16[1024,1152]{1,0:T(8,128)(2,1)} %get-tuple-element.47.n2_ref, bf16[1024,1152]{1,0:T(8,128)(2,1)} %get-tuple-element.48.gm_ref, ...), custom_call_target="tpu_custom_call" | custom-call | tf_op jit(solution)/shard_map/feed_forward/pallas_call | solution.py:305
  504.0 17.8 %pad_maximum_fusion = bf16[4608,2,1152]{2,0,1:T(8,128)(2,1)} fusion(bf16[4608,1,1152]{2,0,1:T(8,128)(2,1)} %bitcast.71, bf16[4608,1,1152]{2,0,1:T(8,128)(2,1)} %bitcast.70), kind=kLoop, calls=%fused_computation | loop fusion | flops 10616832 | bytes 42467328 | tf_op jit(solution)/shard_map/stack | solution.py:613
  524.4 27.9 %middle_backward.1 = (f32[1024,1152]{1,0:T(8,128)}, f32[1024,1152]{1,0:T(8,128)}, bf16[1024,1152]{1,0:T(8,128)(2,1)}, f32[16,1024]{1,0:T(8,128)}, f32[1152,1152]...) custom-call(f32[1024,1152]{1,0:T(8,128)} %get-tuple-element.49.mlp_ref, f32[1024,1152]{1,0:T(8,128)} %get-tuple-element.50.gn2_ref, ...), custom_call_target="tpu_custom_call" | custom-call | tf_op jit(solution)/shard_map/middle_backward/pallas_call | solution.py:416
  552.2 58.5 %attention_backward.1.dqkv_ref = bf16[1024,3456]{1,0:T(8,128)(2,1)} custom-call(f32[1]{0:T(128)} %bitcast.1.off_ref, bf16[1024,3456]{1,0:T(8,128)(2,1)} %get-tuple-element.45.qkv_ref, bf16[1024,1152]{1,0:T(8,128)(2,1)} %get-tuple-element.56.do_ref, f32[16,1024]{1,0:T(8,128)} %get-tuple-element.57.lse_ref, f32[16,1024]{1,0:T(8,128)} %get-tuple-element.58.delta_ref), custom_call_target="tpu_custom_call" | custom-call | tf_op jit(solution)/shard_map/attention_backward/pallas_call | solution.py:209
  610.8 18.3 %qkv_backward.1 = (f32[1024,1152]{1,0:T(8,128)}, f32[4,2,1152]{2,1,0:T(2,128)}) custom-call(bf16[1024,3456]{1,0:T(8,128)(2,1)} %attention_backward.1.dqkv_ref, bf16[1152,3456]{1,0:T(8,128)(2,1)} %reshape.154.w_ref, f32[1024,1152]{1,0:T(8,128)} %tokens_ref.5, f32[1024,1152]{1,0:T(8,128)} %get-tuple-element.59.ga_ref, f32[4,1,1152]{2,1,0:T(1,128)} %get-tuple-element.127.scale_ref), custom_call_target="tpu_custom_call" | custom-call | tf_op jit(solution)/shard_map/qkv_backward/pallas_call | solution.py:482
  632.3 16.5 %qkv_weight_gradient.1 = (bf16[1152,3456]{1,0:T(8,128)(2,1)}, f32[1,3456]{1,0:T(1,128)}) custom-call(bf16[1024,1152]{1,0:T(8,128)(2,1)} %get-tuple-element.63.n1_ref, bf16[1024,3456]{1,0:T(8,128)(2,1)} %attention_backward.1.dqkv_ref), custom_call_target="tpu_custom_call" | custom-call | tf_op jit(solution)/shard_map/qkv_weight_gradient/pallas_call | solution.py:456
  655.4 8.7 pad_maximum_fusion.1
  664.2 190.8 %fusion = bf16[40,4608]{1,0:T(8,128)(2,1)S(1)} fusion(bf16[1152,4608]{1,0:T(8,128)(2,1)} %pad_maximum_fusion.1), kind=kCustom, calls=%all-reduce-scatter | all-reduce-scatter fusion | flops 5898241 | bytes 10985472
  855.0 10.3 %copy.112 = bf16[576,2,1152]{0,1,2:T(2,128)(2,1)} copy(bf16[576,2,1152]{2,0,1:T(8,128)(2,1)} %reduce-scatter.4.cloned.1.call-done) | data formatting | bytes 5308416 | tf_op jit(solution)/shard_map/reduce_scatter | solution.py:612
  865.5 37.3 %all-gather.3 = f32[32,4,48]{2,1,0:T(4,128)S(1)} all-gather(f32[1,4,48]{2,1,0:T(4,128)S(1)} %maximum_bitcast_fusion), channel_id=1, replica_groups=mesh['narrow'=4,'wide'=8] {'narrow','wide'}, dimensions={0}, use_global_device_ids=true | all-gather | bytes 25344 | tf_op jit(solution)/shard_map/all_gather | solution.py:633
  903.0 40.3 %psum.7 = f32[10368]{0:T(1024)S(1)} all-reduce(f32[10368]{0:T(1024)S(1)} %constant_dynamic-update-slice_fusion.4), channel_id=1, replica_groups=mesh['narrow'=4,'wide'=8] {'narrow','wide'}, use_global_device_ids=true, to_apply=%region_3.4 | all-reduce | flops 10368 | bytes 82944 | tf_op jit(solution)/shard_map/psum | solution.py:640
  954.7 5.6 collective-permute-start.3
  962.3 5.8 collective-permute-done.3
  (171 shorter events, 58.0 us)
Async XLA Ops:
  7.2 112.2 %copy-start = (bf16[1152,216]{0,1:T(8,128)(2,1)S(1)}, bf16[1152,216]{0,1:T(8,128)(2,1)}, u32[]{:S(2)}) copy-start(bf16[1152,216]{0,1:T(8,128)(2,1)} %param.29) | copy-start | bytes 1492996
  7.2 35.6 %all-gather.11.cloned.1.call-start = ((), (), s32[]{:S(2)}) async-start(), calls=%async_computation.3 | async-start | bytes 1843200 | tf_op jit(solution)/shard_map/all_gather | solution.py:563
  8.0 66.9 %all-gather.15.cloned.1.call-start = ((), (), s32[]{:S(2)}) async-start(), calls=%async_computation.5 | async-start | bytes 1843200 | tf_op jit(solution)/shard_map/all_gather | solution.py:564
  8.7 128.4 %all-gather.21.cloned.1.call-start = ((), (), s32[]{:S(2)}) async-start(), calls=%async_computation.9 | async-start | bytes 3041280 | tf_op jit(solution)/shard_map/all_gather | solution.py:562
  9.4 208.7 %all-gather.19.cloned.1.call-start = ((), (), s32[]{:S(2)}) async-start(), calls=%async_computation.8 | async-start | bytes 9123840 | tf_op jit(solution)/shard_map/all_gather | solution.py:561
  9.5 109.9 %copy-start.20 = (bf16[216]{0:T(256)(128)(2,1)S(1)}, bf16[216]{0:T(256)(128)(2,1)}, u32[]{:S(2)}) copy-start(bf16[216]{0:T(256)(128)(2,1)} %param.30) | copy-start | bytes 1300
  10.0 113.7 %copy-start.9 = (bf16[1152]{0:T(1024)(128)(2,1)S(1)}, bf16[1152]{0:T(1024)(128)(2,1)}, u32[]{:S(2)}) copy-start(bf16[1152]{0:T(1024)(128)(2,1)} %param.32) | copy-start | bytes 6916
  10.0 113.7 %copy-start.10 = (bf16[1152]{0:T(1024)(128)(2,1)S(1)}, bf16[1152]{0:T(1024)(128)(2,1)}, u32[]{:S(2)}) copy-start(bf16[1152]{0:T(1024)(128)(2,1)} %param.33) | copy-start | bytes 6916
  10.0 113.8 %copy-start.21 = (bf16[16]{0:T(256)(128)(2,1)S(1)}, bf16[16]{0:T(256)(128)(2,1)}, u32[]{:S(2)}) copy-start(bf16[16]{0:T(256)(128)(2,1)} %param.41) | copy-start | bytes 100
  10.0 113.8 %copy-start.22 = (bf16[32]{0:T(256)(128)(2,1)S(1)}, bf16[32]{0:T(256)(128)(2,1)}, u32[]{:S(2)}) copy-start(bf16[32]{0:T(256)(128)(2,1)} %param.43) | copy-start | bytes 196
  10.1 113.8 %copy-start.17 = (bf16[1152,16]{0,1:T(8,128)(2,1)S(1)}, bf16[1152,16]{0,1:T(8,128)(2,1)}, u32[]{:S(2)}) copy-start(bf16[1152,16]{0,1:T(8,128)(2,1)} %param.40) | copy-start | bytes 110596
  10.1 113.8 %copy-start.18 = (s32[4,16]{1,0:T(4,128)S(1)}, s32[4,16]{1,0:T(4,128)}, u32[]{:S(2)}) copy-start(s32[4,16]{1,0:T(4,128)} %param.26) | copy-start | bytes 772
  10.1 114.0 %copy-start.16 = (bf16[1152,32]{0,1:T(8,128)(2,1)S(1)}, bf16[1152,32]{0,1:T(8,128)(2,1)}, u32[]{:S(2)}) copy-start(bf16[1152,32]{0,1:T(8,128)(2,1)} %param.42) | copy-start | bytes 221188
  10.1 114.0 %copy-start.19 = (s32[4,32]{1,0:T(4,128)S(1)}, s32[4,32]{1,0:T(4,128)}, u32[]{:S(2)}) copy-start(s32[4,32]{1,0:T(4,128)} %param.27) | copy-start | bytes 1540
  10.1 308.7 %all-gather.13.cloned.1.call-start = ((), (), s32[]{:S(2)}) async-start(), calls=%async_computation.4 | async-start | bytes 11943936 | tf_op jit(solution)/shard_map/all_gather | solution.py:565
  45.4 373.8 %all-gather.17.cloned.1.call-start = ((), (), s32[]{:S(2)}) async-start(), calls=%async_computation.6 | async-start | bytes 11943936 | tf_op jit(solution)/shard_map/all_gather | solution.py:566
  120.5 10.5 %all-to-all-start = ((bf16[32,4,216]{2,1,0:T(4,128)(2,1)}), bf16[32,4,216]{2,1,0:T(4,128)(2,1)S(1)}, u32[]{:S(2)}, u32[]{:S(2)}) async-start(bf16[32,4,216]{2,1,0:T(4,128)(2,1)} %all_to_all.22), calls=%async_computation | async-start | bytes 131072 | tf_op jit(solution)/shard_map/all_to_all | solution.py:541
  123.0 732.0 %reduce-scatter.4.cloned.1.call-start = ((), (), s32[]{:S(2)}) async-start(), calls=%async_computation.7 | async-start | bytes 23887872 | tf_op jit(solution)/shard_map/reduce_scatter | solution.py:612
  652.5 307.8 %all-to-all-start.1 = ((bf16[4,32,216]{2,0,1:T(4,128)(2,1)}), bf16[4,32,216]{2,0,1:T(4,128)(2,1)S(1)}, u32[]{:S(2)}, u32[]{:S(2)}) async-start(bf16[4,32,216]{2,0,1:T(4,128)(2,1)} %fusion.10), calls=%async_computation.1 | async-start | bytes 131072 | tf_op jit(solution)/shard_map/all_to_all | solution.py:626
  655.2 316.7 %all-reduce.5.cloned.1.call-start = ((), (), s32[]{:S(2)}) async-start(), calls=%async_computation.10 | async-start | bytes 5898240
  946.2 21.9 %collective-permute-start = (bf16[40,4608]{1,0:T(8,128)(2,1)S(1)}, bf16[40,4608]{1,0:T(8,128)(2,1)S(1)}, u32[]{:S(2)}, u32[]{:S(2)}) collective-permute-start(bf16[40,4608]{1,0:T(8,128)(2,1)S(1)} %fusion), channel_id=1, source_target_pairs={{0,1},{1,2},{2,3},{3,4},{4,5},{5,6},{6,7},{7,8},{8,9},{9,10},{10,1... | collective-permute-start | bytes 1105928
  948.0 20.1 %collective-permute-start.1 = (bf16[40,4608]{1,0:T(8,128)(2,1)S(1)}, bf16[40,4608]{1,0:T(8,128)(2,1)S(1)}, u32[]{:S(2)}, u32[]{:S(2)}) collective-permute-start(bf16[40,4608]{1,0:T(8,128)(2,1)S(1)} %fusion), channel_id=1, source_target_pairs={{0,2},{1,3},{2,4},{3,5},{4,6},{5,7},{6,8},{7,9},{8,10},{9,11},{10,... | collective-permute-start | bytes 1105928
  950.4 17.7 %collective-permute-start.2 = (bf16[40,4608]{1,0:T(8,128)(2,1)S(1)}, bf16[40,4608]{1,0:T(8,128)(2,1)S(1)}, u32[]{:S(2)}, u32[]{:S(2)}) collective-permute-start(bf16[40,4608]{1,0:T(8,128)(2,1)S(1)} %fusion), channel_id=1, source_target_pairs={{0,3},{1,4},{2,5},{3,6},{4,7},{5,8},{6,9},{7,10},{8,11},{9,12},{10... | collective-permute-start | bytes 1105928
  954.7 13.4 %collective-permute-start.3 = (bf16[4,4608]{1,0:T(4,128)(2,1)S(1)}, bf16[4,4608]{1,0:T(4,128)(2,1)S(1)}, u32[]{:S(2)}, u32[]{:S(2)}) collective-permute-start(bf16[4,4608]{1,0:T(4,128)(2,1)S(1)} %slice.137), channel_id=1, source_target_pairs={{0,4},{1,5},{2,6},{3,7},{4,8},{5,9},{6,10},{7,11},{8,12},{9,13},{1... | collective-permute-start | bytes 110600
  (14 other events, 574.1 us)
Sparse Core Ops, SparseCore 0:
  9.9 32.8 all-gather.10
  44.6 30.1 all-gather.14
  77.7 59.3 all-gather.20
  139.8 78.2 all-gather.18
  219.6 99.0 all-gather.12
  320.3 98.8 all-gather.16
  522.0 266.4 reduce-scatter.3
  865.5 81.8 all-reduce.4

commit v2 on v1

--- a/solution.py
+++ b/solution.py
@@ -18,6 +18,8 @@
 NT = (((1,), (1,)), ((), ()))
 TN = (((0,), (0,)), ((), ()))
 VMEM_SPEC = pl.BlockSpec(memory_space=pltpu.VMEM)
+ANY_SPEC = pl.BlockSpec(memory_space=pl.ANY)
+MESH = pl.DeviceIdType.MESH
 SMEM_SPEC = pl.BlockSpec(memory_space=pltpu.SMEM)
 
 
@@ -25,8 +27,37 @@
     return lax.dot_general(a, b, dims, preferred_element_type=F32)
 
 
-def params(mib=60):
-    return pltpu.CompilerParams(vmem_limit_bytes=mib << 20)
+def params(mib=60, collective_id=None):
+    if collective_id is None:
+        return pltpu.CompilerParams(vmem_limit_bytes=mib << 20)
+    return pltpu.CompilerParams(
+        vmem_limit_bytes=mib << 20, collective_id=collective_id, has_side_effects=True
+    )
+
+
+def up_to(count, multiple):
+    return -(-count // multiple) * multiple
+
+
+def pad_rows(x):
+    return jnp.pad(x, ((0, up_to(x.shape[0], 16) - x.shape[0]), (0, 0)))
+
+
+def spread_out(steps, count):
+    groups = [[] for _ in range(count)]
+    for i, step in enumerate(steps):
+        groups[i * count // len(steps)].append(step)
+    return groups
+
+
+def run_at(index, groups):
+    for i, group in enumerate(groups):
+        if group:
+
+            @pl.when(index == i)
+            def _(group=group):
+                for step in group:
+                    step()
 
 
 def shape(dims, dtype=F32):
@@ -34,7 +65,7 @@
 
 
 def whole(*dims):
-    return pl.BlockSpec(dims, lambda i: (0,) * len(dims))
+    return pl.BlockSpec(dims, lambda i: (0,) * len(dims), pipeline_mode=pl.Buffered(1))
 
 
 def rows_of(block, width):
@@ -71,25 +102,401 @@
     return x * half, half + 0.5 * x * (1.0 - t * t) * (k0 * (1.0 + 3.0 * k1 * x2))
 
 
-def qkv_kernel(tokens_ref, shift_ref, scale_ref, w_ref, bias_ref, n1_ref, qkv_ref):
+class Place:
+    def __init__(self, planes):
+        self.planes = planes
+        self.n = lax.axis_index("narrow")
+        w = lax.axis_index("wide")
+        self.z = w // 2
+        self.c = w % 2
+        self.xn = self.n + 1 - 2 * (self.n % 2)
+        self.yn = self.n + 2 - 4 * (self.n // 2)
+        self.dn = 3 - self.n
+
+    def dev(self, n, z, c):
+        return (n, z * 2 + c)
+
+    def barrier(self, every_plane=False):
+        sem = pltpu.get_barrier_semaphore()
+
+        def greet(n, z, c):
+            pl.semaphore_signal(sem, inc=1, device_id=self.dev(n, z, c), device_id_type=MESH)
+
+        greet(self.xn, self.z, self.c)
+        greet(self.yn, self.z, self.c)
+        greet(self.n, self.z, 1 - self.c)
+        if every_plane:
+            for k in range(1, self.planes):
+                greet(self.n, lax.rem(self.z + k, self.planes), self.c)
+            pl.semaphore_wait(sem, self.planes + 2)
+            return
+        for step in (-1, 1):
+
+            @pl.when(self.has(step))
+            def _(step=step):
+                greet(self.n, self.z + step, self.c)
+
+        ends = jnp.where(self.z > 0, 1, 0) + jnp.where(self.z < self.planes - 1, 1, 0)
+        pl.semaphore_wait(sem, 3 + ends)
+
+    def has(self, step):
+        return self.z + step >= 0 if step < 0 else self.z + step < self.planes
+
+
+def remote(src, dst, sems, idx, device):
+    return pltpu.make_async_remote_copy(
+        src_ref=src,
+        dst_ref=dst,
+        send_sem=sems.at[0, idx],
+        recv_sem=sems.at[1, idx],
+        device_id=device,
+        device_id_type=MESH,
+    )
+
+
+class Gather:
+    def __init__(self, place, src, out, own, zs, xs, ys, ds, cs):
+        self.p, self.src, self.out = place, src, out
+        self.own, self.zs, self.xs, self.ys, self.ds, self.cs = own, zs, xs, ys, ds, cs
+        self.steps = [0]
+        for k in range(1, place.planes):
+            self.steps += [-k, k]
+
+    def index(self, k):
+        return k + self.p.planes - 1
+
+    def at(self, n, k, c=None):
+        p = self.p
+        return self.out.at[n, p.z + k, p.c if c is None else c]
+
+    def mine(self, k):
+        return self.src if k == 0 else self.at(self.p.n, k)
+
+    def via(self, k):
+        p = self.p
+        return (p.xn, p.yn) if k % 2 == 0 else (p.yn, p.xn)
+
+    def copy(self, kind, k):
+        p = self.p
+        i = self.index(k)
+        if kind == "x":
+            return remote(self.mine(k), self.at(p.n, k), self.xs, i, p.dev(p.xn, p.z, p.c))
+        if kind == "y":
+            return remote(self.mine(k), self.at(p.n, k), self.ys, i, p.dev(p.yn, p.z, p.c))
+        if kind == "d":
+            via, to = self.via(k)
+            return remote(self.at(via, k), self.at(via, k), self.ds, i, p.dev(to, p.z, p.c))
+        if kind == "up" or kind == "down":
+            step = 1 if kind == "up" else -1
+            j = self.index(k - step)
+            return remote(self.mine(k), self.at(p.n, k), self.zs, j, p.dev(p.n, p.z + step, p.c))
+        j = ("c", "C", "d2", "D").index(kind)
+        n = (p.n, p.xn, p.yn, p.dn)[j]
+        shard = self.mine(k) if j == 0 else self.at(n, k)
+        slot = j * (2 * p.planes - 1) + i
+        return remote(shard, self.at(n, k), self.cs, slot, p.dev(p.n, p.z, 1 - p.c))
+
+    def arrived(self, n, k, sems, idx, c=None):
+        p = self.p
+        dst = self.at(n, k, c)
+        remote(dst, dst, sems, idx, p.dev(p.xn, p.z, p.c)).wait_recv()
+
+    def run(self, part):
+        if part == "begin":
+            pltpu.make_async_copy(self.src, self.at(self.p.n, 0), self.own).start()
+            self.spread(0)
+        elif part == "end":
+            pltpu.make_async_copy(self.src, self.at(self.p.n, 0), self.own).wait()
+            for k in self.steps:
+                self.when(self.p.has(k), functools.partial(self.finish, k))
+        else:
+            kind, k = part
+            self.when(self.p.has(k), functools.partial(getattr(self, kind), k))
+
+    def when(self, cond, do):
+        pl.when(cond)(do)
+
+    def onward(self, k, act):
+        p = self.p
+        if k <= 0:
+            self.when(p.has(1), lambda: act(self.copy("up", k)))
+        if k >= 0:
+            self.when(p.has(-1), lambda: act(self.copy("down", k)))
+
+    def spread(self, k):
+        self.onward(k, lambda copy: copy.start())
+        self.copy("x", k).start()
+        self.copy("y", k).start()
+        self.copy("c", k).start()
+
+    def plane(self, k):
+        self.arrived(self.p.n, k, self.zs, self.index(k))
+        self.spread(k)
+
+    def near(self, k):
+        p = self.p
+        self.arrived(p.xn, k, self.xs, self.index(k))
+        if k % 2 == 0:
+            self.copy("d", k).start()
+        self.copy("C", k).start()
+        self.arrived(p.yn, k, self.ys, self.index(k))
+        if k % 2 == 1:
+            self.copy("d", k).start()
+        self.copy("d2", k).start()
+
+    def far(self, k):
+        self.arrived(self.p.dn, k, self.ds, self.index(k))
+        self.copy("D", k).start()
+
+    def finish(self, k):
+        p = self.p
+        for j, n in enumerate((p.n, p.xn, p.yn, p.dn)):
+            self.arrived(n, k, self.cs, j * (2 * p.planes - 1) + self.index(k), 1 - p.c)
+        for kind in ("x", "y", "d", "c", "C", "d2", "D"):
+            self.copy(kind, k).wait_send()
+        self.onward(k, lambda copy: copy.wait_send())
+
+    def parts(self):
+        found = ["begin"]
+        rounds = [[0]] + [[-k, k] for k in range(1, self.p.planes)]
+        for r in range(len(rounds) + 2):
+            if 0 < r < len(rounds):
+                found += [("plane", k) for k in rounds[r]]
+            if 1 <= r <= len(rounds):
+                found += [("near", k) for k in rounds[r - 1]]
+            if 2 <= r:
+                found += [("far", k) for k in rounds[r - 2]]
+        return found + ["end"]
+
+    @staticmethod
+    def scratch(planes):
+        dma = pltpu.SemaphoreType.DMA
+        span = 2 * planes - 1
+        return [dma(())] + [dma((2, span))] * 4 + [dma((2, 4 * span))]
+
+
+class Scatter:
+    def __init__(self, place, part, out, own, r1, r2, r3, r4, own_sem, s1, s2, s3, s4):
+        self.p, self.part, self.out = place, part, out
+        self.own, self.r1, self.r2, self.r3, self.r4 = own, r1, r2, r3, r4
+        self.own_sem, self.s1, self.s2, self.s3, self.s4 = own_sem, s1, s2, s3, s4
+
+    def owner(self, j):
+        return lax.rem(self.p.z + 1 + j, self.p.planes)
+
+    def load(self, j):
+        p = self.p
+        return pltpu.make_async_copy(
+            self.part.at[:, self.owner(j), p.c], self.own.at[j % 2], self.own_sem.at[j % 2]
+        )
+
+    def sides(self, j):
+        p = self.p
+        return (p.xn, p.yn) if j % 2 == 0 else (p.yn, p.xn)
+
+    def copies(self, stage, j):
+        p = self.p
+        side, other = self.sides(j)
+        if stage == 1:
+            to = p.dev(p.n, p.z, 1 - p.c)
+            return [remote(self.part.at[:, self.owner(j), 1 - p.c], self.r1.at[j], self.s1, j, to)]
+        if stage == 2:
+            to = p.dev(side, p.z, p.c)
+            return [
+                remote(self.r1.at[j, side], self.r2.at[j, 0], self.s2, 2 * j, to),
+                remote(self.r1.at[j, p.dn], self.r2.at[j, 1], self.s2, 2 * j + 1, to),
+            ]
+        if stage == 3:
+            to = p.dev(other, p.z, p.c)
+            return [remote(self.r1.at[j, other], self.r3.at[j], self.s3, j, to)]
+        to = p.dev(p.n, self.owner(j), p.c)
+        return [remote(self.r1.at[j, p.n], self.r4.at[j], self.s4, j, to)]
+
+    def issue(self, stage, j):
+        for copy in self.copies(stage, j):
+            copy.start()
+
+    def take(self, stage, j):
+        p = self.p
+        for copy in self.copies(stage, j):
+            copy.wait_recv()
+        side, other = self.sides(j)
+
+        def add(n, value):
+            self.r1[j, n] = (self.r1[j, n].astype(F32) + value.astype(F32)).astype(BF)
+
+        if stage == 1:
+            self.load(j).wait()
+            if j + 1 < p.planes:
+                self.load(j + 1).start()
+            for n in range(4):
+                add(n, self.own[j % 2, n])
+        elif stage == 2:
+            add(p.n, self.r2[j, 0])
+            add(other, self.r2[j, 1])
+        else:
+            add(p.n, self.r3[j])
+            if j + 1 < p.planes:
+                self.issue(4, j)
+
+    def end(self):
+        planes = self.p.planes
+        total = self.r1[planes - 1, self.p.n].astype(F32)
+        for j in range(planes - 1):
+            self.copies(4, j)[0].wait_recv()
+            total = total + self.r4[j].astype(F32)
+        self.out[...] = total
+        for j in range(planes):
+            for stage in (1, 2, 3, 4):
+                if stage < 4 or j + 1 < planes:
+                    for copy in self.copies(stage, j):
+                        copy.wait_send()
+
+    @staticmethod
+    def scratch(planes, rows, cols):
+        dma = pltpu.SemaphoreType.DMA
+        return [
+            pltpu.VMEM((2, 4, rows, cols), BF),
+            pltpu.VMEM((planes, 4, rows, cols), BF),
+            pltpu.VMEM((planes, 2, rows, cols), BF),
+            pltpu.VMEM((planes, rows, cols), BF),
+            pltpu.VMEM((planes - 1, rows, cols), BF),
+            dma((2,)),
+            dma((2, planes)),
+            dma((2, 2 * planes)),
+            dma((2, planes)),
+            dma((2, planes)),
+        ]
+
+
+def scatter_steps(scatters, window=2):
+    planes = scatters[0].p.planes
+    count = len(scatters)
+    queue = [(u, j) for j in range(planes) for u in range(count)]
+    x_items, y_items = [], []
+    for even in range(0, planes, 2):
+        for stage, swap in ((2, 0), (3, 1)):
+            x_items += [(stage, u, even + swap) for u in range(count)]
+            y_items += [(stage, u, even + 1 - swap) for u in range(count)]
+    sent = []
+    done = []
+
+    def begin():
+        for s in scatters:
+            s.load(0).start()
+        for u, j in queue[:window]:
+            scatters[u].issue(1, j)
+            sent.append((u, j))
+
+    def ready(stage, u, j):
+        if stage == 2:
+            while (u, j) not in done:
+                v, i = queue[len(done)]
+                scatters[v].take(1, i)
+                done.append((v, i))
+                if len(sent) < len(queue):
+                    v, i = queue[len(sent)]
+                    scatters[v].issue(1, i)
+                    sent.append((v, i))
+
+    def step(i):
+        for items in (x_items, y_items):
+            if i >= window:
+                stage, u, j = items[i - window]
+                scatters[u].take(stage, j)
+        for items in (x_items, y_items):
+            if i < len(items):
+                stage, u, j = items[i]
+                ready(stage, u, j)
+                scatters[u].issue(stage, j)
+
+    def end():
+        for s in scatters:
+            s.end()
+
+    steps = [functools.partial(step, i) for i in range(len(x_items) + window)]
+    return [begin] + steps + [end]
+
+
+def prologue_kernel(
+    shard_ref, cond_ref, ada_ref, ada_bias_ref, g_ref, conds_ref, mods_ref, mod_local, *sems, planes, items
+):
+    place = Place(planes)
+    place.barrier()
+    weights = Gather(place, shard_ref, g_ref, *sems[:6])
+    conds = Gather(place, cond_ref, conds_ref, *sems[6:12])
+    mods = Gather(place, mod_local, mods_ref, *sems[12:])
+    parts = weights.parts()
+    conds.run("begin")
+    weights.run("begin")
+    for part in parts[1:]:
+        conds.run(part)
+    devices = 8 * planes
+    rows = cond_ref.shape[0]
+    every = conds_ref[...].reshape(devices * rows, cond_ref.shape[1])
+    columns = (dg(every, ada_ref[...], NN) + ada_bias_ref[...]).reshape(devices, rows, -1)
+    width = columns.shape[2]
+    mod_local[...] = jnp.zeros_like(mod_local)
+    for i in range(devices):
+        mod_local[i * items : (i + 1) * items, :width] = columns[i, :items].astype(BF)
+    mods.run("begin")
+    for part in parts[1:]:
+        weights.run(part)
+        mods.run(part)
+
+
+def prologue_call(shard, cond, ada, ada_bias, planes, items):
+    devices = 8 * planes
+    rows, d = cond.shape
+    lanes = up_to(ada.shape[1], 128)
+    slots = devices * items
+    spread = (4, planes, 2)
+    return pl.pallas_call(
+        functools.partial(prologue_kernel, planes=planes, items=items),
+        out_shape=(
+            shape(spread + shard.shape, BF),
+            shape(spread + (rows, d), BF),
+            shape(spread + (slots, lanes), BF),
+        ),
+        in_specs=[ANY_SPEC, VMEM_SPEC, VMEM_SPEC, VMEM_SPEC],
+        out_specs=(ANY_SPEC, VMEM_SPEC, ANY_SPEC),
+        scratch_shapes=[pltpu.VMEM((slots, lanes), BF)] + Gather.scratch(planes) * 3,
+        compiler_params=params(collective_id=1),
+        name="weights_and_modulation",
+    )(shard, cond, ada, ada_bias)
+
+
+def qkv_kernel(tokens_ref, shift_ref, scale_ref, g_ref, bias_ref, n1_ref, qkv_ref, w_ref, wp_ref):
+    d = tokens_ref.shape[1]
+    devices = g_ref.shape[0]
+    r = d // devices
+
+    @pl.when(pl.program_id(0) == 0)
+    def _():
+        for i in range(devices):
+            rows = slice(i * r, (i + 1) * r)
+            for b in range(3):
+                w_ref[rows, b * d : (b + 1) * d] = g_ref[i, b * r : (b + 1) * r, :]
+            wp_ref[rows, :] = g_ref[i, 3 * r : 4 * r, :]
+
     normed, _ = ln_parts(tokens_ref[...])
     low = (normed * (1.0 + scale_ref[0]) + shift_ref[0]).astype(BF)
     n1_ref[...] = low
     qkv_ref[...] = (dg(low, w_ref[...], NN) + bias_ref[...]).astype(BF)
 
 
-def qkv_call(tokens, shift, scale, w, bias, blk):
+def qkv_call(tokens, shift, scale, g, bias, blk):
     t, d = tokens.shape
-    n = w.shape[1]
+    n = 3 * d
     return pl.pallas_call(
         qkv_kernel,
         grid=(t // blk,),
-        out_shape=(shape((t, d), BF), shape((t, n), BF)),
-        in_specs=[rows_of(blk, d), row_vec(d), row_vec(d), whole(d, n), whole(1, n)],
-        out_specs=(rows_of(blk, d), rows_of(blk, n)),
+        out_shape=(shape((t, d), BF), shape((t, n), BF), shape((d, n), BF), shape((d, d), BF)),
+        in_specs=[rows_of(blk, d), row_vec(d), row_vec(d), whole(*g.shape), whole(1, n)],
+        out_specs=(rows_of(blk, d), rows_of(blk, n), whole(d, n), whole(d, d)),
         compiler_params=params(),
         name="qkv_forward",
-    )(tokens, shift, scale, w, bias)
+    )(tokens, shift, scale, g, bias)
 
 
 def head_window(h, hd, width):
@@ -98,7 +505,32 @@
     return a, (lane >= h * hd) & (lane < h * hd + hd)
 
 
-def attn_fwd_kernel(off_ref, gate_ref, qkv_ref, att_ref, gated_ref, lse_ref, lse_sc, *, heads, blk):
+def attn_fwd_kernel(
+    off_ref,
+    gate_ref,
+    qkv_ref,
+    up_ref,
+    down_ref,
+    att_ref,
+    gated_ref,
+    lse_ref,
+    g_up_ref,
+    g_down_ref,
+    lse_sc,
+    *sems,
+    heads,
+    blk,
+    planes,
+):
+    place = Place(planes)
+    place.barrier()
+    gathers = [Gather(place, up_ref, g_up_ref, *sems[:6]), Gather(place, down_ref, g_down_ref, *sems[6:])]
+    parts = gathers[0].parts()
+    for g in gathers:
+        g.run("begin")
+    groups = spread_out(
+        [functools.partial(g.run, part) for part in parts[1:-1] for g in gathers], heads
+    )
     t, d = att_ref.shape
     hd = d // heads
     nb = t // blk
@@ -129,29 +561,56 @@
             att_ref[rows, cols] = jnp.where(mask, o, att_ref[rows, cols])
             gated_ref[rows, cols] = jnp.where(mask, og, gated_ref[rows, cols])
             lse_sc[rows, :] = jnp.where(lane128 == h, m + jnp.log2(total), lse_sc[rows, :])
+        run_at(h, groups)
         return carry
 
     lax.fori_loop(0, heads, body, 0)
     lse_ref[...] = lse_sc[...].T[:heads, :]
-
-
-def attn_fwd(off, gate_rows, qkv, heads, blk):
+    for g in gathers:
+        g.run("end")
+
+
+def attn_fwd(off, gate_rows, qkv, up, down, heads, blk, planes):
     t = qkv.shape[0]
     d = qkv.shape[1] // 3
+    gathered = shape((4, planes, 2) + up.shape, BF)
     return pl.pallas_call(
-        functools.partial(attn_fwd_kernel, heads=heads, blk=blk),
-        out_shape=(shape((t, d)), shape((t, d), BF), shape((heads, t))),
-        in_specs=[SMEM_SPEC, VMEM_SPEC, VMEM_SPEC],
-        out_specs=(VMEM_SPEC,) * 3,
-        scratch_shapes=[pltpu.VMEM((t, 128), F32)],
-        compiler_params=params(),
+        functools.partial(attn_fwd_kernel, heads=heads, blk=blk, planes=planes),
+        out_shape=(shape((t, d)), shape((t, d), BF), shape((heads, t)), gathered, gathered),
+        in_specs=[SMEM_SPEC, VMEM_SPEC, VMEM_SPEC, ANY_SPEC, ANY_SPEC],
+        out_specs=(VMEM_SPEC,) * 3 + (ANY_SPEC,) * 2,
+        scratch_shapes=[pltpu.VMEM((t, 128), F32)] + Gather.scratch(planes) * 2,
+        compiler_params=params(collective_id=2),
         name="attention_forward",
-    )(off, gate_rows, qkv)
+    )(off, gate_rows, qkv, up, down)
 
 
 def attn_bwd_kernel(
-    off_ref, qkv_ref, do_ref, lse_ref, delta_ref, dqkv_ref, kt_sc, dqt_sc, *, heads, blk
+    off_ref,
+    qkv_ref,
+    do_ref,
+    lse_ref,
+    delta_ref,
+    up_ref,
+    down_ref,
+    dqkv_ref,
+    g_up_ref,
+    g_down_ref,
+    kt_sc,
+    dqt_sc,
+    *rest,
+    heads,
+    blk,
+    planes,
 ):
+    place = Place(planes)
+    place.barrier(True)
+    half = len(rest) // 2
+    steps = scatter_steps(
+        [Scatter(place, up_ref, g_up_ref, *rest[:half]), Scatter(place, down_ref, g_down_ref, *rest[half:])]
+    )
+    steps[0]()
+    groups = spread_out(steps[1:-1], heads)
     t, d = do_ref.shape
     hd = d // heads
     nb = t // blk
@@ -199,22 +658,26 @@
         dqkv_ref[:, key_cols] = jnp.where(mask, dk, dqkv_ref[:, key_cols])
         dqkv_ref[:, value_cols] = jnp.where(mask, dv_sum.astype(BF), dqkv_ref[:, value_cols])
         dqkv_ref[:, cols] = jnp.where(mask, dqt_sc[...].T, dqkv_ref[:, cols])
+        run_at(h, groups)
         return carry
 
     lax.fori_loop(0, heads, body, 0)
-
-
-def attn_bwd(off, qkv, do, lse, delta, heads, blk):
+    steps[-1]()
+
+
+def attn_bwd(off, qkv, do, lse, delta, up, down, heads, blk, planes):
     t, d = do.shape
+    rows, cols = up.shape[3:]
     return pl.pallas_call(
-        functools.partial(attn_bwd_kernel, heads=heads, blk=blk),
-        out_shape=shape((t, 3 * d), BF),
-        in_specs=[SMEM_SPEC] + [VMEM_SPEC] * 4,
-        out_specs=VMEM_SPEC,
-        scratch_shapes=[pltpu.VMEM((d, t), BF), pltpu.VMEM((WINDOW, t), BF)],
-        compiler_params=params(),
+        functools.partial(attn_bwd_kernel, heads=heads, blk=blk, planes=planes),
+        out_shape=(shape((t, 3 * d), BF), shape((rows, cols)), shape((rows, cols))),
+        in_specs=[SMEM_SPEC] + [VMEM_SPEC] * 4 + [ANY_SPEC] * 2,
+        out_specs=(VMEM_SPEC,) * 3,
+        scratch_shapes=[pltpu.VMEM((d, t), BF), pltpu.VMEM((WINDOW, t), BF)]
+        + Scatter.scratch(planes, rows, cols) * 2,
+        compiler_params=params(collective_id=3),
         name="attention_backward",
-    )(off, qkv, do, lse, delta)
+    )(off, qkv, do, lse, delta, up, down)
 
 
 def middle_kernel(
@@ -263,62 +726,97 @@
 
 
 def mlp_kernel(
-    n2_ref, gm_ref, w1_ref, w2_ref, b1_ref, cs_ref, mlp_ref, gn2_ref, g1_ref, g2_ref, gb1_ref, gch_ref, sc_s, gp_s, *, blk
+    n2_ref,
+    gm_ref,
+    g1_ref,
+    g2_ref,
+    b1_ref,
+    cs_ref,
+    mlp_ref,
+    gn2_ref,
+    p1_ref,
+    p2_ref,
+    gb1_ref,
+    gch_ref,
+    w1_s,
+    w2_s,
+    sc_s,
+    gp_s,
+    *,
+    blk,
 ):
-    nb = n2_ref.shape[0] // blk
+    t, d = n2_ref.shape
+    nb = t // blk
+    hidden = w1_s.shape[0]
+    quarter = hidden // 8
+    piece = d // 4
 
     @pl.when(pl.program_id(0) == 0)
     def _():
         mlp_ref[...] = jnp.zeros_like(mlp_ref)
         gn2_ref[...] = jnp.zeros_like(gn2_ref)
 
-    w1 = w1_ref[...]
-    w2 = w2_ref[...]
+    def places():
+        for c in range(2):
+            for k in range(4):
+                yield c, slice((4 * c + k) * quarter, (4 * c + k + 1) * quarter), k
+
+    for c, rows, k in places():
+        cols = slice(k * piece, (k + 1) * piece)
+        for w, g in ((w1_s, g1_ref), (w2_s, g2_ref)):
+            w[rows, :] = jnp.concatenate([g[n, 0, c, :quarter, cols] for n in range(4)], axis=1)
+    w1 = w1_s[...]
+    w2 = w2_s[...]
     grad_bias = None
     for i in range(nb):
         rows = slice(i * blk, (i + 1) * blk)
-        pre = dg(n2_ref[rows, :], w1, NT) + b1_ref[...]
+        pre = dg(n2_ref[rows, :], w1, NT) + b1_ref[0]
         grad_scaled = dg(gm_ref[rows, :], w2, NT)
         act, slope = gelu_parts(pre)
-        gate = cs_ref[i]
+        gate = cs_ref[0, i : i + 1]
         scaled = (act * gate).astype(BF)
         grad_pre = (grad_scaled * gate * slope).astype(BF)
-        gch_ref[i] = col_sum(grad_scaled * act)
+        gch_ref[0, i : i + 1] = col_sum(grad_scaled * act)
         part = col_sum(grad_pre.astype(F32))
         grad_bias = part if grad_bias is None else grad_bias + part
         sc_s[rows, :] = scaled
         gp_s[rows, :] = grad_pre
         mlp_ref[rows, :] += dg(scaled, w2, NN)
         gn2_ref[rows, :] += dg(grad_pre, w1, NN)
-    gb1_ref[...] = grad_bias
-    g1_ref[...] = dg(gp_s[...], n2_ref[...], TN).astype(BF)
-    g2_ref[...] = dg(sc_s[...], gm_ref[...], TN).astype(BF)
-
-
-def mlp_call(n2, gm, w1, w2, b1, gates, hb, blk):
+    gb1_ref[0] = grad_bias
+    for left, right, out in ((gp_s, n2_ref, p1_ref), (sc_s, gm_ref, p2_ref)):
+        grad = dg(left[...], right[...], TN).astype(BF)
+        for c, rows, k in places():
+            for n in range(4):
+                out[n, 0, c, :quarter, k * piece : (k + 1) * piece] = grad[rows, n * piece : (n + 1) * piece]
+
+
+def mlp_call(n2, gm, g1, g2, b1, gates, blk):
     t, d = n2.shape
-    ff = w1.shape[0]
-    nb = t // blk
-    w_spec = pl.BlockSpec((hb, d), lambda j: (j, 0))
-    b_spec = pl.BlockSpec((1, hb), lambda j: (0, j))
-    c_spec = pl.BlockSpec((nb, 1, hb), lambda j: (0, 0, j))
-    return pl.pallas_call(
+    planes, rows = g1.shape[1], g1.shape[3]
+    nb, ff = gates.shape
+    hb = ff // planes
+    g_spec = pl.BlockSpec((4, 1, 2, rows, d), lambda j: (0, j, 0, 0, 0))
+    b_spec = pl.BlockSpec((1, 1, hb), lambda j: (j, 0, 0))
+    c_spec = pl.BlockSpec((1, nb, hb), lambda j: (j, 0, 0))
+    mlp, gn2, p1, p2, gb1, gch = pl.pallas_call(
         functools.partial(mlp_kernel, blk=blk),
-        grid=(ff // hb,),
+        grid=(planes,),
         out_shape=(
             shape((t, d)),
             shape((t, d)),
-            shape((ff, d), BF),
-            shape((ff, d), BF),
-            shape((1, ff)),
-            shape((nb, 1, ff)),
+            shape(g1.shape, BF),
+            shape(g1.shape, BF),
+            shape((planes, 1, hb)),
+            shape((planes, nb, hb)),
         ),
-        in_specs=[whole(t, d), whole(t, d), w_spec, w_spec, b_spec, c_spec],
-        out_specs=(whole(t, d), whole(t, d), w_spec, w_spec, b_spec, c_spec),
-        scratch_shapes=[pltpu.VMEM((t, hb), BF), pltpu.VMEM((t, hb), BF)],
+        in_specs=[whole(t, d), whole(t, d), g_spec, g_spec, b_spec, c_spec],
+        out_specs=(whole(t, d), whole(t, d), g_spec, g_spec, b_spec, c_spec),
+        scratch_shapes=[pltpu.VMEM((hb, d), BF)] * 2 + [pltpu.VMEM((t, hb), BF)] * 2,
         compiler_params=params(),
         name="feed_forward",
-    )(n2, gm, w1, w2, b1, gates)
+    )(n2, gm, g1, g2, b1.reshape(planes, 1, hb), gates.reshape(nb, planes, hb).transpose(1, 0, 2))
+    return mlp, gn2, p1, p2, gb1.reshape(ff), gch.transpose(1, 0, 2).reshape(nb, ff)
 
 
 def middle_back_kernel(
@@ -440,32 +938,43 @@
     )(mlp, gn2, after, attn, cot, gm, gated, att, tg, keep, w, b2, router, gate1, shift2, scale2, gate2, head_rows)
 
 
-def qkv_weight_kernel(n1_ref, dqkv_ref, gw_ref, bias_ref, n1t):
+def qkv_weight_kernel(n1_ref, q_ref, k_ref, v_ref, gp_ref, out_ref, bias_ref, n1t):
     @pl.when(pl.program_id(0) == 0)
     def _():
         n1t[...] = n1_ref[...].T
 
-    dqkv = dqkv_ref[...]
-    gw_ref[...] = dg(n1t[...], dqkv, NN).astype(gw_ref.dtype)
-    bias_ref[...] = col_sum(dqkv.astype(F32))
-
-
-def qkv_weight_call(n1, dqkv, width, dtype):
+    width = q_ref.shape[1]
+    devices = out_ref.shape[1]
+    r = n1_ref.shape[1] // devices
+    dqkv = jnp.concatenate([q_ref[...], k_ref[...], v_ref[...]], axis=1)
+    grad = dg(n1t[...], dqkv, NN).astype(BF)
+    bias_ref[0] = col_sum(dqkv.astype(F32))
+    for i in range(devices):
+        rows = slice(i * r, (i + 1) * r)
+        for b in range(3):
+            out_ref[0, i, b * r : (b + 1) * r, :] = grad[rows, b * width : (b + 1) * width]
+        out_ref[0, i, 3 * r : 4 * r, :] = gp_ref[rows, :].astype(BF)
+
+
+def qkv_weight_call(n1, dqkv, g_proj, devices, cuts):
     t, d = n1.shape
-    n = dqkv.shape[1]
-    return pl.pallas_call(
+    width = d // cuts
+    rows = up_to(4 * d // devices, 16)
+    third = [pl.BlockSpec((t, width), lambda j, b=b: (0, b * cuts + j)) for b in range(3)]
+    parts, bias = pl.pallas_call(
         qkv_weight_kernel,
-        grid=(n // width,),
-        out_shape=(shape((d, n), dtype), shape((1, n))),
-        in_specs=[whole(t, d), pl.BlockSpec((t, width), lambda j: (0, j))],
+        grid=(cuts,),
+        out_shape=(shape((cuts, devices, rows, width), BF), shape((cuts, 1, 3 * width))),
+        in_specs=[whole(t, d)] + third + [pl.BlockSpec((d, width), lambda j: (0, j))],
         out_specs=(
-            pl.BlockSpec((d, width), lambda j: (0, j)),
-            pl.BlockSpec((1, width), lambda j: (0, j)),
+            pl.BlockSpec((1, devices, rows, width), lambda j: (j, 0, 0, 0)),
+            pl.BlockSpec((1, 1, 3 * width), lambda j: (j, 0, 0)),
         ),
         scratch_shapes=[pltpu.VMEM((d, t), BF)],
         compiler_params=params(),
         name="qkv_weight_gradient",
-    )(n1, dqkv)
+    )(n1, dqkv, dqkv, dqkv, g_proj)
+    return parts, bias.reshape(cuts, 3, width).transpose(1, 0, 2).reshape(3, d)
 
 
 def qkv_back_kernel(dqkv_ref, w_ref, tokens_ref, ga_ref, scale_ref, out_ref, mod_ref):
@@ -490,7 +999,58 @@
     )(dqkv, w, tokens, ga, scale)
 
 
+def final_kernel(part_ref, sums_ref, mods_ref, out_ref, all_sums_ref, all_mods_ref, *rest, planes, cuts):
+    place = Place(planes)
+    place.barrier(True)
+    width = out_ref.shape[1] // cuts
+    sums = Gather(place, sums_ref, all_sums_ref, *rest[:6])
+    mods = Gather(place, mods_ref, all_mods_ref, *rest[6:12])
+    rest = rest[12:]
+    each = len(rest) // cuts
+    scatters = [
+        Scatter(
+            place,
+            part_ref.at[m],
+            out_ref.at[:, pl.ds(m * width, width)],
+            *rest[each * m : each * (m + 1)],
+        )
+        for m in range(cuts)
+    ]
+    steps = scatter_steps(scatters)
+    parts = sums.parts()
+    steps[0]()
+    sums.run("begin")
+    mods.run("begin")
+    small = [functools.partial(g.run, part) for part in parts[1:-1] for g in (sums, mods)]
+    for step, group in zip(steps[1:-1], spread_out(small, len(steps) - 2)):
+        step()
+        for part in group:
+            part()
+    steps[-1]()
+    sums.run("end")
+    mods.run("end")
+
+
+def final_call(parts, sums, mods, planes):
+    cuts, _, rows, width = parts.shape
+    spread = (4, planes, 2)
+    return pl.pallas_call(
+        functools.partial(final_kernel, planes=planes, cuts=cuts),
+        out_shape=(
+            shape((rows, cuts * width)),
+            shape(spread + sums.shape),
+            shape(spread + mods.shape, BF),
+        ),
+        in_specs=[ANY_SPEC] * 3,
+        out_specs=(VMEM_SPEC, ANY_SPEC, ANY_SPEC),
+        scratch_shapes=Gather.scratch(planes) * 2 + Scatter.scratch(planes, rows, width) * cuts,
+        compiler_params=params(collective_id=4),
+        name="attention_weight_sums",
+    )(parts.reshape((cuts,) + spread + (rows, width)), sums, mods)
+
+
 def on_device(
+    planes,
     tokens,
     conditioning,
     row_items,
@@ -515,7 +1075,6 @@
     token_router,
     cotangent,
 ):
-    axes = ("narrow", "wide")
     t, d = tokens.shape
     slots = conditioning.shape[0]
     heads = head_mask.shape[1]
@@ -535,12 +1094,30 @@
         first = (jnp.arange(slots) == 0).reshape((slots,) + (1,) * (blocks.ndim - 1))
         return jnp.where(single, jnp.where(first, total, 0.0), blocks)
 
+    devices = 8 * planes
+    me = lax.axis_index("narrow") * (2 * planes) + lax.axis_index("wide")
+
+    def pack_rows(*blocks):
+        return pad_rows(jnp.concatenate(blocks, axis=0))
+
+    def pack_piece(weight):
+        rows, cols = weight.shape
+        return pad_rows(weight.reshape(4, rows // 4, cols).transpose(1, 0, 2).reshape(rows // 4, d))
+
+    def unpack_piece(piece, rows):
+        cols = d // 4
+        return piece[: rows // 4].reshape(rows // 4, 4, cols).transpose(1, 0, 2).reshape(rows, cols)
+
     silu_cond = jax.nn.silu(conditioning.astype(F32)).astype(BF)
-    every_cond = lax.all_gather(silu_cond, axes, axis=0, tiled=True)
-    mod_columns = jnp.dot(every_cond, ada_weight, preferred_element_type=F32) + ada_bias.astype(F32)
-    modulation = lax.all_to_all(
-        mod_columns.astype(BF), axes, split_axis=0, concat_axis=1, tiled=True
-    )
+    shard = pack_rows(qkv_weight[:, :d], qkv_weight[:, d : 2 * d], qkv_weight[:, 2 * d :], proj_weight)
+    g_attn, conds, mod_columns = prologue_call(
+        shard, pad_rows(silu_cond), ada_weight, ada_bias.astype(F32)[None], planes, slots
+    )
+    every_cond = conds.reshape((devices,) + conds.shape[3:])[:, :slots].reshape(devices * slots, d)
+    mod_width = ada_bias.shape[0]
+    mod_columns = mod_columns.reshape((devices,) + mod_columns.shape[3:])
+    mod_columns = lax.dynamic_slice_in_dim(mod_columns, me * slots, slots, axis=1)
+    modulation = mod_columns[:, :, :mod_width].transpose(1, 0, 2).reshape(slots, devices * mod_width)
     mod_rows = per_block(modulation.astype(F32)).reshape(slots, 6, 1, d)
     shift1, scale1, gate1, shift2, scale2, gate2 = [mod_rows[:, k] for k in range(6)]
     cond_float = silu_cond.astype(F32)
@@ -555,19 +1132,21 @@
     head_gate, head_slope = router(head_router, head_router_bias, head_mask)
     chan_gate, chan_slope = router(chan_router, chan_router_bias, chan_mask)
     head_rows = jnp.repeat(per_block(head_gate), hd, axis=1)[:, None, :]
-    chan_rows = jnp.repeat(per_block(chan_gate), unit, axis=1)[:, None, :]
+    chan_rows = jnp.repeat(per_block(chan_gate), unit, axis=1)
     keep = (1.0 - skip_mask.astype(F32))[:, None]
 
-    full_qkv = lax.all_gather(qkv_weight, axes, axis=0, tiled=True)
-    full_proj = lax.all_gather(proj_weight, axes, axis=0, tiled=True)
-    fc1_rows = lax.all_gather(fc1_weight, "narrow", axis=1, tiled=True)
-    fc2_rows = lax.all_gather(fc2_weight, "narrow", axis=1, tiled=True)
-    full_fc1 = lax.all_gather(fc1_rows, "wide", axis=0, tiled=True)
-    full_fc2 = lax.all_gather(fc2_rows, "wide", axis=0, tiled=True)
-
     qkv_bias = jnp.concatenate([query_bias, jnp.zeros_like(query_bias), value_bias])
-    n1, qkv = qkv_call(tokens, shift1, scale1, full_qkv, qkv_bias.astype(F32)[None], blk)
-    att, gated, lse = attn_fwd(off, head_rows, qkv, heads, blk)
+    n1, qkv, full_qkv, full_proj = qkv_call(
+        tokens,
+        shift1,
+        scale1,
+        g_attn.reshape((devices,) + shard.shape),
+        qkv_bias.astype(F32)[None],
+        blk,
+    )
+    att, gated, lse, g_up, g_down = attn_fwd(
+        off, head_rows, qkv, pack_piece(fc1_weight), pack_piece(fc2_weight), heads, blk, planes
+    )
     router_row = token_router.astype(F32)[None]
     attn, after, n2, gm, tg = middle_call(
         gated,
@@ -583,8 +1162,8 @@
         gate2,
         blk,
     )
-    mlp, gn2, g_fc1, g_fc2, gb1, gch = mlp_call(
-        n2, gm, full_fc1, full_fc2, fc1_bias.astype(F32)[None], chan_rows, hidden // 6, blk
+    mlp, gn2, p_up, p_down, gb1, gch = mlp_call(
+        n2, gm, g_up, g_down, fc1_bias.astype(F32), chan_rows, blk
     )
     output, ga, do, delta, g_proj, mods, sums = middle_back_call(
         mlp,
@@ -609,47 +1188,36 @@
         blk,
     )
     mods = mods.reshape(slots, 8, d)
-    fc_sum = lax.psum_scatter(
-        jnp.stack([g_fc1, g_fc2], axis=1), "wide", scatter_dimension=0, tiled=True
-    )
-    fc_grads = lax.psum_scatter(fc_sum, "narrow", scatter_dimension=2, tiled=True).astype(F32)
-    dqkv = attn_bwd(off, qkv, do, lse, delta, heads, blk)
-    g_qkv, qkv_sums = qkv_weight_call(n1, dqkv, 3 * d // 9, BF)
-    attn_grads = lax.psum_scatter(
-        jnp.concatenate([g_qkv, g_proj.astype(BF)], axis=1), axes, scatter_dimension=0, tiled=True
-    ).astype(F32)
+    dqkv, g_up, g_down = attn_bwd(off, qkv, do, lse, delta, p_up, p_down, heads, blk, planes)
+    parts, qkv_sums = qkv_weight_call(n1, dqkv, g_proj, devices, 3)
     grad_tokens, mods1 = qkv_back_call(dqkv, full_qkv, tokens, ga, scale1, blk)
     block_mods = jnp.concatenate(
         [mods1[:, 0], mods1[:, 1], mods[:, 0], mods[:, 1], mods[:, 2], mods[:, 3]], axis=1
     )
     grad_slot_mod = per_slot(block_mods).astype(BF)
-    grad_mod_columns = lax.all_to_all(
-        grad_slot_mod, axes, split_axis=1, concat_axis=0, tiled=True
-    )
+    g_head = per_slot(jnp.sum(mods[:, 4].reshape(slots, heads, hd), axis=2)) * head_slope
+    g_chan = per_slot(jnp.sum(gch.reshape(slots, groups, unit), axis=2)) * chan_slope
+    logits = jnp.concatenate([g_head, g_chan], axis=1)
+    vector = jnp.concatenate(
+        [qkv_sums[0], qkv_sums[2], sums[1], gb1, sums[2], sums[0], logits.reshape(-1)]
+    )
+    length = vector.shape[0]
+    vector = jnp.pad(vector, (0, up_to(length, 1024) - length)).reshape(-1, 128)
+    g_attn, all_sums, all_mods = final_call(
+        parts, vector, pad_rows(grad_slot_mod.reshape(-1, 128)), planes
+    )
+    g_attn = g_attn[: 4 * (d // devices)].reshape(4, d // devices, d)
+    all_mods = all_mods.reshape(devices, -1)[:, : slots * 6 * d].reshape(devices * slots, 6 * d)
+    grad_mod_columns = lax.dynamic_slice_in_dim(all_mods, me * mod_width, mod_width, axis=1)
     grad_ada_weight = dg(every_cond, grad_mod_columns, TN)
     grad_ada_bias = jnp.sum(grad_mod_columns.astype(F32), axis=0)
-    g_head = per_slot(jnp.sum(mods[:, 4].reshape(slots, heads, hd), axis=2)) * head_slope
-    g_chan = per_slot(jnp.sum(gch.reshape(slots, groups, unit), axis=2)) * chan_slope
-    logits = lax.all_gather(
-        jnp.concatenate([g_head, g_chan], axis=1), axes, axis=0, tiled=True
-    )
+    all_sums = all_sums.reshape(devices, -1)
+    logits = all_sums[:, length - logits.size : length].reshape(devices * slots, heads + groups)
     router_grads = lax.dot_general(
         every_cond.astype(F32), logits, TN, precision=HIGHEST, preferred_element_type=F32
     )
     logit_sums = jnp.sum(logits, axis=0)
-    small = lax.psum(
-        jnp.concatenate(
-            [
-                qkv_sums[0, :d],
-                qkv_sums[0, 2 * d :],
-                sums[1],
-                gb1[0],
-                sums[2],
-                sums[0],
-            ]
-        ),
-        axes,
-    )
+    small = jnp.sum(all_sums[:, : length - slots * (heads + groups)], axis=0)
     ends = [d, 2 * d, 3 * d, 3 * d + hidden, 4 * d + hidden]
     g_query, g_value, g_proj_bias, g_b1, g_b2, g_router = jnp.split(small, ends)
     return (
@@ -657,14 +1225,14 @@
         grad_tokens,
         grad_ada_weight,
         grad_ada_bias,
-        attn_grads[:, : 3 * d],
+        g_attn[:3].transpose(1, 0, 2).reshape(d // devices, 3 * d),
         g_query,
         g_value,
-        attn_grads[:, 3 * d :],
+        g_attn[3],
         g_proj_bias,
-        fc_grads[:, 0],
+        unpack_piece(g_up, fc1_weight.shape[0]),
         g_b1,
-        fc_grads[:, 1],
+        unpack_piece(g_down, fc2_weight.shape[0]),
         g_b2,
         router_grads[:, :heads],
         logit_sums[:heads],
@@ -675,8 +1243,9 @@
 
 
 def solution(mesh):
+    planes = mesh.shape["wide"] // 2
     return jax.shard_map(
-        on_device,
+        functools.partial(on_device, planes),
         mesh=mesh,
         in_specs=(
             P(("narrow", "wide"), None),

time: 1000 us -> 624 us (0.62)
  blocking collectives: 310 us -> 0 us
  Pallas kernels: 278 us -> 562 us
  waiting for transfers between devices: 269 us -> 0 us
  other arithmetic: 34.3 us -> 9.81 us
  starting transfers between devices: 19.1 us -> 0 us
  local copies, waits for them, and re-layouts: 53.3 us -> 37.9 us
  between operations: 16.7 us -> 2.47 us
    pallas_call x4 -> x6, Pallas kernels: 202 us -> 484 us  [the longest x1 122 us: attn_bwd(): pl.pallas_call(functools.partial(attn_bwd_kernel, heads=heads, blk=blk, p...]
    all_gather x6 -> x0, waiting for transfers between devices: 259 us -> none  [the longest x1 100 us: on_device(): full_fc2 = lax.all_gather(fc2_rows, 'wide', axis=0, tiled=True)]
    unnamed x1 -> x0, blocking collectives: 191 us -> none
    all_gather x2 -> x0, blocking collectives: 79.1 us -> none  [the longest x1 41.8 us: on_device(): every_cond = lax.all_gather(silu_cond, axes, axis=0, tiled=True)]
    psum x1 -> x0, blocking collectives: 40.3 us -> none  [on_device(): lax.psum(jnp.concatenate([qkv_sums[0, :d], qkv_sums[0, 2 * d:], sums[1],...]
    another operation x1 -> x0, other arithmetic: 17.8 us -> none  [on_device(): jnp.stack([g_fc1, g_fc2], axis=1)]
    unnamed x5 -> x0, starting transfers between devices: 13.5 us -> none
    unnamed x65 -> x44, local copies, waits for them, and re-layouts: 22.8 us -> 9.83 us
  transfers between devices with their start and end apart: 14 -> 0, of which waited for: 8 -> 0; matrix products, arithmetic and copies ran while one was open for 26% -> 0% of each run, Pallas kernels for 20% -> 0%
where the time goes in v2:
time: 624 us; the launch traced here: 616 us
  Pallas kernels  562 us (90%)
  local copies, waits for them, and re-layouts  37.9 us (6%)
  other arithmetic  9.81 us (2%)
    pallas_call x1, Pallas kernels, attn_bwd(): pl.pallas_call(functools.partial(attn_bwd_kernel, heads=heads, blk=blk, p...  122 us
    pallas_call x1, Pallas kernels, attn_fwd(): pl.pallas_call(functools.partial(attn_fwd_kernel, heads=heads, blk=blk, p...  101 us
    pallas_call x1, Pallas kernels, mlp_call(): pl.pallas_call(functools.partial(mlp_kernel, blk=blk), grid=(planes,), ou...  92.3 us
    pallas_call x1, Pallas kernels, prologue_call(): pl.pallas_call(functools.partial(prologue_kernel, planes=planes, items=it...  80 us
    pallas_call x1, Pallas kernels, final_call(): pl.pallas_call(functools.partial(final_kernel, planes=planes, cuts=cuts),...  72.6 us
    pallas_call x1, Pallas kernels, middle_back_call(): pl.pallas_call(functools.partial(middle_back_kernel, heads=heads), grid=(...  26.8 us
    pallas_call x1, Pallas kernels, qkv_call(): pl.pallas_call(qkv_kernel, grid=(t // blk,), out_shape=(shape((t, d), BF)...  19.1 us
    pallas_call x1, Pallas kernels, qkv_back_call(): pl.pallas_call(qkv_back_kernel, grid=(t // blk,), out_shape=(shape((t, d)...  18.2 us

profile of v2, /device:TPU:0, one launch (start us, length us, event | category | flops | bytes accessed | tf_op | source)
XLA Modules:
  0.0 616.3 jit_solution(5411297827018732708)
XLA Ops:
  2.9 1.2 broadcast_in_dim.170
  4.8 1.3 reshape.238.router_ref
  8.1 1.3 reshape.237.bias_ref
  9.4 1.3 reshape.241.b2_ref
  13.2 1.3 reshape.240.b1_ref
  17.8 1.7 pad_maximum_fusion.shard_ref
  19.5 1.2 copy.71
  25.5 80.0 %weights_and_modulation.1 = (bf16[4,4,2,144,1152]{4,3,2,1,0:T(8,128)(2,1)}, bf16[4,4,2,16,1152]{4,3,2,1,0:T(8,128)(2,1)}, bf16[4,4,2,128,256]{4,3,2,1,0:T(8,128)(2,1)}) custom-call(bf16[144,1152]{1,0:T(8,128)(2,1)} %pad_maximum_fusion.shard_ref, bf16[16,1152]{1,0:T(8,128)(2,1)} %pad.12.cond_ref, bf16[1152,216]{1,0:T(8,128)(2,1)} %copy.69.ada_ref, ...), custom_call_target="tpu_custom_call" | custom-call | tf_op jit(solution)/shard_map/weights_and_modulation/pallas_call | solution.py:454
  108.6 19.1 %qkv_forward.1 = (bf16[1024,1152]{1,0:T(8,128)(2,1)}, bf16[1024,3456]{1,0:T(8,128)(2,1)}, bf16[1152,3456]{1,0:T(8,128)(2,1)}, bf16[1152,1152]{1,0:T(8,128)(2,1)}) custom-call(f32[1024,1152]{1,0:T(8,128)} %tokens_ref.5, f32[4,1,1152]{2,1,0:T(1,128)} %get-tuple-element.155.shift_ref, f32[4,1,1152]{2,1,0:T(1,128)} %get-tuple-element.154.scale_ref, ...), custom_call_target="tpu_custom_call" | custom-call | tf_op jit(solution)/shard_map/qkv_forward/pallas_call | solution.py:491
  127.8 101.3 %attention_forward.1 = (f32[1024,1152]{1,0:T(8,128)}, bf16[1024,1152]{1,0:T(8,128)(2,1)}, f32[16,1024]{1,0:T(8,128)}, bf16[4,4,2,144,1152]{4,3,2,1,0:T(8,128)(2,1)}, bf16[4,4,2,144,1152]{4,3,2,1,0:T(8,128)(2,1)}) custom-call(f32[1]{0:T(128)} %bitcast.1.off_ref, f32[4,1,1152]{2,1,0:T(1,128)} %broadcast_in_dim_reshape.3.gate_ref.head_ref, ...), custom_call_target="tpu_custom_call" | custom-call | tf_op jit(solution)/shard_map/attention_forward/pallas_call | solution.py:577
  229.1 13.8 %middle_forward.1 = (f32[1024,1152]{1,0:T(8,128)}, f32[1024,1152]{1,0:T(8,128)}, bf16[1024,1152]{1,0:T(8,128)(2,1)}, bf16[1024,1152]{1,0:T(8,128)(2,1)}, f32[1024,1]{1,0:T(8,128)}) custom-call(bf16[1024,1152]{1,0:T(8,128)(2,1)} %get-tuple-element.61.gated_ref, bf16[1152,1152]{1,0:T(8,128)(2,1)} %get-tuple-element.62.w_ref, f32[1,1152]{1,0:T(1,128)} %reshape.237.bias_ref, ...), custom_call_target="tpu_custom_call" | custom-call | tf_op jit(solution)/shard_map/middle_forward/pallas_call | solution.py:717
  242.8 92.3 %feed_forward.1 = (f32[1024,1152]{1,0:T(8,128)}, f32[1024,1152]{1,0:T(8,128)}, bf16[4,4,2,144,1152]{4,3,2,1,0:T(8,128)(2,1)}, bf16[4,4,2,144,1152]{4,3,2,1,0:T(8...) custom-call(bf16[1024,1152]{1,0:T(8,128)(2,1)} %get-tuple-element.63.n2_ref, ...), custom_call_target="tpu_custom_call" | custom-call | tf_op jit(solution)/shard_map/feed_forward/pallas_call | solution.py:802
  335.1 26.8 %middle_backward.1 = (f32[1024,1152]{1,0:T(8,128)}, f32[1024,1152]{1,0:T(8,128)}, bf16[1024,1152]{1,0:T(8,128)(2,1)}, f32[16,1024]{1,0:T(8,128)}, f32[1152,1152]...) custom-call(f32[1024,1152]{1,0:T(8,128)} %get-tuple-element.67.mlp_ref, f32[1024,1152]{1,0:T(8,128)} %get-tuple-element.68.gn2_ref, ...), custom_call_target="tpu_custom_call" | custom-call | tf_op jit(solution)/shard_map/middle_backward/pallas_call | solution.py:914
  361.9 121.8 %attention_backward.1 = (bf16[1024,3456]{1,0:T(8,128)(2,1)}, f32[144,1152]{1,0:T(8,128)}, f32[144,1152]{1,0:T(8,128)}) custom-call(f32[1]{0:T(128)} %bitcast.1.off_ref, bf16[1024,3456]{1,0:T(8,128)(2,1)} %get-tuple-element.60.qkv_ref, bf16[1024,1152]{1,0:T(8,128)(2,1)} %get-tuple-element.74.do_ref, f32[16,1024]{1,0:T(8,128)} %get-tuple-element.75.lse_ref, ...), custom_call_target="tpu_custom_call" | custom-call | tf_op jit(solution)/shard_map/attention_backward/pallas_call | solution.py:671
  483.8 18.2 %qkv_backward.1 = (f32[1024,1152]{1,0:T(8,128)}, f32[4,2,1152]{2,1,0:T(2,128)}) custom-call(bf16[1024,3456]{1,0:T(8,128)(2,1)} %get-tuple-element.79.dqkv_ref.q_ref.k_ref.v_ref, bf16[1152,3456]{1,0:T(8,128)(2,1)} %get-tuple-element.80.w_ref, f32[1024,1152]{1,0:T(8,128)} %tokens_ref.5, f32[1024,1152]{1,0:T(8,128)} %get-tuple-element.81.ga_ref, ...), custom_call_target="tpu_custom_call" | custom-call | tf_op jit(solution)/shard_map/qkv_backward/pallas_call | solution.py:991
  506.9 1.2 copy.87
  508.7 1.2 copy.88
  509.9 15.9 %qkv_weight_gradient.1 = (bf16[3,32,144,384]{3,2,1,0:T(8,128)(2,1)}, f32[3,1,1152]{2,1,0:T(1,128)}) custom-call(bf16[1024,1152]{1,0:T(8,128)(2,1)} %get-tuple-element.84.n1_ref, bf16[1024,3456]{1,0:T(8,128)(2,1)} %get-tuple-element.79.dqkv_ref.q_ref.k_ref.v_ref, bf16[1024,3456]{1,0:T(8,128)(2,1)} %get-tuple-element.79.dqkv_ref.q_ref.k_ref.v_ref, ...), custom_call_target="tpu_custom_call" | custom-call | tf_op jit(solution)/shard_map/qkv_weight_gradient/pallas_call | solution.py:964
  527.3 72.6 %attention_weight_sums.1 = (f32[144,1152]{1,0:T(8,128)}, f32[4,4,2,88,128]{4,3,2,1,0:T(8,128)}, bf16[4,4,2,224,128]{4,3,2,1,0:T(8,128)(2,1)}) custom-call(bf16[3,4,4,2,144,384]{5,4,3,2,1,0:T(8,128)(2,1)} %bitcast.95, f32[88,128]{1,0:T(8,128)} %pad_bitcast_fusion.sums_ref, bf16[224,128]{1,0:T(8,128)(2,1)} %pad.14.mods_ref), custom_call_target="tpu_custom_call" | custom-call | tf_op jit(solution)/shard_map/attention_weight_sums/pallas_call | solution.py:1037
  600.0 2.2 copy.119
  602.3 2.4 reshape.226
  604.7 1.6 copy.120
  606.3 1.6 convert_reduce_fusion
  607.9 2.3 fusion.8
  (133 shorter events, 30.4 us)
Async XLA Ops:
  0.7 10.8 %copy-start = (bf16[1152,32]{0,1:T(8,128)(2,1)S(1)}, bf16[1152,32]{0,1:T(8,128)(2,1)}, u32[]{:S(2)}) copy-start(bf16[1152,32]{0,1:T(8,128)(2,1)} %param.42) | copy-start | bytes 221188
  0.7 21.3 %copy-start.6 = (bf16[576,288]{0,1:T(8,128)(2,1)S(1)}, bf16[576,288]{0,1:T(8,128)(2,1)}, u32[]{:S(2)}) copy-start(bf16[576,288]{0,1:T(8,128)(2,1)} %param.38) | copy-start | bytes 995332
  0.7 23.7 %copy-start.5 = (bf16[1152,216]{0,1:T(8,128)(2,1)S(1)}, bf16[1152,216]{0,1:T(8,128)(2,1)}, u32[]{:S(2)}) copy-start(bf16[1152,216]{0,1:T(8,128)(2,1)} %param.29) | copy-start | bytes 1492996
  483.7 19.9 %copy-start.9 = (f32[4,1,1152]{2,1,0:T(1,128)S(1)}, f32[4,1,1152]{2,1,0:T(1,128)}, u32[]{:S(2)}) copy-start(f32[4,1,1152]{2,1,0:T(1,128)} %get-tuple-element.89) | copy-start | bytes 55300
  483.8 20.0 %copy-start.7 = (f32[4,4,1152]{2,1,0:T(4,128)S(1)}, f32[4,4,1152]{2,1,0:T(4,128)}, u32[]{:S(2)}) copy-start(f32[4,4,1152]{2,1,0:T(4,128)} %get-tuple-element.91) | copy-start | bytes 221188
  483.8 20.3 %copy-start.10 = (f32[3,1152]{1,0:T(4,128)S(1)}, f32[3,1152]{1,0:T(4,128)}, u32[]{:S(2)}) copy-start(f32[3,1152]{1,0:T(4,128)} %get-tuple-element.88) | copy-start | bytes 41476
  483.8 20.7 %copy-start.8 = (f32[8,4,1152]{2,1,0:T(4,128)S(1)}, f32[8,4,1152]{2,1,0:T(4,128)}, u32[]{:S(2)}) copy-start(f32[8,4,1152]{2,1,0:T(4,128)} %get-tuple-element.90) | copy-start | bytes 442372
  483.8 22.5 %copy-start.4 = (f32[144,1152]{1,0:T(8,128)S(1)}, f32[144,1152]{1,0:T(8,128)}, u32[]{:S(2)}) copy-start(f32[144,1152]{1,0:T(8,128)} %get-tuple-element.96) | copy-start | bytes 1990660
  502.0 6.0 copy-start.3
  602.3 11.6 %copy-start.2 = (f32[144,1152]{1,0:T(8,128)S(1)}, f32[144,1152]{1,0:T(8,128)}, u32[]{:S(2)}) copy-start(f32[144,1152]{1,0:T(8,128)} %get-tuple-element.94) | copy-start | bytes 1990660
  607.9 7.9 %copy-start.1 = (bf16[1152,32]{0,1:T(8,128)(2,1)S(1)}, bf16[1152,32]{0,1:T(8,128)(2,1)}, u32[]{:S(2)}) copy-start(bf16[1152,32]{0,1:T(8,128)(2,1)} %param.42) | copy-start | bytes 221188
  612.0 3.8 copy-start.11

commit v3 on v2

--- a/solution.py
+++ b/solution.py
@@ -276,114 +276,138 @@
 
 
 class Scatter:
-    def __init__(self, place, part, out, own, r1, r2, r3, r4, own_sem, s1, s2, s3, s4):
-        self.p, self.part, self.out = place, part, out
+    def __init__(self, place, turn, js, source, own, r1, r2, r3, r4, own_sem, s1, s2, s3, s4):
+        self.p, self.turn, self.js, self.source = place, turn, js, source
         self.own, self.r1, self.r2, self.r3, self.r4 = own, r1, r2, r3, r4
         self.own_sem, self.s1, self.s2, self.s3, self.s4 = own_sem, s1, s2, s3, s4
 
     def owner(self, j):
         return lax.rem(self.p.z + 1 + j, self.p.planes)
 
+    def moves_on(self, j):
+        return j + 1 < self.p.planes
+
     def load(self, j):
-        p = self.p
+        slot = self.js.index(j) % 2
         return pltpu.make_async_copy(
-            self.part.at[:, self.owner(j), p.c], self.own.at[j % 2], self.own_sem.at[j % 2]
+            self.source(j, self.p.c), self.own.at[slot], self.own_sem.at[slot]
         )
+
+    def x_first(self, j):
+        return (self.js.index(j) + self.turn) % 2 == 0
 
     def sides(self, j):
         p = self.p
-        return (p.xn, p.yn) if j % 2 == 0 else (p.yn, p.xn)
+        return (p.xn, p.yn) if self.x_first(j) else (p.yn, p.xn)
 
     def copies(self, stage, j):
         p = self.p
+        i = self.js.index(j)
         side, other = self.sides(j)
         if stage == 1:
             to = p.dev(p.n, p.z, 1 - p.c)
-            return [remote(self.part.at[:, self.owner(j), 1 - p.c], self.r1.at[j], self.s1, j, to)]
+            return [remote(self.source(j, 1 - p.c), self.r1.at[i], self.s1, i, to)]
         if stage == 2:
             to = p.dev(side, p.z, p.c)
             return [
-                remote(self.r1.at[j, side], self.r2.at[j, 0], self.s2, 2 * j, to),
-                remote(self.r1.at[j, p.dn], self.r2.at[j, 1], self.s2, 2 * j + 1, to),
+                remote(self.r1.at[i, side], self.r2.at[i, 0], self.s2, 2 * i, to),
+                remote(self.r1.at[i, p.dn], self.r2.at[i, 1], self.s2, 2 * i + 1, to),
             ]
         if stage == 3:
             to = p.dev(other, p.z, p.c)
-            return [remote(self.r1.at[j, other], self.r3.at[j], self.s3, j, to)]
+            return [remote(self.r1.at[i, other], self.r3.at[i], self.s3, i, to)]
         to = p.dev(p.n, self.owner(j), p.c)
-        return [remote(self.r1.at[j, p.n], self.r4.at[j], self.s4, j, to)]
+        return [remote(self.r1.at[i, p.n], self.r4.at[i], self.s4, i, to)]
 
     def issue(self, stage, j):
         for copy in self.copies(stage, j):
             copy.start()
 
+    def sent(self, stage, j):
+        for copy in self.copies(stage, j):
+            copy.wait_send()
+
+    def begin(self):
+        if self.own is not None:
+            self.load(self.js[0]).start()
+
     def take(self, stage, j):
         p = self.p
+        i = self.js.index(j)
         for copy in self.copies(stage, j):
             copy.wait_recv()
         side, other = self.sides(j)
 
         def add(n, value):
-            self.r1[j, n] = (self.r1[j, n].astype(F32) + value.astype(F32)).astype(BF)
+            self.r1[i, n] = (self.r1[i, n].astype(F32) + value.astype(F32)).astype(BF)
 
         if stage == 1:
-            self.load(j).wait()
-            if j + 1 < p.planes:
-                self.load(j + 1).start()
+            if self.own is None:
+                mine = self.source(j, p.c)
+            else:
+                self.load(j).wait()
+                if i + 1 < len(self.js):
+                    self.load(self.js[i + 1]).start()
+                mine = self.own.at[i % 2]
             for n in range(4):
-                add(n, self.own[j % 2, n])
+                add(n, mine[n])
         elif stage == 2:
-            add(p.n, self.r2[j, 0])
-            add(other, self.r2[j, 1])
+            add(p.n, self.r2[i, 0])
+            add(other, self.r2[i, 1])
         else:
-            add(p.n, self.r3[j])
-            if j + 1 < p.planes:
+            add(p.n, self.r3[i])
+            if self.moves_on(j):
                 self.issue(4, j)
 
-    def end(self):
-        planes = self.p.planes
-        total = self.r1[planes - 1, self.p.n].astype(F32)
-        for j in range(planes - 1):
-            self.copies(4, j)[0].wait_recv()
-            total = total + self.r4[j].astype(F32)
-        self.out[...] = total
-        for j in range(planes):
-            for stage in (1, 2, 3, 4):
-                if stage < 4 or j + 1 < planes:
-                    for copy in self.copies(stage, j):
-                        copy.wait_send()
+    def total(self, stages=(1, 2, 3, 4)):
+        found = None
+        for i, j in enumerate(self.js):
+            if self.moves_on(j):
+                self.copies(4, j)[0].wait_recv()
+                part = self.r4[i].astype(F32)
+            else:
+                part = self.r1[i, self.p.n].astype(F32)
+            found = part if found is None else found + part
+        for j in self.js:
+            for stage in stages:
+                if stage < 4 or self.moves_on(j):
+                    self.sent(stage, j)
+        return found
 
     @staticmethod
-    def scratch(planes, rows, cols):
+    def scratch(count, rows, cols, load=True):
         dma = pltpu.SemaphoreType.DMA
-        return [
-            pltpu.VMEM((2, 4, rows, cols), BF),
-            pltpu.VMEM((planes, 4, rows, cols), BF),
-            pltpu.VMEM((planes, 2, rows, cols), BF),
-            pltpu.VMEM((planes, rows, cols), BF),
-            pltpu.VMEM((planes - 1, rows, cols), BF),
+        own = [pltpu.VMEM((2, 4, rows, cols), BF)] if load else []
+        return own + [
+            pltpu.VMEM((count, 4, rows, cols), BF),
+            pltpu.VMEM((count, 2, rows, cols), BF),
+            pltpu.VMEM((count, rows, cols), BF),
+            pltpu.VMEM((count, rows, cols), BF),
             dma((2,)),
-            dma((2, planes)),
-            dma((2, 2 * planes)),
-            dma((2, planes)),
-            dma((2, planes)),
+            dma((2, count)),
+            dma((2, 2 * count)),
+            dma((2, count)),
+            dma((2, count)),
         ]
 
 
 def scatter_steps(scatters, window=2):
-    planes = scatters[0].p.planes
-    count = len(scatters)
-    queue = [(u, j) for j in range(planes) for u in range(count)]
+    js = scatters[0].js
+    units = range(len(scatters))
+    queue = [(u, j) for j in js for u in units]
     x_items, y_items = [], []
-    for even in range(0, planes, 2):
-        for stage, swap in ((2, 0), (3, 1)):
-            x_items += [(stage, u, even + swap) for u in range(count)]
-            y_items += [(stage, u, even + 1 - swap) for u in range(count)]
+    for i in range(0, len(js), 2):
+        pair = [(u, j) for j in js[i : i + 2] for u in units]
+        for stage in (2, 3):
+            for u, j in pair:
+                first = scatters[u].x_first(j)
+                (x_items if first == (stage == 2) else y_items).append((stage, u, j))
     sent = []
     done = []
 
     def begin():
         for s in scatters:
-            s.load(0).start()
+            s.begin()
         for u, j in queue[:window]:
             scatters[u].issue(1, j)
             sent.append((u, j))
@@ -401,7 +425,7 @@
 
     def step(i):
         for items in (x_items, y_items):
-            if i >= window:
+            if window <= i < len(items) + window:
                 stage, u, j = items[i - window]
                 scatters[u].take(stage, j)
         for items in (x_items, y_items):
@@ -410,93 +434,140 @@
                 ready(stage, u, j)
                 scatters[u].issue(stage, j)
 
-    def end():
-        for s in scatters:
-            s.end()
-
-    steps = [functools.partial(step, i) for i in range(len(x_items) + window)]
-    return [begin] + steps + [end]
+    count = max(len(x_items), len(y_items)) + window
+    return [begin] + [functools.partial(step, i) for i in range(count)]
+
+
+class Exchange:
+    def __init__(self, place, src, out, sems, same):
+        self.p, self.src, self.out, self.sems, self.same = place, src, out, sems, same
+        self.wide = 2 * place.planes
+        self.total = 4 * self.wide
+        self.me = place.n * self.wide + place.z * 2 + place.c
+
+    def device(self, i):
+        other = lax.rem(self.me + i, self.total)
+        return other // self.wide, lax.rem(other, self.wide)
+
+    def greet(self):
+        sem = pltpu.get_barrier_semaphore()
+
+        def signal(i, carry):
+            pl.semaphore_signal(sem, inc=1, device_id=self.device(i), device_id_type=MESH)
+            return carry
+
+        lax.fori_loop(1, self.total, signal, 0)
+        pl.semaphore_wait(sem, self.total - 1)
+
+    def copy(self, i):
+        other = lax.rem(self.me + i, self.total)
+        src = self.src if self.same else self.src.at[other]
+        return remote(src, self.out.at[self.me], self.sems, i, self.device(i))
+
+    def each(self, do):
+        def body(i, carry):
+            do(i)
+            return carry
+
+        lax.fori_loop(1, self.total, body, 0)
+
+    def start(self):
+        self.each(lambda i: self.copy(i).start())
+        self.out[self.me] = self.src[...] if self.same else self.src[self.me]
+
+    def arrive(self):
+        def wait(i):
+            dst = self.out.at[lax.rem(self.me + self.total - i, self.total)]
+            remote(dst, dst, self.sems, i, self.device(i)).wait_recv()
+
+        self.each(wait)
+
+    def end(self):
+        self.each(lambda i: self.copy(i).wait_send())
+
+    @staticmethod
+    def scratch(planes):
+        return pltpu.SemaphoreType.DMA((2, 8 * planes))
+
+
+class Stream:
+    def __init__(self, slots, sems, out):
+        self.slots, self.sems, self.out = slots, sems, out
+        self.count = 0
+
+    def copy(self, i):
+        rows = self.slots.shape[1]
+        return pltpu.make_async_copy(
+            self.slots.at[i % 2], self.out.at[pl.ds(i * rows, rows)], self.sems.at[i % 2]
+        )
+
+    def put(self, value):
+        i = self.count
+        if i >= 2:
+            self.copy(i - 2).wait()
+        self.slots[i % 2] = value
+        self.copy(i).start()
+        self.count = i + 1
+
+    def end(self):
+        for i in range(max(self.count - 2, 0), self.count):
+            self.copy(i).wait()
+
+    @staticmethod
+    def scratch(rows, width, dtype):
+        return [pltpu.VMEM((2, rows, width), dtype), pltpu.SemaphoreType.DMA((2,))]
 
 
 def prologue_kernel(
-    shard_ref, cond_ref, ada_ref, ada_bias_ref, g_ref, conds_ref, mods_ref, mod_local, *sems, planes, items
+    shard_ref, cond_ref, ada_ref, ada_bias_ref, g_ref, conds_ref, mods_ref, mod_local, cond_sems, mod_sems, *sems, planes, slots
 ):
     place = Place(planes)
-    place.barrier()
-    weights = Gather(place, shard_ref, g_ref, *sems[:6])
-    conds = Gather(place, cond_ref, conds_ref, *sems[6:12])
-    mods = Gather(place, mod_local, mods_ref, *sems[12:])
+    weights = Gather(place, shard_ref, g_ref, *sems)
+    conds = Exchange(place, cond_ref, conds_ref, cond_sems, True)
+    mods = Exchange(place, mod_local, mods_ref, mod_sems, False)
+    conds.greet()
+    weights.run("begin")
+    conds.start()
+    mod_local[...] = jnp.zeros_like(mod_local)
     parts = weights.parts()
-    conds.run("begin")
-    weights.run("begin")
-    for part in parts[1:]:
-        conds.run(part)
+    for part in parts[1:4]:
+        weights.run(part)
+    conds.arrive()
+    devices, rows, lanes = conds_ref.shape
+    d, width = ada_ref.shape
+    every = conds_ref[...].reshape(devices * rows, lanes)
+    columns = ada_bias_ref[...]
+    for j in range(d // lanes):
+        piece = dg(every, ada_ref[j * lanes : (j + 1) * lanes, :], NN).reshape(devices, rows, width)
+        columns = columns + piece[:, slots * j : slots * (j + 1)]
+    mod_local[:, :slots, :width] = columns.astype(BF)
+    mods.start()
+    for part in parts[4:-1]:
+        weights.run(part)
+    mods.arrive()
+    conds.end()
+    mods.end()
+    weights.run("end")
+
+
+def prologue_call(shard, cond, ada, ada_bias, planes, slots):
     devices = 8 * planes
-    rows = cond_ref.shape[0]
-    every = conds_ref[...].reshape(devices * rows, cond_ref.shape[1])
-    columns = (dg(every, ada_ref[...], NN) + ada_bias_ref[...]).reshape(devices, rows, -1)
-    width = columns.shape[2]
-    mod_local[...] = jnp.zeros_like(mod_local)
-    for i in range(devices):
-        mod_local[i * items : (i + 1) * items, :width] = columns[i, :items].astype(BF)
-    mods.run("begin")
-    for part in parts[1:]:
-        weights.run(part)
-        mods.run(part)
-
-
-def prologue_call(shard, cond, ada, ada_bias, planes, items):
-    devices = 8 * planes
-    rows, d = cond.shape
     lanes = up_to(ada.shape[1], 128)
-    slots = devices * items
-    spread = (4, planes, 2)
     return pl.pallas_call(
-        functools.partial(prologue_kernel, planes=planes, items=items),
+        functools.partial(prologue_kernel, planes=planes, slots=slots),
         out_shape=(
-            shape(spread + shard.shape, BF),
-            shape(spread + (rows, d), BF),
-            shape(spread + (slots, lanes), BF),
+            shape((4, planes, 2) + shard.shape, BF),
+            shape((devices,) + cond.shape, BF),
+            shape((devices, 16, lanes), BF),
         ),
         in_specs=[ANY_SPEC, VMEM_SPEC, VMEM_SPEC, VMEM_SPEC],
-        out_specs=(ANY_SPEC, VMEM_SPEC, ANY_SPEC),
-        scratch_shapes=[pltpu.VMEM((slots, lanes), BF)] + Gather.scratch(planes) * 3,
+        out_specs=(ANY_SPEC, VMEM_SPEC, VMEM_SPEC),
+        scratch_shapes=[pltpu.VMEM((devices, 16, lanes), BF)]
+        + [Exchange.scratch(planes)] * 2
+        + Gather.scratch(planes),
         compiler_params=params(collective_id=1),
         name="weights_and_modulation",
     )(shard, cond, ada, ada_bias)
-
-
-def qkv_kernel(tokens_ref, shift_ref, scale_ref, g_ref, bias_ref, n1_ref, qkv_ref, w_ref, wp_ref):
-    d = tokens_ref.shape[1]
-    devices = g_ref.shape[0]
-    r = d // devices
-
-    @pl.when(pl.program_id(0) == 0)
-    def _():
-        for i in range(devices):
-            rows = slice(i * r, (i + 1) * r)
-            for b in range(3):
-                w_ref[rows, b * d : (b + 1) * d] = g_ref[i, b * r : (b + 1) * r, :]
-            wp_ref[rows, :] = g_ref[i, 3 * r : 4 * r, :]
-
-    normed, _ = ln_parts(tokens_ref[...])
-    low = (normed * (1.0 + scale_ref[0]) + shift_ref[0]).astype(BF)
-    n1_ref[...] = low
-    qkv_ref[...] = (dg(low, w_ref[...], NN) + bias_ref[...]).astype(BF)
-
-
-def qkv_call(tokens, shift, scale, g, bias, blk):
-    t, d = tokens.shape
-    n = 3 * d
-    return pl.pallas_call(
-        qkv_kernel,
-        grid=(t // blk,),
-        out_shape=(shape((t, d), BF), shape((t, n), BF), shape((d, n), BF), shape((d, d), BF)),
-        in_specs=[rows_of(blk, d), row_vec(d), row_vec(d), whole(*g.shape), whole(1, n)],
-        out_specs=(rows_of(blk, d), rows_of(blk, n), whole(d, n), whole(d, d)),
-        compiler_params=params(),
-        name="qkv_forward",
-    )(tokens, shift, scale, g, bias)
 
 
 def head_window(h, hd, width):
@@ -505,84 +576,245 @@
     return a, (lane >= h * hd) & (lane < h * hd + hd)
 
 
-def attn_fwd_kernel(
+QUERY_BIAS, VALUE_BIAS, PROJ_BIAS, DOWN_BIAS, ROUTER = range(5)
+SHIFT1, SCALE1, GATE1, SHIFT2, SCALE2, GATE2 = range(6)
+
+
+def forward_kernel(
     off_ref,
     gate_ref,
-    qkv_ref,
+    mod_ref,
+    vec_ref,
+    keep_ref,
+    tokens_ref,
+    cot_ref,
+    g_ref,
     up_ref,
     down_ref,
+    lse_ref,
+    tg_ref,
+    n1_ref,
+    qkv_ref,
+    w_ref,
+    wp_ref,
     att_ref,
     gated_ref,
-    lse_ref,
+    attn_ref,
+    after_ref,
+    n2_ref,
+    gm_ref,
     g_up_ref,
     g_down_ref,
     lse_sc,
-    *sems,
+    g_s,
+    tok_s,
+    w_s,
+    wp_s,
+    n1_s,
+    qkv_s,
+    att_s,
+    gated_s,
+    cot_s,
+    cot_sems,
+    sems,
+    attn_slots,
+    attn_sems,
+    after_slots,
+    after_sems,
+    n2_slots,
+    n2_sems,
+    gm_slots,
+    gm_sems,
+    *gather_sems,
     heads,
     blk,
     planes,
 ):
+    t, d = tok_s.shape
+    hd = d // heads
+    nb = t // blk
+    c = hd**-0.5 * LOG2E
     place = Place(planes)
     place.barrier()
-    gathers = [Gather(place, up_ref, g_up_ref, *sems[:6]), Gather(place, down_ref, g_down_ref, *sems[6:])]
+    half = len(gather_sems) // 2
+    gathers = [
+        Gather(place, up_ref, g_up_ref, *gather_sems[:half]),
+        Gather(place, down_ref, g_down_ref, *gather_sems[half:]),
+    ]
     parts = gathers[0].parts()
     for g in gathers:
         g.run("begin")
     groups = spread_out(
-        [functools.partial(g.run, part) for part in parts[1:-1] for g in gathers], heads
-    )
-    t, d = att_ref.shape
-    hd = d // heads
-    nb = t // blk
-    c = hd**-0.5 * LOG2E
+        [functools.partial(g.run, part) for part in parts[1:-1] for g in gathers], 2 * nb + heads
+    )
+
+    def run_group(i):
+        for step in groups[i]:
+            step()
+
+    moves = {
+        name: pltpu.make_async_copy(src, dst, sems.at[i])
+        for i, (name, src, dst) in enumerate(
+            (
+                ("g", g_ref, g_s),
+                ("tok", tokens_ref, tok_s),
+                ("w", w_s, w_ref),
+                ("wp", wp_s, wp_ref),
+                ("n1", n1_s, n1_ref),
+                ("qkv", qkv_s, qkv_ref),
+                ("att", att_s, att_ref),
+                ("gated", gated_s, gated_ref),
+            )
+        )
+    }
+
+    def cot_copy(i):
+        return pltpu.make_async_copy(
+            cot_ref.at[pl.ds(i * blk, blk)], cot_s.at[i % 2], cot_sems.at[i % 2]
+        )
+
+    moves["g"].start()
+    moves["tok"].start()
+    for i in range(2):
+        cot_copy(i).start()
+    devices = g_s.shape[0]
+    r = d // devices
+    moves["g"].wait()
+    for i in range(devices):
+        rows = slice(i * r, (i + 1) * r)
+        for b in range(3):
+            w_s[rows, b * d : (b + 1) * d] = g_s[i, b * r : (b + 1) * r, :]
+        wp_s[rows, :] = g_s[i, 3 * r : 4 * r, :]
+    moves["w"].start()
+    moves["wp"].start()
+    moves["tok"].wait()
+
+    def vector(i):
+        return vec_ref[i : i + 1, :]
+
+    def mod(i, k):
+        return mod_ref[i, k : k + 1, :]
+
+    bias = jnp.concatenate(
+        [vector(QUERY_BIAS), jnp.zeros((1, d), F32), vector(VALUE_BIAS)], axis=1
+    )
+    for i in range(nb):
+        rows = slice(i * blk, (i + 1) * blk)
+        normed, _ = ln_parts(tok_s[rows, :])
+        low = (normed * (1.0 + mod(i, SCALE1)) + mod(i, SHIFT1)).astype(BF)
+        n1_s[rows, :] = low
+        qkv_s[rows, :] = (dg(low, w_s[...], NN) + bias).astype(BF)
+        run_group(i)
+    moves["n1"].start()
+    moves["qkv"].start()
     off = off_ref[0]
     lane128 = lax.broadcasted_iota(jnp.int32, (1, 128), 1)
 
     def body(h, carry):
         a, mask = head_window(h, hd, d)
-        keys = qkv_ref[:, pl.ds(pl.multiple_of(d + a, 128), WINDOW)]
-        values = qkv_ref[:, pl.ds(pl.multiple_of(2 * d + a, 128), WINDOW)]
+        keys = qkv_s[:, pl.ds(pl.multiple_of(d + a, 128), WINDOW)]
+        values = qkv_s[:, pl.ds(pl.multiple_of(2 * d + a, 128), WINDOW)]
         cols = pl.ds(a, WINDOW)
         for i in range(nb):
             rows = pl.ds(i * blk, blk)
-            q = qkv_ref[rows, cols]
+            q = qkv_s[rows, cols]
             q = jnp.where(mask, q, jnp.zeros_like(q))
             s = dg(q, keys, NT)
-            parts = [s[:, j * blk : (j + 1) * blk] for j in range(nb)]
-            own = jnp.max(parts[i], axis=1, keepdims=True) * c
-            others = functools.reduce(jnp.maximum, [parts[j] for j in range(nb) if j != i])
+            cuts = [s[:, j * blk : (j + 1) * blk] for j in range(nb)]
+            own = jnp.max(cuts[i], axis=1, keepdims=True) * c
+            others = functools.reduce(jnp.maximum, [cuts[j] for j in range(nb) if j != i])
             m = jnp.maximum(own, jnp.max(others, axis=1, keepdims=True) * c + off)
             m_off = m - off
-            ps = [jnp.exp2(parts[j] * c - (m if j == i else m_off)) for j in range(nb)]
+            ps = [jnp.exp2(cuts[j] * c - (m if j == i else m_off)) for j in range(nb)]
             total = jnp.sum(functools.reduce(jnp.add, ps), axis=1, keepdims=True)
             p = jnp.concatenate([x.astype(BF) for x in ps], axis=1)
             o = dg(p, values, NN) * (1.0 / total)
             og = (o * gate_ref[i, :, cols]).astype(BF)
-            att_ref[rows, cols] = jnp.where(mask, o, att_ref[rows, cols])
-            gated_ref[rows, cols] = jnp.where(mask, og, gated_ref[rows, cols])
+            att_s[rows, cols] = jnp.where(mask, o, att_s[rows, cols])
+            gated_s[rows, cols] = jnp.where(mask, og, gated_s[rows, cols])
             lse_sc[rows, :] = jnp.where(lane128 == h, m + jnp.log2(total), lse_sc[rows, :])
-        run_at(h, groups)
+        run_at(h, groups[nb : nb + heads])
         return carry
 
     lax.fori_loop(0, heads, body, 0)
+    moves["att"].start()
+    moves["gated"].start()
     lse_ref[...] = lse_sc[...].T[:heads, :]
+    streams = [
+        Stream(attn_slots, attn_sems, attn_ref),
+        Stream(after_slots, after_sems, after_ref),
+        Stream(n2_slots, n2_sems, n2_ref),
+        Stream(gm_slots, gm_sems, gm_ref),
+    ]
+    for i in range(nb):
+        rows = slice(i * blk, (i + 1) * blk)
+        attn = dg(gated_s[rows, :], wp_s[...], NN) + vector(PROJ_BIAS)
+        streams[0].put(attn)
+        after = tok_s[rows, :] + mod(i, GATE1) * attn
+        streams[1].put(after)
+        normed, _ = ln_parts(after)
+        y = normed * (1.0 + mod(i, SCALE2)) + mod(i, SHIFT2)
+        streams[2].put(y.astype(BF))
+        token_gate = jax.nn.sigmoid(jnp.sum(y * vector(ROUTER), axis=1, keepdims=True))
+        tg_ref[rows, :] = token_gate
+        cot_copy(i).wait()
+        cot = cot_s[i % 2]
+        streams[3].put((cot * (mod(i, GATE2) * (keep_ref[rows, :] * token_gate))).astype(BF))
+        if i + 2 < nb:
+            cot_copy(i + 2).start()
+        run_group(nb + heads + i)
     for g in gathers:
         g.run("end")
-
-
-def attn_fwd(off, gate_rows, qkv, up, down, heads, blk, planes):
-    t = qkv.shape[0]
-    d = qkv.shape[1] // 3
+    for stream in streams:
+        stream.end()
+    for name in ("w", "wp", "n1", "qkv", "att", "gated"):
+        moves[name].wait()
+
+
+def forward_call(off, gate_rows, mods, vecs, keep, tokens, cot, g, up, down, heads, blk, planes):
+    t, d = tokens.shape
     gathered = shape((4, planes, 2) + up.shape, BF)
+    dma = pltpu.SemaphoreType.DMA
     return pl.pallas_call(
-        functools.partial(attn_fwd_kernel, heads=heads, blk=blk, planes=planes),
-        out_shape=(shape((t, d)), shape((t, d), BF), shape((heads, t)), gathered, gathered),
-        in_specs=[SMEM_SPEC, VMEM_SPEC, VMEM_SPEC, ANY_SPEC, ANY_SPEC],
-        out_specs=(VMEM_SPEC,) * 3 + (ANY_SPEC,) * 2,
-        scratch_shapes=[pltpu.VMEM((t, 128), F32)] + Gather.scratch(planes) * 2,
-        compiler_params=params(collective_id=2),
-        name="attention_forward",
-    )(off, gate_rows, qkv, up, down)
+        functools.partial(forward_kernel, heads=heads, blk=blk, planes=planes),
+        out_shape=(
+            shape((heads, t)),
+            shape((t, 1)),
+            shape((t, d), BF),
+            shape((t, 3 * d), BF),
+            shape((d, 3 * d), BF),
+            shape((d, d), BF),
+            shape((t, d)),
+            shape((t, d), BF),
+            shape((t, d)),
+            shape((t, d)),
+            shape((t, d), BF),
+            shape((t, d), BF),
+            gathered,
+            gathered,
+        ),
+        in_specs=[SMEM_SPEC] + [VMEM_SPEC] * 4 + [ANY_SPEC] * 5,
+        out_specs=(VMEM_SPEC,) * 2 + (ANY_SPEC,) * 12,
+        scratch_shapes=[
+            pltpu.VMEM((t, 128), F32),
+            pltpu.VMEM(g.shape, BF),
+            pltpu.VMEM((t, d), F32),
+            pltpu.VMEM((d, 3 * d), BF),
+            pltpu.VMEM((d, d), BF),
+            pltpu.VMEM((t, d), BF),
+            pltpu.VMEM((t, 3 * d), BF),
+            pltpu.VMEM((t, d), F32),
+            pltpu.VMEM((t, d), BF),
+            pltpu.VMEM((2, blk, d), F32),
+            dma((2,)),
+            dma((8,)),
+        ]
+        + Stream.scratch(blk, d, F32) * 2
+        + Stream.scratch(blk, d, BF) * 2
+        + Gather.scratch(planes) * 2,
+        compiler_params=params(62, collective_id=2),
+        name="attention_and_middle_forward",
+    )(off, gate_rows, mods, vecs, keep, tokens, cot, g, up, down)
 
 
 def attn_bwd_kernel(
@@ -606,11 +838,19 @@
     place = Place(planes)
     place.barrier(True)
     half = len(rest) // 2
-    steps = scatter_steps(
-        [Scatter(place, up_ref, g_up_ref, *rest[:half]), Scatter(place, down_ref, g_down_ref, *rest[half:])]
-    )
+    first = planes // 2
+
+    def source(ref):
+        return lambda j, c: ref.at[:, j - first, c]
+
+    js = list(range(first, planes))
+    scatters = [
+        Scatter(place, 0, js, source(up_ref), *rest[:half]),
+        Scatter(place, 1, js, source(down_ref), *rest[half:]),
+    ]
+    steps = scatter_steps(scatters)
     steps[0]()
-    groups = spread_out(steps[1:-1], heads)
+    groups = spread_out(steps[1:], heads)
     t, d = do_ref.shape
     hd = d // heads
     nb = t // blk
@@ -662,7 +902,8 @@
         return carry
 
     lax.fori_loop(0, heads, body, 0)
-    steps[-1]()
+    g_up_ref[...] = scatters[0].total()
+    g_down_ref[...] = scatters[1].total()
 
 
 def attn_bwd(off, qkv, do, lse, delta, up, down, heads, blk, planes):
@@ -674,97 +915,117 @@
         in_specs=[SMEM_SPEC] + [VMEM_SPEC] * 4 + [ANY_SPEC] * 2,
         out_specs=(VMEM_SPEC,) * 3,
         scratch_shapes=[pltpu.VMEM((d, t), BF), pltpu.VMEM((WINDOW, t), BF)]
-        + Scatter.scratch(planes, rows, cols) * 2,
+        + Scatter.scratch(planes - planes // 2, rows, cols) * 2,
         compiler_params=params(collective_id=3),
         name="attention_backward",
     )(off, qkv, do, lse, delta, up, down)
 
 
-def middle_kernel(
-    gated_ref,
-    w_ref,
-    bias_ref,
-    tokens_ref,
-    cot_ref,
-    keep_ref,
-    router_ref,
-    gate1_ref,
-    shift2_ref,
-    scale2_ref,
-    gate2_ref,
-    attn_ref,
-    after_ref,
-    n2_ref,
-    gm_ref,
-    tg_ref,
-):
-    attn = dg(gated_ref[...], w_ref[...], NN) + bias_ref[...]
-    attn_ref[...] = attn
-    after = tokens_ref[...] + gate1_ref[0] * attn
-    after_ref[...] = after
-    normed, _ = ln_parts(after)
-    y = normed * (1.0 + scale2_ref[0]) + shift2_ref[0]
-    n2_ref[...] = y.astype(BF)
-    token_gate = jax.nn.sigmoid(jnp.sum(y * router_ref[...], axis=1, keepdims=True))
-    tg_ref[...] = token_gate
-    gm_ref[...] = (cot_ref[...] * (gate2_ref[0] * (keep_ref[...] * token_gate))).astype(BF)
-
-
-def middle_call(gated, w, bias, tokens, cot, keep, router, gate1, shift2, scale2, gate2, blk):
-    t, d = tokens.shape
-    r, v = rows_of(blk, d), row_vec(d)
-    column = rows_of(blk, 1)
-    return pl.pallas_call(
-        middle_kernel,
-        grid=(t // blk,),
-        out_shape=(shape((t, d)), shape((t, d)), shape((t, d), BF), shape((t, d), BF), shape((t, 1))),
-        in_specs=[r, whole(d, d), whole(1, d), r, r, column, whole(1, d), v, v, v, v],
-        out_specs=(r, r, r, r, column),
-        compiler_params=params(),
-        name="middle_forward",
-    )(gated, w, bias, tokens, cot, keep, router, gate1, shift2, scale2, gate2)
-
-
 def mlp_kernel(
     n2_ref,
     gm_ref,
+    b1_ref,
+    cs_ref,
     g1_ref,
     g2_ref,
-    b1_ref,
-    cs_ref,
     mlp_ref,
     gn2_ref,
+    gb1_ref,
+    gch_ref,
+    o1_ref,
+    o2_ref,
     p1_ref,
     p2_ref,
-    gb1_ref,
-    gch_ref,
+    g1_s,
+    g2_s,
     w1_s,
     w2_s,
     sc_s,
     gp_s,
-    *,
+    p1_s,
+    p2_s,
+    g_sems,
+    p_sems,
+    *rest,
     blk,
+    planes,
 ):
     t, d = n2_ref.shape
     nb = t // blk
     hidden = w1_s.shape[0]
     quarter = hidden // 8
     piece = d // 4
-
-    @pl.when(pl.program_id(0) == 0)
-    def _():
-        mlp_ref[...] = jnp.zeros_like(mlp_ref)
-        gn2_ref[...] = jnp.zeros_like(gn2_ref)
+    j = pl.program_id(0)
+    place = Place(planes)
+    hosted = planes // 2
+    half = len(rest) // 2
+    scatters = [
+        Scatter(place, u, list(range(hosted)), lambda j, c, p=p: p.at[:, c], None, *scratch)
+        for u, (p, scratch) in enumerate(((p1_s, rest[:half]), (p2_s, rest[half:])))
+    ]
+
+    def loads(step):
+        plane = lax.rem(place.z + 1 + step, planes)
+        return [
+            pltpu.make_async_copy(g.at[:, plane], slot, g_sems.at[i])
+            for i, (g, slot) in enumerate(((g1_ref, g1_s), (g2_ref, g2_s)))
+        ]
+
+    def keeps(step):
+        return [
+            pltpu.make_async_copy(slot, p.at[:, step - hosted], p_sems.at[i])
+            for i, (slot, p) in enumerate(((p1_s, p1_ref), (p2_s, p2_ref)))
+        ]
+
+    def early(step):
+        for s in scatters:
+            if step - 1 < hosted:
+                s.take(1, step - 1)
+                s.issue(2, step - 1)
+        for s in scatters:
+            if 0 <= step - 2 < hosted:
+                s.take(3, step - 2)
+
+    def late(step):
+        for s in scatters:
+            if step - 1 < hosted:
+                s.take(2, step - 1)
+                s.issue(3, step - 1)
+                s.sent(1, step - 1)
+        if step - 1 >= hosted:
+            for copy in keeps(step - 1):
+                copy.wait()
+
+    def at_steps(do):
+        for step in range(1, planes):
+            pl.when(j == step)(functools.partial(do, step))
 
     def places():
         for c in range(2):
             for k in range(4):
                 yield c, slice((4 * c + k) * quarter, (4 * c + k + 1) * quarter), k
 
+    @pl.when(j == 0)
+    def _():
+        for copy in loads(0):
+            copy.start()
+        place.barrier(True)
+        mlp_ref[...] = jnp.zeros_like(mlp_ref)
+        gn2_ref[...] = jnp.zeros_like(gn2_ref)
+
+    for copy in loads(j):
+        copy.wait()
     for c, rows, k in places():
         cols = slice(k * piece, (k + 1) * piece)
-        for w, g in ((w1_s, g1_ref), (w2_s, g2_ref)):
-            w[rows, :] = jnp.concatenate([g[n, 0, c, :quarter, cols] for n in range(4)], axis=1)
+        for w, g in ((w1_s, g1_s), (w2_s, g2_s)):
+            w[rows, :] = jnp.concatenate([g[n, c, :quarter, cols] for n in range(4)], axis=1)
+
+    @pl.when(j + 1 < planes)
+    def _():
+        for copy in loads(j + 1):
+            copy.start()
+
+    at_steps(early)
     w1 = w1_s[...]
     w2 = w2_s[...]
     grad_bias = None
@@ -784,11 +1045,30 @@
         mlp_ref[rows, :] += dg(scaled, w2, NN)
         gn2_ref[rows, :] += dg(grad_pre, w1, NN)
     gb1_ref[0] = grad_bias
-    for left, right, out in ((gp_s, n2_ref, p1_ref), (sc_s, gm_ref, p2_ref)):
+
+    at_steps(late)
+    for left, right, out in ((gp_s, n2_ref, p1_s), (sc_s, gm_ref, p2_s)):
         grad = dg(left[...], right[...], TN).astype(BF)
         for c, rows, k in places():
             for n in range(4):
-                out[n, 0, c, :quarter, k * piece : (k + 1) * piece] = grad[rows, n * piece : (n + 1) * piece]
+                out[n, c, :quarter, k * piece : (k + 1) * piece] = grad[rows, n * piece : (n + 1) * piece]
+    for step in range(planes):
+
+        @pl.when(j == step)
+        def _(step=step):
+            if step < hosted:
+                for s in scatters:
+                    s.issue(1, step)
+            else:
+                for copy in keeps(step):
+                    copy.start()
+
+    @pl.when(j == planes - 1)
+    def _():
+        o1_ref[...] = scatters[0].total((2, 3, 4))
+        o2_ref[...] = scatters[1].total((2, 3, 4))
+        for copy in keeps(planes - 1):
+            copy.wait()
 
 
 def mlp_call(n2, gm, g1, g2, b1, gates, blk):
@@ -796,27 +1076,41 @@
     planes, rows = g1.shape[1], g1.shape[3]
     nb, ff = gates.shape
     hb = ff // planes
-    g_spec = pl.BlockSpec((4, 1, 2, rows, d), lambda j: (0, j, 0, 0, 0))
-    b_spec = pl.BlockSpec((1, 1, hb), lambda j: (j, 0, 0))
-    c_spec = pl.BlockSpec((1, nb, hb), lambda j: (j, 0, 0))
-    mlp, gn2, p1, p2, gb1, gch = pl.pallas_call(
-        functools.partial(mlp_kernel, blk=blk),
+    hosted = planes // 2
+
+    def turn(j):
+        return lax.rem(lax.axis_index("wide") // 2 + 1 + j, planes)
+
+    b_spec = pl.BlockSpec((1, 1, hb), lambda j: (turn(j), 0, 0))
+    c_spec = pl.BlockSpec((1, nb, hb), lambda j: (turn(j), 0, 0))
+    kept = shape((4, planes - hosted, 2, rows, d), BF)
+    dma = pltpu.SemaphoreType.DMA
+    mlp, gn2, gb1, gch, o1, o2, p1, p2 = pl.pallas_call(
+        functools.partial(mlp_kernel, blk=blk, planes=planes),
         grid=(planes,),
         out_shape=(
             shape((t, d)),
             shape((t, d)),
-            shape(g1.shape, BF),
-            shape(g1.shape, BF),
             shape((planes, 1, hb)),
             shape((planes, nb, hb)),
+            shape((rows, d)),
+            shape((rows, d)),
+            kept,
+            kept,
         ),
-        in_specs=[whole(t, d), whole(t, d), g_spec, g_spec, b_spec, c_spec],
-        out_specs=(whole(t, d), whole(t, d), g_spec, g_spec, b_spec, c_spec),
-        scratch_shapes=[pltpu.VMEM((hb, d), BF)] * 2 + [pltpu.VMEM((t, hb), BF)] * 2,
-        compiler_params=params(),
+        in_specs=[whole(t, d), whole(t, d), b_spec, c_spec, ANY_SPEC, ANY_SPEC],
+        out_specs=(whole(t, d), whole(t, d), b_spec, c_spec, whole(rows, d), whole(rows, d))
+        + (ANY_SPEC,) * 2,
+        scratch_shapes=[pltpu.VMEM((4, 2, rows, d), BF)] * 2
+        + [pltpu.VMEM((hb, d), BF)] * 2
+        + [pltpu.VMEM((t, hb), BF)] * 2
+        + [pltpu.VMEM((4, 2, rows, d), BF)] * 2
+        + [dma((2,))] * 2
+        + Scatter.scratch(hosted, rows, d, False) * 2,
+        compiler_params=params(62, collective_id=5),
         name="feed_forward",
-    )(n2, gm, g1, g2, b1.reshape(planes, 1, hb), gates.reshape(nb, planes, hb).transpose(1, 0, 2))
-    return mlp, gn2, p1, p2, gb1.reshape(ff), gch.transpose(1, 0, 2).reshape(nb, ff)
+    )(n2, gm, b1.reshape(planes, 1, hb), gates.reshape(nb, planes, hb).transpose(1, 0, 2), g1, g2)
+    return mlp, gn2, o1, o2, p1, p2, gb1.reshape(ff), gch.transpose(1, 0, 2).reshape(nb, ff)
 
 
 def middle_back_kernel(
@@ -831,12 +1125,8 @@
     tg_ref,
     keep_ref,
     w_ref,
-    b2_ref,
-    router_ref,
-    gate1_ref,
-    shift2_ref,
-    scale2_ref,
-    gate2_ref,
+    vec_ref,
+    table_ref,
     head_ref,
     out_ref,
     ga_ref,
@@ -853,23 +1143,23 @@
     first = pl.program_id(0) == 0
     after = after_ref[...]
     cot = cot_ref[...]
-    gate2 = gate2_ref[0]
+    gate2 = table_ref[0, GATE2 : GATE2 + 1]
     tg = tg_ref[...]
     keep = keep_ref[...]
     normed, rstd = ln_parts(after)
-    scale2 = scale2_ref[0]
-    y = normed * (1.0 + scale2) + shift2_ref[0]
-    mlp_out = mlp_ref[...] + b2_ref[...]
+    scale2 = table_ref[0, SCALE2 : SCALE2 + 1]
+    y = normed * (1.0 + scale2) + table_ref[0, SHIFT2 : SHIFT2 + 1]
+    mlp_out = mlp_ref[...] + vec_ref[DOWN_BIAS : DOWN_BIAS + 1]
     open_gate = keep * tg
     out_ref[...] = after + (gate2 * open_gate) * mlp_out
     weighted = cot * mlp_out
     grad_tg = jnp.sum(weighted * gate2, axis=1, keepdims=True) * keep
     coef = grad_tg * tg * (1.0 - tg)
-    gy = gn2_ref[...] + coef * router_ref[...]
+    gy = gn2_ref[...] + coef * vec_ref[ROUTER : ROUTER + 1]
     ga = cot + ln_back(gy, normed, rstd, scale2)
     ga_ref[...] = ga
     attn = attn_ref[...]
-    g_attn = (ga * gate1_ref[0]).astype(BF)
+    g_attn = (ga * table_ref[0, GATE1 : GATE1 + 1]).astype(BF)
     mod_ref[0] = jnp.concatenate(
         [col_sum(ga * attn), col_sum(gy), col_sum(gy * normed), col_sum(weighted * open_gate)], axis=0
     )
@@ -906,7 +1196,7 @@
 
 
 def middle_back_call(
-    mlp, gn2, after, attn, cot, gm, gated, att, tg, keep, w, b2, router, gate1, shift2, scale2, gate2, head_rows, heads, blk
+    mlp, gn2, after, attn, cot, gm, gated, att, tg, keep, w, vecs, table, head_rows, heads, blk
 ):
     t, d = after.shape
     nb = t // blk
@@ -923,7 +1213,8 @@
             shape((nb * 2, 4, d)),
             shape((3, d)),
         ),
-        in_specs=[r] * 8 + [column, column, whole(d, d), whole(1, d), whole(1, d), v, v, v, v, v],
+        in_specs=[r] * 8 + [column, column, whole(d, d), whole(*vecs.shape)]
+        + [pl.BlockSpec((1,) + table.shape[1:], lambda i: (i, 0, 0)), v],
         out_specs=(
             r,
             r,
@@ -935,7 +1226,7 @@
         ),
         compiler_params=params(),
         name="middle_backward",
-    )(mlp, gn2, after, attn, cot, gm, gated, att, tg, keep, w, b2, router, gate1, shift2, scale2, gate2, head_rows)
+    )(mlp, gn2, after, attn, cot, gm, gated, att, tg, keep, w, vecs, table, head_rows)
 
 
 def qkv_weight_kernel(n1_ref, q_ref, k_ref, v_ref, gp_ref, out_ref, bias_ref, n1t):
@@ -977,14 +1268,14 @@
     return parts, bias.reshape(cuts, 3, width).transpose(1, 0, 2).reshape(3, d)
 
 
-def qkv_back_kernel(dqkv_ref, w_ref, tokens_ref, ga_ref, scale_ref, out_ref, mod_ref):
+def qkv_back_kernel(dqkv_ref, w_ref, tokens_ref, ga_ref, table_ref, out_ref, mod_ref):
     gy = dg(dqkv_ref[...], w_ref[...], NT)
     normed, rstd = ln_parts(tokens_ref[...])
-    out_ref[...] = ga_ref[...] + ln_back(gy, normed, rstd, scale_ref[0])
+    out_ref[...] = ga_ref[...] + ln_back(gy, normed, rstd, table_ref[0, SCALE1 : SCALE1 + 1])
     mod_ref[0] = jnp.concatenate([col_sum(gy), col_sum(gy * normed)], axis=0)
 
 
-def qkv_back_call(dqkv, w, tokens, ga, scale, blk):
+def qkv_back_call(dqkv, w, tokens, ga, table, blk):
     t, d = tokens.shape
     n = dqkv.shape[1]
     r = rows_of(blk, d)
@@ -992,61 +1283,116 @@
         qkv_back_kernel,
         grid=(t // blk,),
         out_shape=(shape((t, d)), shape((t // blk, 2, d))),
-        in_specs=[rows_of(blk, n), whole(d, n), r, r, row_vec(d)],
+        in_specs=[rows_of(blk, n), whole(d, n), r, r]
+        + [pl.BlockSpec((1,) + table.shape[1:], lambda i: (i, 0, 0))],
         out_specs=(r, pl.BlockSpec((1, 2, d), lambda i: (i, 0, 0))),
         compiler_params=params(),
         name="qkv_backward",
-    )(dqkv, w, tokens, ga, scale)
-
-
-def final_kernel(part_ref, sums_ref, mods_ref, out_ref, all_sums_ref, all_mods_ref, *rest, planes, cuts):
+    )(dqkv, w, tokens, ga, table)
+
+
+def final_kernel(
+    part_ref,
+    sums_ref,
+    mods_ref,
+    logits_ref,
+    conds_ref,
+    out_ref,
+    sum_ref,
+    ada_ref,
+    ada_bias_ref,
+    router_ref,
+    logit_ref,
+    all_sums,
+    all_mods,
+    all_logits,
+    mod_sems,
+    logit_sems,
+    *rest,
+    planes,
+    cuts,
+):
     place = Place(planes)
-    place.barrier(True)
+    mods = Exchange(place, mods_ref, all_mods, mod_sems, False)
+    logits = Exchange(place, logits_ref, all_logits, logit_sems, True)
+    mods.greet()
     width = out_ref.shape[1] // cuts
-    sums = Gather(place, sums_ref, all_sums_ref, *rest[:6])
-    mods = Gather(place, mods_ref, all_mods_ref, *rest[6:12])
-    rest = rest[12:]
+    sums = Gather(place, sums_ref, all_sums, *rest[:6])
+    rest = rest[6:]
     each = len(rest) // cuts
+
+    def source(m):
+        return lambda j, c: part_ref.at[m, :, lax.rem(place.z + 1 + j, planes), c]
+
     scatters = [
-        Scatter(
-            place,
-            part_ref.at[m],
-            out_ref.at[:, pl.ds(m * width, width)],
-            *rest[each * m : each * (m + 1)],
-        )
+        Scatter(place, m, list(range(planes)), source(m), *rest[each * m : each * (m + 1)])
         for m in range(cuts)
     ]
     steps = scatter_steps(scatters)
     parts = sums.parts()
     steps[0]()
     sums.run("begin")
-    mods.run("begin")
-    small = [functools.partial(g.run, part) for part in parts[1:-1] for g in (sums, mods)]
-    for step, group in zip(steps[1:-1], spread_out(small, len(steps) - 2)):
+    mods.start()
+    logits.start()
+
+    def products():
+        mods.arrive()
+        logits.arrive()
+        devices, rows, d = conds_ref.shape
+        conds = conds_ref[...].reshape(devices * rows, d)
+        got = all_mods[...].reshape(devices * rows, -1)
+        columns = ada_bias_ref.shape[1]
+        ada_ref[...] = dg(conds, got, TN)[:, :columns]
+        ada_bias_ref[...] = col_sum(got.astype(F32))[:, :columns]
+        got = all_logits[...].reshape(devices * rows, -1)
+        router_ref[...] = lax.dot_general(
+            conds.astype(F32), got, TN, precision=HIGHEST, preferred_element_type=F32
+        )
+        logit_ref[...] = col_sum(got)
+
+    small = [functools.partial(sums.run, part) for part in parts[1:-1]]
+    groups = spread_out(small, len(steps) - 1)
+    for i, (step, group) in enumerate(zip(steps[1:], groups)):
         step()
         for part in group:
             part()
-    steps[-1]()
+        if i == 2:
+            products()
     sums.run("end")
-    mods.run("end")
-
-
-def final_call(parts, sums, mods, planes):
-    cuts, _, rows, width = parts.shape
+    sum_ref[...] = jnp.sum(all_sums[...].reshape((8 * planes,) + sum_ref.shape), axis=0)
+    for m, s in enumerate(scatters):
+        out_ref[:, m * width : (m + 1) * width] = s.total()
+    mods.end()
+    logits.end()
+
+
+def final_call(parts, sums, mods, logits, conds, mod_width, planes):
+    cuts, devices, rows, width = parts.shape
+    d = conds.shape[2]
     spread = (4, planes, 2)
     return pl.pallas_call(
         functools.partial(final_kernel, planes=planes, cuts=cuts),
         out_shape=(
             shape((rows, cuts * width)),
-            shape(spread + sums.shape),
-            shape(spread + mods.shape, BF),
+            shape(sums.shape),
+            shape((d, mod_width)),
+            shape((1, mod_width)),
+            shape((d, logits.shape[1])),
+            shape((1, logits.shape[1])),
         ),
-        in_specs=[ANY_SPEC] * 3,
-        out_specs=(VMEM_SPEC, ANY_SPEC, ANY_SPEC),
-        scratch_shapes=Gather.scratch(planes) * 2 + Scatter.scratch(planes, rows, width) * cuts,
+        in_specs=[ANY_SPEC] + [VMEM_SPEC] * 4,
+        out_specs=(VMEM_SPEC,) * 6,
+        scratch_shapes=[
+            pltpu.VMEM(spread + sums.shape, F32),
+            pltpu.VMEM(mods.shape, BF),
+            pltpu.VMEM((devices,) + logits.shape, F32),
+        ]
+        + [Exchange.scratch(planes)] * 2
+        + Gather.scratch(planes)
+        + Scatter.scratch(planes, rows, width) * cuts,
         compiler_params=params(collective_id=4),
         name="attention_weight_sums",
-    )(parts.reshape((cuts,) + spread + (rows, width)), sums, mods)
+    )(parts.reshape((cuts,) + spread + (rows, width)), sums, mods, logits, conds)
 
 
 def on_device(
@@ -1095,8 +1441,6 @@
         return jnp.where(single, jnp.where(first, total, 0.0), blocks)
 
     devices = 8 * planes
-    me = lax.axis_index("narrow") * (2 * planes) + lax.axis_index("wide")
-
     def pack_rows(*blocks):
         return pad_rows(jnp.concatenate(blocks, axis=0))
 
@@ -1110,22 +1454,19 @@
 
     silu_cond = jax.nn.silu(conditioning.astype(F32)).astype(BF)
     shard = pack_rows(qkv_weight[:, :d], qkv_weight[:, d : 2 * d], qkv_weight[:, 2 * d :], proj_weight)
+    conds_pad = pad_rows(silu_cond.reshape(slots, -1, 128).transpose(1, 0, 2).reshape(-1, 128))
     g_attn, conds, mod_columns = prologue_call(
-        shard, pad_rows(silu_cond), ada_weight, ada_bias.astype(F32)[None], planes, slots
-    )
-    every_cond = conds.reshape((devices,) + conds.shape[3:])[:, :slots].reshape(devices * slots, d)
+        shard, conds_pad, ada_weight, ada_bias.astype(F32)[None], planes, slots
+    )
     mod_width = ada_bias.shape[0]
-    mod_columns = mod_columns.reshape((devices,) + mod_columns.shape[3:])
-    mod_columns = lax.dynamic_slice_in_dim(mod_columns, me * slots, slots, axis=1)
-    modulation = mod_columns[:, :, :mod_width].transpose(1, 0, 2).reshape(slots, devices * mod_width)
-    mod_rows = per_block(modulation.astype(F32)).reshape(slots, 6, 1, d)
-    shift1, scale1, gate1, shift2, scale2, gate2 = [mod_rows[:, k] for k in range(6)]
-    cond_float = silu_cond.astype(F32)
-
+    every_cond = conds[:, : slots * d // 128].reshape(devices, -1, slots, 128).transpose(0, 2, 1, 3)
+    every_cond = jnp.pad(
+        every_cond.reshape(devices, slots, d), ((0, 0), (0, up_to(slots, 16) - slots), (0, 0))
+    )
+    modulation = mod_columns[:, :slots, :mod_width].transpose(1, 0, 2).reshape(slots, 6, d)
+    table = per_block(modulation.astype(F32))
     def router(weight, bias, mask):
-        gate = jax.nn.sigmoid(
-            jnp.dot(cond_float, weight.astype(F32), precision=HIGHEST) + bias.astype(F32)
-        )
+        gate = jax.nn.sigmoid(dg(silu_cond, weight, NN) + bias.astype(F32))
         mask = mask.astype(F32)
         return mask * gate, mask * gate * (1.0 - gate)
 
@@ -1135,34 +1476,24 @@
     chan_rows = jnp.repeat(per_block(chan_gate), unit, axis=1)
     keep = (1.0 - skip_mask.astype(F32))[:, None]
 
-    qkv_bias = jnp.concatenate([query_bias, jnp.zeros_like(query_bias), value_bias])
-    n1, qkv, full_qkv, full_proj = qkv_call(
-        tokens,
-        shift1,
-        scale1,
-        g_attn.reshape((devices,) + shard.shape),
-        qkv_bias.astype(F32)[None],
-        blk,
-    )
-    att, gated, lse, g_up, g_down = attn_fwd(
-        off, head_rows, qkv, pack_piece(fc1_weight), pack_piece(fc2_weight), heads, blk, planes
-    )
-    router_row = token_router.astype(F32)[None]
-    attn, after, n2, gm, tg = middle_call(
-        gated,
-        full_proj,
-        proj_bias.astype(F32)[None],
+    vecs = jnp.concatenate([query_bias, value_bias, proj_bias, fc2_bias, token_router])
+    vecs = vecs.astype(F32).reshape(5, d)
+    lse, tg, n1, qkv, full_qkv, full_proj, att, gated, attn, after, n2, gm, g_up, g_down = forward_call(
+        off,
+        head_rows,
+        table,
+        vecs,
+        keep,
         tokens,
         cotangent,
-        keep,
-        router_row,
-        gate1,
-        shift2,
-        scale2,
-        gate2,
+        g_attn.reshape((devices,) + shard.shape),
+        pack_piece(fc1_weight),
+        pack_piece(fc2_weight),
+        heads,
         blk,
-    )
-    mlp, gn2, p_up, p_down, gb1, gch = mlp_call(
+        planes,
+    )
+    mlp, gn2, o_up, o_down, p_up, p_down, gb1, gch = mlp_call(
         n2, gm, g_up, g_down, fc1_bias.astype(F32), chan_rows, blk
     )
     output, ga, do, delta, g_proj, mods, sums = middle_back_call(
@@ -1177,12 +1508,8 @@
         tg,
         keep,
         full_proj,
-        fc2_bias.astype(F32)[None],
-        router_row,
-        gate1,
-        shift2,
-        scale2,
-        gate2,
+        vecs,
+        table,
         head_rows,
         heads,
         blk,
@@ -1190,34 +1517,32 @@
     mods = mods.reshape(slots, 8, d)
     dqkv, g_up, g_down = attn_bwd(off, qkv, do, lse, delta, p_up, p_down, heads, blk, planes)
     parts, qkv_sums = qkv_weight_call(n1, dqkv, g_proj, devices, 3)
-    grad_tokens, mods1 = qkv_back_call(dqkv, full_qkv, tokens, ga, scale1, blk)
+    grad_tokens, mods1 = qkv_back_call(dqkv, full_qkv, tokens, ga, table, blk)
     block_mods = jnp.concatenate(
         [mods1[:, 0], mods1[:, 1], mods[:, 0], mods[:, 1], mods[:, 2], mods[:, 3]], axis=1
     )
     grad_slot_mod = per_slot(block_mods).astype(BF)
     g_head = per_slot(jnp.sum(mods[:, 4].reshape(slots, heads, hd), axis=2)) * head_slope
     g_chan = per_slot(jnp.sum(gch.reshape(slots, groups, unit), axis=2)) * chan_slope
-    logits = jnp.concatenate([g_head, g_chan], axis=1)
-    vector = jnp.concatenate(
-        [qkv_sums[0], qkv_sums[2], sums[1], gb1, sums[2], sums[0], logits.reshape(-1)]
-    )
+    logits = jnp.pad(
+        jnp.concatenate([g_head, g_chan], axis=1),
+        ((0, up_to(slots, 16) - slots), (0, up_to(heads + groups, 128) - heads - groups)),
+    )
+    blocks = grad_slot_mod.reshape(slots, devices, mod_width).transpose(1, 0, 2)
+    blocks = jnp.pad(
+        blocks,
+        ((0, 0), (0, up_to(slots, 16) - slots), (0, up_to(mod_width, 128) - mod_width)),
+    )
+    vector = jnp.concatenate([qkv_sums[0], qkv_sums[2], sums[1], gb1, sums[2], sums[0]])
     length = vector.shape[0]
     vector = jnp.pad(vector, (0, up_to(length, 1024) - length)).reshape(-1, 128)
-    g_attn, all_sums, all_mods = final_call(
-        parts, vector, pad_rows(grad_slot_mod.reshape(-1, 128)), planes
+    g_attn, small, grad_ada_weight, grad_ada_bias, router_grads, logit_sums = final_call(
+        parts, vector, blocks, logits, every_cond, mod_width, planes
     )
     g_attn = g_attn[: 4 * (d // devices)].reshape(4, d // devices, d)
-    all_mods = all_mods.reshape(devices, -1)[:, : slots * 6 * d].reshape(devices * slots, 6 * d)
-    grad_mod_columns = lax.dynamic_slice_in_dim(all_mods, me * mod_width, mod_width, axis=1)
-    grad_ada_weight = dg(every_cond, grad_mod_columns, TN)
-    grad_ada_bias = jnp.sum(grad_mod_columns.astype(F32), axis=0)
-    all_sums = all_sums.reshape(devices, -1)
-    logits = all_sums[:, length - logits.size : length].reshape(devices * slots, heads + groups)
-    router_grads = lax.dot_general(
-        every_cond.astype(F32), logits, TN, precision=HIGHEST, preferred_element_type=F32
-    )
-    logit_sums = jnp.sum(logits, axis=0)
-    small = jnp.sum(all_sums[:, : length - slots * (heads + groups)], axis=0)
+    small = small.reshape(-1)[:length]
+    grad_ada_bias = grad_ada_bias[0]
+    logit_sums = logit_sums[0]
     ends = [d, 2 * d, 3 * d, 3 * d + hidden, 4 * d + hidden]
     g_query, g_value, g_proj_bias, g_b1, g_b2, g_router = jnp.split(small, ends)
     return (
@@ -1230,14 +1555,14 @@
         g_value,
         g_attn[3],
         g_proj_bias,
-        unpack_piece(g_up, fc1_weight.shape[0]),
+        unpack_piece(g_up + o_up, fc1_weight.shape[0]),
         g_b1,
-        unpack_piece(g_down, fc2_weight.shape[0]),
+        unpack_piece(g_down + o_down, fc2_weight.shape[0]),
         g_b2,
         router_grads[:, :heads],
         logit_sums[:heads],
-        router_grads[:, heads:],
-        logit_sums[heads:],
+        router_grads[:, heads : heads + groups],
+        logit_sums[heads : heads + groups],
         g_router,
     )
 

time: 624 us -> 551 us (0.88)
  Pallas kernels: 562 us -> 498 us
    pallas_call x1, Pallas kernels: 122 us -> 69.3 us  [attn_bwd(): pl.pallas_call(functools.partial(attn_bwd_kernel, heads=heads, blk=blk, p...]
    pallas_call x5 -> x3, Pallas kernels: 306 us -> 298 us  [the longest x1 131 us: mlp_call(): pl.pallas_call(functools.partial(mlp_kernel, blk=blk, planes=planes), gri...]
where the time goes in v3:
time: 551 us; the launch traced here: 543 us
  Pallas kernels  498 us (90%)
  local copies, waits for them, and re-layouts  31.7 us (6%)
  other arithmetic  9.67 us (2%)
    pallas_call x1, Pallas kernels, mlp_call(): pl.pallas_call(functools.partial(mlp_kernel, blk=blk, planes=planes), gri...  131 us
    pallas_call x1, Pallas kernels, forward_call(): pl.pallas_call(functools.partial(forward_kernel, heads=heads, blk=blk, pl...  98.8 us
    pallas_call x1, Pallas kernels, final_call(): pl.pallas_call(functools.partial(final_kernel, planes=planes, cuts=cuts),...  69.7 us
    pallas_call x1, Pallas kernels, attn_bwd(): pl.pallas_call(functools.partial(attn_bwd_kernel, heads=heads, blk=blk, p...  69.3 us
    pallas_call x1, Pallas kernels, prologue_call(): pl.pallas_call(functools.partial(prologue_kernel, planes=planes, slots=sl...  67.7 us
    pallas_call x1, Pallas kernels, middle_back_call(): pl.pallas_call(functools.partial(middle_back_kernel, heads=heads), grid=(...  27.9 us
    pallas_call x1, Pallas kernels, qkv_back_call(): pl.pallas_call(qkv_back_kernel, grid=(t // blk,), out_shape=(shape((t, d)...  18 us
    pallas_call x1, Pallas kernels, qkv_weight_call(): pl.pallas_call(qkv_weight_kernel, grid=(cuts,), out_shape=(shape((cuts, d...  15.9 us

profile of v3, /device:TPU:0, one launch (start us, length us, event | category | flops | bytes accessed | tf_op | source)
XLA Modules:
  0.0 543.0 jit_solution(1360917772723449106)
XLA Ops:
  0.8 1.1 fusion.18
  1.8 1.7 pad_maximum_fusion.shard_ref
  4.9 2.1 copy.83.ada_ref
  7.0 1.2 broadcast_in_dim.132
  8.2 67.7 %weights_and_modulation.1 = (bf16[4,4,2,144,1152]{4,3,2,1,0:T(8,128)(2,1)}, bf16[32,48,128]{2,1,0:T(8,128)(2,1)}, bf16[32,16,256]{2,1,0:T(8,128)(2,1)}) custom-call(bf16[144,1152]{1,0:T(8,128)(2,1)} %pad_maximum_fusion.shard_ref, bf16[48,128]{1,0:T(8,128)(2,1)} %pad.20.cond_ref, bf16[1152,216]{1,0:T(8,128)(2,1)} %copy.83.ada_ref, f32[1,216]{1,0:T(1,128)} %bitcast.105), custom_call_target="tpu_custom_call" | custom-call | tf_op jit(solution)/shard_map/weights_and_modulation/pallas_call | solution.py:556
  75.9 0.9 convert_bitcast_fusion
  79.2 0.9 convert_multiply_fusion.2
  80.9 1.0 copy.89.keep_ref
  84.3 1.0 reshape.161.up_ref
  85.7 1.0 reshape.163.down_ref
  86.8 98.8 %attention_and_middle_forward.1 = (f32[16,1024]{1,0:T(8,128)}, f32[1024,1]{1,0:T(8,128)}, bf16[1024,1152]{1,0:T(8,128)(2,1)}, bf16[1024,3456]{1,0:T(8,128)(2,1)}...) custom-call(f32[1]{0:T(128)} %bitcast.1.off_ref, ...), custom_call_target="tpu_custom_call" | custom-call | tf_op jit(solution)/shard_map/attention_and_middle_forward/pallas_call | solution.py:778
  187.3 131.1 %feed_forward.1 = (f32[1024,1152]{1,0:T(8,128)}, f32[1024,1152]{1,0:T(8,128)}, f32[4,1,1152]{2,1,0:T(1,128)}, f32[4,4,1152]{2,1,0:T(4,128)}, f32[144,1152]{1,0:T...) custom-call(bf16[1024,1152]{1,0:T(8,128)(2,1)} %get-tuple-element.65.n2_r, ...), custom_call_target="tpu_custom_call" | custom-call | tf_op jit(solution)/shard_map/feed_forward/pallas_call | solution.py:1088
  318.5 27.9 %middle_backward.1 = (f32[1024,1152]{1,0:T(8,128)}, f32[1024,1152]{1,0:T(8,128)}, bf16[1024,1152]{1,0:T(8,128)(2,1)}, f32[16,1024]{1,0:T(8,128)}, f32[1152,1152]...) custom-call(f32[1024,1152]{1,0:T(8,128)} %get-tuple-element.69.mlp_ref, f32[1024,1152]{1,0:T(8,128)} %get-tuple-element.70.gn2_ref, ...), custom_call_target="tpu_custom_call" | custom-call | tf_op jit(solution)/shard_map/middle_backward/pallas_call | solution.py:1204
  346.4 69.3 %attention_backward.1 = (bf16[1024,3456]{1,0:T(8,128)(2,1)}, f32[144,1152]{1,0:T(8,128)}, f32[144,1152]{1,0:T(8,128)}) custom-call(f32[1]{0:T(128)} %bitcast.1.off_ref, bf16[1024,3456]{1,0:T(8,128)(2,1)} %get-tuple-element.78.qkv_ref, bf16[1024,1152]{1,0:T(8,128)(2,1)} %get-tuple-element.79.do_ref, f32[16,1024]{1,0:T(8,128)} %get-tuple-element.80.lse_ref, ...), custom_call_target="tpu_custom_call" | custom-call | tf_op jit(solution)/shard_map/attention_backward/pallas_call | solution.py:912
  415.8 1.3 add.50
  417.7 1.2 copy.107
  419.6 1.2 copy.106
  422.7 18.0 %qkv_backward.1 = (f32[1024,1152]{1,0:T(8,128)}, f32[4,2,1152]{2,1,0:T(2,128)}) custom-call(bf16[1024,3456]{1,0:T(8,128)(2,1)} %get-tuple-element.84.dqkv_ref.q_ref.k_ref.v_ref, bf16[1152,3456]{1,0:T(8,128)(2,1)} %get-tuple-element.85.w_ref, f32[1024,1152]{1,0:T(8,128)} %tokens_ref.3, f32[1024,1152]{1,0:T(8,128)} %get-tuple-element.86.ga_ref, ...), custom_call_target="tpu_custom_call" | custom-call | tf_op jit(solution)/shard_map/qkv_backward/pallas_call | solution.py:1282
  443.6 15.9 %qkv_weight_gradient.1 = (bf16[3,32,144,384]{3,2,1,0:T(8,128)(2,1)}, f32[3,1,1152]{2,1,0:T(1,128)}) custom-call(bf16[1024,1152]{1,0:T(8,128)(2,1)} %get-tuple-element.88.n1_ref, bf16[1024,3456]{1,0:T(8,128)(2,1)} %get-tuple-element.84.dqkv_ref.q_ref.k_ref.v_ref, bf16[1024,3456]{1,0:T(8,128)(2,1)} %get-tuple-element.84.dqkv_ref.q_ref.k_ref.v_ref, ...), custom_call_target="tpu_custom_call" | custom-call | tf_op jit(solution)/shard_map/qkv_weight_gradient/pallas_call | solution.py:1255
  461.8 1.1 pad.24.conds_ref
  462.9 69.7 %attention_weight_sums.1 = (f32[144,1152]{1,0:T(8,128)}, f32[88,128]{1,0:T(8,128)}, f32[1152,216]{1,0:T(8,128)}, f32[1,216]{1,0:T(1,128)}, f32[1152,128]{1,0:T(8,128)}, /*index=5*/f32[1,128]{1,0:T(1,128)}) custom-call(bf16[3,4,4,2,144,384]{5,4,3,2,1,0:T(8,128)(2,1)} %bitcast.89, f32[88,128]{1,0:T(8,128)} %pad_bitcast_fusion.sums_ref, ...), custom_call_target="tpu_custom_call" | custom-call | tf_op jit(solution)/shard_map/attention_weight_sums/pallas_call | solution.py:1373
  532.6 1.2 slice.125
  535.0 1.3 copy.105
  537.4 1.6 slice.127
  (153 shorter events, 22.6 us)
Async XLA Ops:
  0.7 185.0 %copy-start = (bf16[1152,32]{0,1:T(8,128)(2,1)S(1)}, bf16[1152,32]{0,1:T(8,128)(2,1)}, u32[]{:S(2)}) copy-start(bf16[1152,32]{0,1:T(8,128)(2,1)} %param.42) | copy-start | bytes 221188
  0.7 80.2 %copy-start.21 = (s32[1024]{0:T(1024)S(1)}, s32[1024]{0:T(1024)}, u32[]{:S(2)}) copy-start(s32[1024]{0:T(1024)} %param.28) | copy-start | bytes 12292
  0.7 81.3 %copy-start.16 = (bf16[1152]{0:T(1024)(128)(2,1)S(1)}, bf16[1152]{0:T(1024)(128)(2,1)}, u32[]{:S(2)}) copy-start(bf16[1152]{0:T(1024)(128)(2,1)} %param.32) | copy-start | bytes 6916
  0.7 81.4 %copy-start.17 = (bf16[1152]{0:T(1024)(128)(2,1)S(1)}, bf16[1152]{0:T(1024)(128)(2,1)}, u32[]{:S(2)}) copy-start(bf16[1152]{0:T(1024)(128)(2,1)} %param.33) | copy-start | bytes 6916
  0.7 81.7 %copy-start.18 = (bf16[1152]{0:T(1024)(128)(2,1)S(1)}, bf16[1152]{0:T(1024)(128)(2,1)}, u32[]{:S(2)}) copy-start(bf16[1152]{0:T(1024)(128)(2,1)} %param.35) | copy-start | bytes 6916
  0.7 82.0 %copy-start.19 = (bf16[1152]{0:T(1024)(128)(2,1)S(1)}, bf16[1152]{0:T(1024)(128)(2,1)}, u32[]{:S(2)}) copy-start(bf16[1152]{0:T(1024)(128)(2,1)} %param.39) | copy-start | bytes 6916
  0.7 82.2 %copy-start.20 = (bf16[1152]{0:T(1024)(128)(2,1)S(1)}, bf16[1152]{0:T(1024)(128)(2,1)}, u32[]{:S(2)}) copy-start(bf16[1152]{0:T(1024)(128)(2,1)} %param.44) | copy-start | bytes 6916
  0.7 83.1 %copy-start.7 = (bf16[576,288]{0,1:T(8,128)(2,1)S(1)}, bf16[576,288]{0,1:T(8,128)(2,1)}, u32[]{:S(2)}) copy-start(bf16[576,288]{0,1:T(8,128)(2,1)} %param.36) | copy-start | bytes 995332
  0.7 84.6 %copy-start.8 = (bf16[576,288]{0,1:T(8,128)(2,1)S(1)}, bf16[576,288]{0,1:T(8,128)(2,1)}, u32[]{:S(2)}) copy-start(bf16[576,288]{0,1:T(8,128)(2,1)} %param.38) | copy-start | bytes 995332
  86.8 98.8 %copy-start.24 = (bf16[32]{0:T(256)(128)(2,1)S(1)}, bf16[32]{0:T(256)(128)(2,1)}, u32[]{:S(2)}) copy-start(bf16[32]{0:T(256)(128)(2,1)} %param.43) | copy-start | bytes 196
  86.8 98.9 %copy-start.23 = (s32[4,32]{1,0:T(4,128)S(1)}, s32[4,32]{1,0:T(4,128)}, u32[]{:S(2)}) copy-start(s32[4,32]{1,0:T(4,128)} %param.27) | copy-start | bytes 1540
  86.8 99.9 %copy-start.15 = (bf16[4608]{0:T(1024)(128)(2,1)S(1)}, bf16[4608]{0:T(1024)(128)(2,1)}, u32[]{:S(2)}) copy-start(bf16[4608]{0:T(1024)(128)(2,1)} %param.37) | copy-start | bytes 27652
  346.4 69.3 %copy-start.5 = (f32[144,1152]{1,0:T(8,128)S(1)}, f32[144,1152]{1,0:T(8,128)}, u32[]{:S(2)}) copy-start(f32[144,1152]{1,0:T(8,128)} %get-tuple-element.105) | copy-start | bytes 1990660
  415.7 3.1 copy-start.4
  415.7 3.1 copy-start.6
  417.7 3.7 copy-start.9
  443.6 16.8 %copy-start.14 = (f32[3,1152]{1,0:T(4,128)S(1)}, f32[3,1152]{1,0:T(4,128)}, u32[]{:S(2)}) copy-start(f32[3,1152]{1,0:T(4,128)} %get-tuple-element.92) | copy-start | bytes 41476
  443.6 16.9 %copy-start.13 = (f32[4,1,1152]{2,1,0:T(1,128)S(1)}, f32[4,1,1152]{2,1,0:T(1,128)}, u32[]{:S(2)}) copy-start(f32[4,1,1152]{2,1,0:T(1,128)} %get-tuple-element.93) | copy-start | bytes 55300
  443.6 17.6 %copy-start.10 = (bf16[32,48,128]{2,1,0:T(8,128)(2,1)S(1)}, bf16[32,48,128]{2,1,0:T(8,128)(2,1)}, u32[]{:S(2)}) copy-start(bf16[32,48,128]{2,1,0:T(8,128)(2,1)} %get-tuple-element.97) | copy-start | bytes 1179652
  532.6 3.8 copy-start.2
  533.8 9.0 %copy-start.1 = (bf16[1152,32]{0,1:T(8,128)(2,1)S(1)}, bf16[1152,32]{0,1:T(8,128)(2,1)}, u32[]{:S(2)}) copy-start(bf16[1152,32]{0,1:T(8,128)(2,1)} %param.42) | copy-start | bytes 221188
  533.9 6.0 %copy-start.12 = (f32[88,128]{1,0:T(8,128)S(1)}, f32[88,128]{1,0:T(8,128)}, u32[]{:S(2)}) copy-start(f32[88,128]{1,0:T(8,128)} %get-tuple-element.101) | copy-start | bytes 135172
  533.9 7.3 %copy-start.25 = (f32[1,128]{1,0:T(1,128)S(1)}, f32[1,128]{1,0:T(1,128)}, u32[]{:S(2)}) copy-start(f32[1,128]{1,0:T(1,128)} %get-tuple-element.107) | copy-start | bytes 1540
  533.9 8.3 %copy-start.22 = (f32[1,216]{1,0:T(1,128)S(1)}, f32[1,216]{1,0:T(1,128)}, u32[]{:S(2)}) copy-start(f32[1,216]{1,0:T(1,128)} %get-tuple-element.99) | copy-start | bytes 2596
  (2 other events, 5.6 us)

commit v4 on v3

--- a/solution.py
+++ b/solution.py
@@ -141,6 +141,13 @@
 
     def has(self, step):
         return self.z + step >= 0 if step < 0 else self.z + step < self.planes
+
+
+def plane_turn(planes, j):
+    order = sorted(range(1, planes), key=lambda k: (-min(k, planes - k), k)) + [0]
+    if isinstance(j, int):
+        return order[j]
+    return sum(jnp.where(j == i, k, 0) for i, k in enumerate(order))
 
 
 def remote(src, dst, sems, idx, device):
@@ -282,7 +289,7 @@
         self.own_sem, self.s1, self.s2, self.s3, self.s4 = own_sem, s1, s2, s3, s4
 
     def owner(self, j):
-        return lax.rem(self.p.z + 1 + j, self.p.planes)
+        return lax.rem(self.p.z + plane_turn(self.p.planes, j), self.p.planes)
 
     def moves_on(self, j):
         return j + 1 < self.p.planes
@@ -339,7 +346,7 @@
         side, other = self.sides(j)
 
         def add(n, value):
-            self.r1[i, n] = (self.r1[i, n].astype(F32) + value.astype(F32)).astype(BF)
+            self.r1[i, n] = self.r1[i, n] + value
 
         if stage == 1:
             if self.own is None:
@@ -391,13 +398,13 @@
         ]
 
 
-def scatter_steps(scatters, window=2):
+def scatter_steps(scatters, span=2, window=2):
     js = scatters[0].js
     units = range(len(scatters))
     queue = [(u, j) for j in js for u in units]
     x_items, y_items = [], []
-    for i in range(0, len(js), 2):
-        pair = [(u, j) for j in js[i : i + 2] for u in units]
+    for i in range(0, len(js), span):
+        pair = [(u, j) for j in js[i : i + span] for u in units]
         for stage in (2, 3):
             for u, j in pair:
                 first = scatters[u].x_first(j)
@@ -702,7 +709,7 @@
         rows = slice(i * blk, (i + 1) * blk)
         normed, _ = ln_parts(tok_s[rows, :])
         low = (normed * (1.0 + mod(i, SCALE1)) + mod(i, SHIFT1)).astype(BF)
-        n1_s[rows, :] = low
+        n1_s[:, rows] = low.T
         qkv_s[rows, :] = (dg(low, w_s[...], NN) + bias).astype(BF)
         run_group(i)
     moves["n1"].start()
@@ -780,7 +787,7 @@
         out_shape=(
             shape((heads, t)),
             shape((t, 1)),
-            shape((t, d), BF),
+            shape((d, t), BF),
             shape((t, 3 * d), BF),
             shape((d, 3 * d), BF),
             shape((d, d), BF),
@@ -801,7 +808,7 @@
             pltpu.VMEM((t, d), F32),
             pltpu.VMEM((d, 3 * d), BF),
             pltpu.VMEM((d, d), BF),
-            pltpu.VMEM((t, d), BF),
+            pltpu.VMEM((d, t), BF),
             pltpu.VMEM((t, 3 * d), BF),
             pltpu.VMEM((t, d), F32),
             pltpu.VMEM((t, d), BF),
@@ -817,49 +824,84 @@
     )(off, gate_rows, mods, vecs, keep, tokens, cot, g, up, down)
 
 
-def attn_bwd_kernel(
+def backward_kernel(
     off_ref,
     qkv_ref,
     do_ref,
     lse_ref,
     delta_ref,
+    n1t_ref,
+    gp_ref,
     up_ref,
     down_ref,
     dqkv_ref,
+    bias_ref,
     g_up_ref,
     g_down_ref,
+    done_ref,
+    part_ref,
     kt_sc,
     dqt_sc,
+    part_sem,
     *rest,
     heads,
     blk,
     planes,
+    cuts,
 ):
-    place = Place(planes)
-    place.barrier(True)
-    half = len(rest) // 2
-    first = planes // 2
-
-    def source(ref):
-        return lambda j, c: ref.at[:, j - first, c]
-
-    js = list(range(first, planes))
-    scatters = [
-        Scatter(place, 0, js, source(up_ref), *rest[:half]),
-        Scatter(place, 1, js, source(down_ref), *rest[half:]),
-    ]
-    steps = scatter_steps(scatters)
-    steps[0]()
-    groups = spread_out(steps[1:], heads)
     t, d = do_ref.shape
     hd = d // heads
     nb = t // blk
     scale = hd**-0.5
     c = scale * LOG2E
+    width = d // cuts
+    devices = 8 * planes
+    r = d // devices
+    first = planes // 2
+    place = Place(planes)
+    place.barrier(True)
+    slots, rest = rest[: cuts - 1], rest[cuts - 1 :]
+    each = 10
+    js = list(range(first, planes))
+
+    def kept(ref):
+        return lambda j, c: ref.at[:, j - first, c]
+
+    def local(ref):
+        return lambda j, c: ref.at[:, lax.rem(place.z + plane_turn(planes, j), planes), c]
+
+    ups = [
+        Scatter(place, u, js, kept(ref), *rest[each * u : each * (u + 1)])
+        for u, ref in enumerate((up_ref, down_ref))
+    ]
+    rest = rest[2 * each :]
+    each -= 1
+    chains = [
+        Scatter(
+            place, m, list(range(planes)), local(slots[m]), None, *rest[each * m : each * (m + 1)]
+        )
+        for m in range(cuts - 1)
+    ]
+    up_steps = scatter_steps(ups)
+    chain_steps = [scatter_steps([chain], planes) for chain in chains]
+    up_steps[0]()
+    ends = [-(-width * (m + 1) // hd) for m in range(cuts)]
+    queues = [[] for _ in range(heads + 1)]
+
+    def place_steps(steps, start, first, stop):
+        queues[start] += steps[:2]
+        for i, step in enumerate(steps[2:]):
+            queues[first + i * (stop - first) // max(len(steps) - 3, 1)].append(step)
+
+    place_steps(up_steps[1:], 0, ends[0] + 1, ends[1] + 1)
+    for m in range(cuts - 1):
+        steps = chain_steps[m][1:]
+        place_steps(steps, ends[m], min(ends[m] + 4 - m, heads), min(ends[m] + 7, heads))
+
     off = off_ref[0]
     kt_sc[...] = qkv_ref[:, d : 2 * d].T
 
-    def body(h, carry):
+    def body(h, carry, start, end):
         a, mask = head_window(h, hd, d)
         cols = pl.ds(a, WINDOW)
         key_cols = pl.ds(pl.multiple_of(d + a, 128), WINDOW)
@@ -883,10 +925,10 @@
             ps = []
             ds = []
             for j in range(nb):
-                part = slice(j * blk, (j + 1) * blk)
-                p = jnp.exp2(s_t[part] * c - (lse if j == i else lse - off))
+                cut = slice(j * blk, (j + 1) * blk)
+                p = jnp.exp2(s_t[cut] * c - (lse if j == i else lse - off))
                 ps.append(p.astype(BF))
-                ds.append((p * (dp_t[part] - delta)).astype(BF))
+                ds.append((p * (dp_t[cut] - delta)).astype(BF))
             p = jnp.concatenate(ps, axis=0)
             grad_s = jnp.concatenate(ds, axis=0)
             dv = dg(p, do, NN)
@@ -898,27 +940,71 @@
         dqkv_ref[:, key_cols] = jnp.where(mask, dk, dqkv_ref[:, key_cols])
         dqkv_ref[:, value_cols] = jnp.where(mask, dv_sum.astype(BF), dqkv_ref[:, value_cols])
         dqkv_ref[:, cols] = jnp.where(mask, dqt_sc[...].T, dqkv_ref[:, cols])
-        run_at(h, groups)
+        run_at(h - start, queues[start:end])
         return carry
 
-    lax.fori_loop(0, heads, body, 0)
-    g_up_ref[...] = scatters[0].total()
-    g_down_ref[...] = scatters[1].total()
-
-
-def attn_bwd(off, qkv, do, lse, delta, up, down, heads, blk, planes):
+    def weight_part(m, out):
+        dqkv = jnp.concatenate(
+            [dqkv_ref[:, b * d + m * width : b * d + (m + 1) * width] for b in range(3)], axis=1
+        )
+        bias_ref[m] = col_sum(dqkv.astype(F32))
+        grad = dg(n1t_ref[...], dqkv, NN).astype(BF)
+        for i in range(devices):
+            rows = slice(i * r, (i + 1) * r)
+            at = (i // (2 * planes), i // 2 % planes, i % 2)
+            for b in range(3):
+                out[at + (slice(b * r, (b + 1) * r),)] = grad[rows, b * width : (b + 1) * width]
+            out[at + (slice(3 * r, 4 * r),)] = gp_ref[rows, m * width : (m + 1) * width]
+
+    for m in range(cuts):
+        start = 0 if m == 0 else ends[m - 1]
+        lax.fori_loop(start, ends[m], functools.partial(body, start=start, end=ends[m]), 0)
+        if m + 1 < cuts:
+            weight_part(m, slots[m])
+            chain_steps[m][0]()
+    for j in chains[0].js:
+        chains[0].sent(1, j)
+    weight_part(cuts - 1, slots[0])
+    keep = pltpu.make_async_copy(slots[0], part_ref, part_sem)
+    keep.start()
+    for step in queues[heads]:
+        step()
+    g_up_ref[...] = ups[0].total()
+    g_down_ref[...] = ups[1].total()
+    for m, chain in enumerate(chains):
+        stages = (2, 3, 4) if m == 0 else (1, 2, 3, 4)
+        done_ref[:, m * width : (m + 1) * width] = chain.total(stages)
+    keep.wait()
+
+
+def backward_call(off, qkv, do, lse, delta, n1t, g_proj, up, down, heads, blk, planes, cuts):
     t, d = do.shape
     rows, cols = up.shape[3:]
+    width = d // cuts
+    part = (4, planes, 2, up_to(4 * d // (8 * planes), 16), width)
     return pl.pallas_call(
-        functools.partial(attn_bwd_kernel, heads=heads, blk=blk, planes=planes),
-        out_shape=(shape((t, 3 * d), BF), shape((rows, cols)), shape((rows, cols))),
-        in_specs=[SMEM_SPEC] + [VMEM_SPEC] * 4 + [ANY_SPEC] * 2,
-        out_specs=(VMEM_SPEC,) * 3,
-        scratch_shapes=[pltpu.VMEM((d, t), BF), pltpu.VMEM((WINDOW, t), BF)]
-        + Scatter.scratch(planes - planes // 2, rows, cols) * 2,
-        compiler_params=params(collective_id=3),
+        functools.partial(backward_kernel, heads=heads, blk=blk, planes=planes, cuts=cuts),
+        out_shape=(
+            shape((t, 3 * d), BF),
+            shape((cuts, 1, 3 * width)),
+            shape((rows, cols)),
+            shape((rows, cols)),
+            shape((part[3], (cuts - 1) * width)),
+            shape(part, BF),
+        ),
+        in_specs=[SMEM_SPEC] + [VMEM_SPEC] * 6 + [ANY_SPEC] * 2,
+        out_specs=(VMEM_SPEC,) * 5 + (ANY_SPEC,),
+        scratch_shapes=[
+            pltpu.VMEM((d, t), BF),
+            pltpu.VMEM((WINDOW, t), BF),
+            pltpu.SemaphoreType.DMA(()),
+        ]
+        + [pltpu.VMEM(part, BF)] * (cuts - 1)
+        + Scatter.scratch(planes - planes // 2, rows, cols) * 2
+        + Scatter.scratch(planes, part[3], width, False) * (cuts - 1),
+        compiler_params=params(63, collective_id=3),
         name="attention_backward",
-    )(off, qkv, do, lse, delta, up, down)
+    )(off, qkv, do, lse, delta, n1t, g_proj, up, down)
 
 
 def mlp_kernel(
@@ -965,7 +1051,7 @@
     ]
 
     def loads(step):
-        plane = lax.rem(place.z + 1 + step, planes)
+        plane = lax.rem(place.z + plane_turn(planes, step), planes)
         return [
             pltpu.make_async_copy(g.at[:, plane], slot, g_sems.at[i])
             for i, (g, slot) in enumerate(((g1_ref, g1_s), (g2_ref, g2_s)))
@@ -1079,7 +1165,7 @@
     hosted = planes // 2
 
     def turn(j):
-        return lax.rem(lax.axis_index("wide") // 2 + 1 + j, planes)
+        return lax.rem(lax.axis_index("wide") // 2 + plane_turn(planes, j), planes)
 
     b_spec = pl.BlockSpec((1, 1, hb), lambda j: (turn(j), 0, 0))
     c_spec = pl.BlockSpec((1, nb, hb), lambda j: (turn(j), 0, 0))
@@ -1135,6 +1221,7 @@
     gw_ref,
     mod_ref,
     sums_ref,
+    gw_s,
     *,
     heads,
 ):
@@ -1187,12 +1274,16 @@
     @pl.when(first)
     def _():
         sums_ref[...] = sums
-        gw_ref[...] = gw
+        gw_s[...] = gw
 
     @pl.when(jnp.logical_not(first))
     def _():
         sums_ref[...] += sums
-        gw_ref[...] += gw
+        gw_s[...] += gw
+
+    @pl.when(pl.program_id(0) == pl.num_programs(0) - 1)
+    def _():
+        gw_ref[...] = gw_s[...].astype(BF)
 
 
 def middle_back_call(
@@ -1209,7 +1300,7 @@
             shape((t, d)),
             shape((t, d), BF),
             shape((heads, t)),
-            shape((d, d)),
+            shape((d, d), BF),
             shape((nb * 2, 4, d)),
             shape((3, d)),
         ),
@@ -1224,121 +1315,110 @@
             pl.BlockSpec((2, 4, d), lambda i: (i, 0, 0)),
             whole(3, d),
         ),
+        scratch_shapes=[pltpu.VMEM((d, d), F32)],
         compiler_params=params(),
         name="middle_backward",
     )(mlp, gn2, after, attn, cot, gm, gated, att, tg, keep, w, vecs, table, head_rows)
 
 
-def qkv_weight_kernel(n1_ref, q_ref, k_ref, v_ref, gp_ref, out_ref, bias_ref, n1t):
-    @pl.when(pl.program_id(0) == 0)
-    def _():
-        n1t[...] = n1_ref[...].T
-
-    width = q_ref.shape[1]
-    devices = out_ref.shape[1]
-    r = n1_ref.shape[1] // devices
-    dqkv = jnp.concatenate([q_ref[...], k_ref[...], v_ref[...]], axis=1)
-    grad = dg(n1t[...], dqkv, NN).astype(BF)
-    bias_ref[0] = col_sum(dqkv.astype(F32))
-    for i in range(devices):
-        rows = slice(i * r, (i + 1) * r)
-        for b in range(3):
-            out_ref[0, i, b * r : (b + 1) * r, :] = grad[rows, b * width : (b + 1) * width]
-        out_ref[0, i, 3 * r : 4 * r, :] = gp_ref[rows, :].astype(BF)
-
-
-def qkv_weight_call(n1, dqkv, g_proj, devices, cuts):
-    t, d = n1.shape
-    width = d // cuts
-    rows = up_to(4 * d // devices, 16)
-    third = [pl.BlockSpec((t, width), lambda j, b=b: (0, b * cuts + j)) for b in range(3)]
-    parts, bias = pl.pallas_call(
-        qkv_weight_kernel,
-        grid=(cuts,),
-        out_shape=(shape((cuts, devices, rows, width), BF), shape((cuts, 1, 3 * width))),
-        in_specs=[whole(t, d)] + third + [pl.BlockSpec((d, width), lambda j: (0, j))],
-        out_specs=(
-            pl.BlockSpec((1, devices, rows, width), lambda j: (j, 0, 0, 0)),
-            pl.BlockSpec((1, 1, 3 * width), lambda j: (j, 0, 0)),
-        ),
-        scratch_shapes=[pltpu.VMEM((d, t), BF)],
-        compiler_params=params(),
-        name="qkv_weight_gradient",
-    )(n1, dqkv, dqkv, dqkv, g_proj)
-    return parts, bias.reshape(cuts, 3, width).transpose(1, 0, 2).reshape(3, d)
-
-
-def qkv_back_kernel(dqkv_ref, w_ref, tokens_ref, ga_ref, table_ref, out_ref, mod_ref):
-    gy = dg(dqkv_ref[...], w_ref[...], NT)
-    normed, rstd = ln_parts(tokens_ref[...])
-    out_ref[...] = ga_ref[...] + ln_back(gy, normed, rstd, table_ref[0, SCALE1 : SCALE1 + 1])
-    mod_ref[0] = jnp.concatenate([col_sum(gy), col_sum(gy * normed)], axis=0)
-
-
-def qkv_back_call(dqkv, w, tokens, ga, table, blk):
-    t, d = tokens.shape
-    n = dqkv.shape[1]
-    r = rows_of(blk, d)
-    return pl.pallas_call(
-        qkv_back_kernel,
-        grid=(t // blk,),
-        out_shape=(shape((t, d)), shape((t // blk, 2, d))),
-        in_specs=[rows_of(blk, n), whole(d, n), r, r]
-        + [pl.BlockSpec((1,) + table.shape[1:], lambda i: (i, 0, 0))],
-        out_specs=(r, pl.BlockSpec((1, 2, d), lambda i: (i, 0, 0))),
-        compiler_params=params(),
-        name="qkv_backward",
-    )(dqkv, w, tokens, ga, table)
-
-
 def final_kernel(
-    part_ref,
+    single_ref,
+    table_ref,
+    mods_ref,
     sums_ref,
-    mods_ref,
     logits_ref,
     conds_ref,
+    part_ref,
+    dqkv_ref,
+    w_ref,
+    tokens_ref,
+    ga_ref,
     out_ref,
     sum_ref,
     ada_ref,
     ada_bias_ref,
     router_ref,
     logit_ref,
+    grad_ref,
     all_sums,
+    own_mods,
     all_mods,
     all_logits,
+    w_s,
+    dq_s,
+    tok_s,
+    ga_s,
+    w_sem,
+    in_sems,
+    out_slots,
+    out_sems,
     mod_sems,
     logit_sems,
     *rest,
     planes,
-    cuts,
+    blk,
 ):
     place = Place(planes)
-    mods = Exchange(place, mods_ref, all_mods, mod_sems, False)
+    mods = Exchange(place, own_mods, all_mods, mod_sems, False)
     logits = Exchange(place, logits_ref, all_logits, logit_sems, True)
+
+    def source(j, c):
+        return part_ref.at[:, lax.rem(place.z + plane_turn(planes, j), planes), c]
+
+    sums = Gather(place, sums_ref, all_sums, *rest[:6])
+    chain = Scatter(place, 0, list(range(planes)), source, *rest[6:])
+    t, d = tokens_ref.shape
+    nb = t // blk
+    w_load = pltpu.make_async_copy(w_ref, w_s, w_sem)
+
+    def loads(i):
+        rows = pl.ds(i * blk, blk)
+        return [
+            pltpu.make_async_copy(src.at[rows], dst.at[i % 2], in_sems.at[k, i % 2])
+            for k, (src, dst) in enumerate(((dqkv_ref, dq_s), (tokens_ref, tok_s), (ga_ref, ga_s)))
+        ]
+
+    w_load.start()
+    for copy in loads(0) + loads(1):
+        copy.start()
     mods.greet()
-    width = out_ref.shape[1] // cuts
-    sums = Gather(place, sums_ref, all_sums, *rest[:6])
-    rest = rest[6:]
-    each = len(rest) // cuts
-
-    def source(m):
-        return lambda j, c: part_ref.at[m, :, lax.rem(place.z + 1 + j, planes), c]
-
-    scatters = [
-        Scatter(place, m, list(range(planes)), source(m), *rest[each * m : each * (m + 1)])
-        for m in range(cuts)
-    ]
-    steps = scatter_steps(scatters)
-    parts = sums.parts()
+    steps = scatter_steps([chain], planes)
     steps[0]()
     sums.run("begin")
-    mods.start()
     logits.start()
+    own_mods[...] = jnp.zeros_like(own_mods)
+    out = Stream(out_slots, out_sems, grad_ref)
+    tables = []
+
+    def block(i):
+        if i == 0:
+            w_load.wait()
+        for copy in loads(i):
+            copy.wait()
+        gy = dg(dq_s[i % 2], w_s[...], NT)
+        normed, rstd = ln_parts(tok_s[i % 2])
+        out.put(ga_s[i % 2] + ln_back(gy, normed, rstd, table_ref[i, SCALE1 : SCALE1 + 1]))
+        tables.append([col_sum(gy), col_sum(gy * normed)] + [mods_ref[i, k : k + 1] for k in range(4)])
+        if i + 2 < nb:
+            for copy in loads(i + 2):
+                copy.start()
+
+    def exchange():
+        single = single_ref[0]
+        devices = own_mods.shape[0]
+        width = ada_bias_ref.shape[1]
+        flat = [jnp.concatenate(row, axis=1) for row in tables]
+        rows = [(1.0 - single) * row for row in flat]
+        rows[0] = flat[0] + single * functools.reduce(jnp.add, flat[1:])
+        every = jnp.concatenate(rows, axis=0).astype(BF)
+        for i in range(devices):
+            own_mods[i, :nb, :width] = every[:, i * width : (i + 1) * width]
+        mods.start()
 
     def products():
         mods.arrive()
         logits.arrive()
-        devices, rows, d = conds_ref.shape
+        devices, rows, _ = conds_ref.shape
         conds = conds_ref[...].reshape(devices * rows, d)
         got = all_mods[...].reshape(devices * rows, -1)
         columns = ada_bias_ref.shape[1]
@@ -1350,49 +1430,69 @@
         )
         logit_ref[...] = col_sum(got)
 
-    small = [functools.partial(sums.run, part) for part in parts[1:-1]]
-    groups = spread_out(small, len(steps) - 1)
-    for i, (step, group) in enumerate(zip(steps[1:], groups)):
-        step()
+    parts = [functools.partial(sums.run, part) for part in sums.parts()[1:-1]]
+    rest = steps[3:]
+    work = [
+        [functools.partial(block, 0)],
+        steps[1:3],
+        [functools.partial(block, i) for i in range(1, nb - 1)],
+        rest[:1],
+        [functools.partial(block, nb - 1), exchange],
+        rest[1:],
+    ]
+    work = [do for group in work for do in group]
+    for do, group in zip(work, spread_out(parts, len(work))):
+        do()
         for part in group:
             part()
-        if i == 2:
-            products()
+    products()
     sums.run("end")
     sum_ref[...] = jnp.sum(all_sums[...].reshape((8 * planes,) + sum_ref.shape), axis=0)
-    for m, s in enumerate(scatters):
-        out_ref[:, m * width : (m + 1) * width] = s.total()
+    out_ref[...] = chain.total()
+    out.end()
     mods.end()
     logits.end()
 
 
-def final_call(parts, sums, mods, logits, conds, mod_width, planes):
-    cuts, devices, rows, width = parts.shape
-    d = conds.shape[2]
+def final_call(single, table, mods, sums, logits, conds, part, dqkv, w, tokens, ga, mod_width, planes, blk):
+    rows, width = part.shape[3:]
+    t, d = tokens.shape
+    devices = 8 * planes
     spread = (4, planes, 2)
+    blocks = (devices, conds.shape[1], up_to(mod_width, 128))
+    dma = pltpu.SemaphoreType.DMA
     return pl.pallas_call(
-        functools.partial(final_kernel, planes=planes, cuts=cuts),
+        functools.partial(final_kernel, planes=planes, blk=blk),
         out_shape=(
-            shape((rows, cuts * width)),
+            shape((rows, width)),
             shape(sums.shape),
             shape((d, mod_width)),
             shape((1, mod_width)),
             shape((d, logits.shape[1])),
             shape((1, logits.shape[1])),
+            shape((t, d)),
         ),
-        in_specs=[ANY_SPEC] + [VMEM_SPEC] * 4,
-        out_specs=(VMEM_SPEC,) * 6,
+        in_specs=[SMEM_SPEC] + [VMEM_SPEC] * 5 + [ANY_SPEC] * 5,
+        out_specs=(VMEM_SPEC,) * 6 + (ANY_SPEC,),
         scratch_shapes=[
             pltpu.VMEM(spread + sums.shape, F32),
-            pltpu.VMEM(mods.shape, BF),
+            pltpu.VMEM(blocks, BF),
+            pltpu.VMEM(blocks, BF),
             pltpu.VMEM((devices,) + logits.shape, F32),
+            pltpu.VMEM(w.shape, BF),
+            pltpu.VMEM((2, blk, 3 * d), BF),
+            pltpu.VMEM((2, blk, d), F32),
+            pltpu.VMEM((2, blk, d), F32),
+            dma(()),
+            dma((3, 2)),
         ]
+        + Stream.scratch(blk, d, F32)
         + [Exchange.scratch(planes)] * 2
         + Gather.scratch(planes)
-        + Scatter.scratch(planes, rows, width) * cuts,
+        + Scatter.scratch(planes, rows, width),
         compiler_params=params(collective_id=4),
-        name="attention_weight_sums",
-    )(parts.reshape((cuts,) + spread + (rows, width)), sums, mods, logits, conds)
+        name="last_sums",
+    )(single, table, mods, sums, logits, conds, part, dqkv, w, tokens, ga)
 
 
 def on_device(
@@ -1478,7 +1578,7 @@
 
     vecs = jnp.concatenate([query_bias, value_bias, proj_bias, fc2_bias, token_router])
     vecs = vecs.astype(F32).reshape(5, d)
-    lse, tg, n1, qkv, full_qkv, full_proj, att, gated, attn, after, n2, gm, g_up, g_down = forward_call(
+    lse, tg, n1t, qkv, full_qkv, full_proj, att, gated, attn, after, n2, gm, g_up, g_down = forward_call(
         off,
         head_rows,
         table,
@@ -1515,30 +1615,36 @@
         blk,
     )
     mods = mods.reshape(slots, 8, d)
-    dqkv, g_up, g_down = attn_bwd(off, qkv, do, lse, delta, p_up, p_down, heads, blk, planes)
-    parts, qkv_sums = qkv_weight_call(n1, dqkv, g_proj, devices, 3)
-    grad_tokens, mods1 = qkv_back_call(dqkv, full_qkv, tokens, ga, table, blk)
-    block_mods = jnp.concatenate(
-        [mods1[:, 0], mods1[:, 1], mods[:, 0], mods[:, 1], mods[:, 2], mods[:, 3]], axis=1
+    dqkv, qkv_sums, g_up, g_down, g_done, part = backward_call(
+        off, qkv, do, lse, delta, n1t, g_proj, p_up, p_down, heads, blk, planes, 3
     )
-    grad_slot_mod = per_slot(block_mods).astype(BF)
+    qkv_sums = qkv_sums.reshape(3, 3, d // 3).transpose(1, 0, 2).reshape(3, d)
     g_head = per_slot(jnp.sum(mods[:, 4].reshape(slots, heads, hd), axis=2)) * head_slope
     g_chan = per_slot(jnp.sum(gch.reshape(slots, groups, unit), axis=2)) * chan_slope
     logits = jnp.pad(
         jnp.concatenate([g_head, g_chan], axis=1),
         ((0, up_to(slots, 16) - slots), (0, up_to(heads + groups, 128) - heads - groups)),
     )
-    blocks = grad_slot_mod.reshape(slots, devices, mod_width).transpose(1, 0, 2)
-    blocks = jnp.pad(
-        blocks,
-        ((0, 0), (0, up_to(slots, 16) - slots), (0, up_to(mod_width, 128) - mod_width)),
-    )
     vector = jnp.concatenate([qkv_sums[0], qkv_sums[2], sums[1], gb1, sums[2], sums[0]])
     length = vector.shape[0]
     vector = jnp.pad(vector, (0, up_to(length, 1024) - length)).reshape(-1, 128)
-    g_attn, small, grad_ada_weight, grad_ada_bias, router_grads, logit_sums = final_call(
-        parts, vector, blocks, logits, every_cond, mod_width, planes
+    g_last, small, grad_ada_weight, grad_ada_bias, router_grads, logit_sums, grad_tokens = final_call(
+        jnp.where(single, 1.0, 0.0).astype(F32).reshape(1),
+        table,
+        mods,
+        vector,
+        logits,
+        every_cond,
+        part,
+        dqkv,
+        full_qkv,
+        tokens,
+        ga,
+        mod_width,
+        planes,
+        blk,
     )
+    g_attn = jnp.concatenate([g_done, g_last], axis=1)
     g_attn = g_attn[: 4 * (d // devices)].reshape(4, d // devices, d)
     small = small.reshape(-1)[:length]
     grad_ada_bias = grad_ada_bias[0]

time: 551 us -> 518 us (0.940)
  Pallas kernels: 498 us -> 465 us
    pallas_call x4 -> x2, Pallas kernels: 173 us -> 148 us  [the longest x1 101 us: backward_call(): pl.pallas_call(functools.partial(backward_kernel, heads=heads, blk=blk, p...]
    pallas_call x1, Pallas kernels: 131 us -> 123 us  [mlp_call(): pl.pallas_call(functools.partial(mlp_kernel, blk=blk, planes=planes), gri...]
    unnamed x77 -> x80, local copies, waits for them, and re-layouts: 10.7 us -> 15.5 us
where the time goes in v4:
time: 518 us; the launch traced here: 511 us
  Pallas kernels  465 us (90%)
  local copies, waits for them, and re-layouts  32.9 us (6%)
  other arithmetic  8.75 us (2%)
    pallas_call x1, Pallas kernels, mlp_call(): pl.pallas_call(functools.partial(mlp_kernel, blk=blk, planes=planes), gri...  123 us
    pallas_call x1, Pallas kernels, backward_call(): pl.pallas_call(functools.partial(backward_kernel, heads=heads, blk=blk, p...  101 us
    pallas_call x1, Pallas kernels, forward_call(): pl.pallas_call(functools.partial(forward_kernel, heads=heads, blk=blk, pl...  98.8 us
    pallas_call x1, Pallas kernels, prologue_call(): pl.pallas_call(functools.partial(prologue_kernel, planes=planes, slots=sl...  67.7 us
    pallas_call x1, Pallas kernels, final_call(): pl.pallas_call(functools.partial(final_kernel, planes=planes, blk=blk), o...  46.5 us
    pallas_call x1, Pallas kernels, middle_back_call(): pl.pallas_call(functools.partial(middle_back_kernel, heads=heads), grid=(...  27.8 us
    unnamed x80, local copies, waits for them, and re-layouts  15.5 us

profile of v4, /device:TPU:0, one launch (start us, length us, event | category | flops | bytes accessed | tf_op | source)
XLA Modules:
  0.0 510.5 jit_solution(14490928071232297506)
XLA Ops:
  0.8 1.1 fusion.11
  1.8 1.7 pad_maximum_fusion.shard_ref
  4.9 2.1 copy.76.ada_ref
  7.0 1.2 broadcast_in_dim.105
  8.2 67.7 %weights_and_modulation.1 = (bf16[4,4,2,144,1152]{4,3,2,1,0:T(8,128)(2,1)}, bf16[32,48,128]{2,1,0:T(8,128)(2,1)}, bf16[32,16,256]{2,1,0:T(8,128)(2,1)}) custom-call(bf16[144,1152]{1,0:T(8,128)(2,1)} %pad_maximum_fusion.shard_ref, bf16[48,128]{1,0:T(8,128)(2,1)} %pad.16.cond_ref, bf16[1152,216]{1,0:T(8,128)(2,1)} %copy.76.ada_ref, f32[1,216]{1,0:T(1,128)} %bitcast.80), custom_call_target="tpu_custom_call" | custom-call | tf_op jit(solution)/shard_map/weights_and_modulation/pallas_call | solution.py:563
  75.9 0.9 convert_bitcast_fusion
  79.2 0.9 convert_multiply_fusion.2
  80.9 1.0 copy.82.keep_ref
  84.3 1.0 reshape.147.up_ref
  85.7 1.0 reshape.149.down_ref
  86.8 98.8 %attention_and_middle_forward.1 = (f32[16,1024]{1,0:T(8,128)}, f32[1024,1]{1,0:T(8,128)}, bf16[1152,1024]{1,0:T(8,128)(2,1)}, bf16[1024,3456]{1,0:T(8,128)(2,1)}...) custom-call(f32[1]{0:T(128)} %bitcast.1.off_ref, ...), custom_call_target="tpu_custom_call" | custom-call | tf_op jit(solution)/shard_map/attention_and_middle_forward/pallas_call | solution.py:785
  187.3 123.4 %feed_forward.1 = (f32[1024,1152]{1,0:T(8,128)}, f32[1024,1152]{1,0:T(8,128)}, f32[4,1,1152]{2,1,0:T(1,128)}, f32[4,4,1152]{2,1,0:T(4,128)}, f32[144,1152]{1,0:T...) custom-call(bf16[1024,1152]{1,0:T(8,128)(2,1)} %get-tuple-element.65.n2_r, ...), custom_call_target="tpu_custom_call" | custom-call | tf_op jit(solution)/shard_map/feed_forward/pallas_call | solution.py:1174
  310.7 27.8 %middle_backward.1 = (f32[1024,1152]{1,0:T(8,128)}, f32[1024,1152]{1,0:T(8,128)}, bf16[1024,1152]{1,0:T(8,128)(2,1)}, f32[16,1024]{1,0:T(8,128)}, bf16[1152,1152...) custom-call(f32[1024,1152]{1,0:T(8,128)} %get-tuple-element.69.mlp_ref, ...), custom_call_target="tpu_custom_call" | custom-call | tf_op jit(solution)/shard_map/middle_backward/pallas_call | solution.py:1295
  338.5 101.3 %attention_backward.1 = (bf16[1024,3456]{1,0:T(8,128)(2,1)}, f32[3,1,1152]{2,1,0:T(1,128)}, f32[144,1152]{1,0:T(8,128)}, f32[144,1152]{1,0:T(8,128)}, f32[144,76...) custom-call(f32[1]{0:T(128)} %bitcast.1.off_ref, bf16[1024,3456]{1,0:T(8,128)(2,1)} %get-tuple-element.79.qkv_ref, ...), custom_call_target="tpu_custom_call" | custom-call | tf_op jit(solution)/shard_map/attention_backward/pallas_call | solution.py:985
  439.8 1.3 add.48
  441.8 1.2 copy.94
  443.7 1.2 copy.93
  448.3 1.2 pad.19.conds_ref
  449.5 46.5 %last_sums.1 = (f32[144,384]{1,0:T(8,128)}, f32[88,128]{1,0:T(8,128)}, f32[1152,216]{1,0:T(8,128)}, f32[1,216]{1,0:T(1,128)}, f32[1152,128]{1,0:T(8,128)}, /*index=5*/f32[1,128]{1,0:T(1,128)}, f32[1024,1152]{1,0:T(8,128)}) custom-call(f32[1]{0:T(128)} %bitcast.14.single_ref, f32[4,6,1152]{2,1,0:T(8,128)} %broadcast_select_fusion.mod_ref.table_ref, ...), custom_call_target="tpu_custom_call" | custom-call | tf_op jit(solution)/shard_map/last_sums/pallas_call | solution.py:1464
  496.1 1.0 constant_dynamic-update-slice_fusion.1
  497.5 0.8 copy.99
  499.0 1.3 copy.92
  500.6 0.9 copy.96
  504.6 4.9 copy.119
  (147 shorter events, 18.0 us)
Async XLA Ops:
  0.7 184.9 %copy-start = (bf16[1152,32]{0,1:T(8,128)(2,1)S(1)}, bf16[1152,32]{0,1:T(8,128)(2,1)}, u32[]{:S(2)}) copy-start(bf16[1152,32]{0,1:T(8,128)(2,1)} %param.42) | copy-start | bytes 221188
  0.7 80.2 %copy-start.24 = (s32[1024]{0:T(1024)S(1)}, s32[1024]{0:T(1024)}, u32[]{:S(2)}) copy-start(s32[1024]{0:T(1024)} %param.28) | copy-start | bytes 12292
  0.7 81.3 %copy-start.19 = (bf16[1152]{0:T(1024)(128)(2,1)S(1)}, bf16[1152]{0:T(1024)(128)(2,1)}, u32[]{:S(2)}) copy-start(bf16[1152]{0:T(1024)(128)(2,1)} %param.32) | copy-start | bytes 6916
  0.7 81.4 %copy-start.20 = (bf16[1152]{0:T(1024)(128)(2,1)S(1)}, bf16[1152]{0:T(1024)(128)(2,1)}, u32[]{:S(2)}) copy-start(bf16[1152]{0:T(1024)(128)(2,1)} %param.33) | copy-start | bytes 6916
  0.7 81.7 %copy-start.21 = (bf16[1152]{0:T(1024)(128)(2,1)S(1)}, bf16[1152]{0:T(1024)(128)(2,1)}, u32[]{:S(2)}) copy-start(bf16[1152]{0:T(1024)(128)(2,1)} %param.35) | copy-start | bytes 6916
  0.7 82.0 %copy-start.22 = (bf16[1152]{0:T(1024)(128)(2,1)S(1)}, bf16[1152]{0:T(1024)(128)(2,1)}, u32[]{:S(2)}) copy-start(bf16[1152]{0:T(1024)(128)(2,1)} %param.39) | copy-start | bytes 6916
  0.7 82.2 %copy-start.23 = (bf16[1152]{0:T(1024)(128)(2,1)S(1)}, bf16[1152]{0:T(1024)(128)(2,1)}, u32[]{:S(2)}) copy-start(bf16[1152]{0:T(1024)(128)(2,1)} %param.44) | copy-start | bytes 6916
  0.7 83.1 %copy-start.9 = (bf16[576,288]{0,1:T(8,128)(2,1)S(1)}, bf16[576,288]{0,1:T(8,128)(2,1)}, u32[]{:S(2)}) copy-start(bf16[576,288]{0,1:T(8,128)(2,1)} %param.36) | copy-start | bytes 995332
  0.7 84.6 %copy-start.10 = (bf16[576,288]{0,1:T(8,128)(2,1)S(1)}, bf16[576,288]{0,1:T(8,128)(2,1)}, u32[]{:S(2)}) copy-start(bf16[576,288]{0,1:T(8,128)(2,1)} %param.38) | copy-start | bytes 995332
  86.8 98.8 %copy-start.27 = (bf16[32]{0:T(256)(128)(2,1)S(1)}, bf16[32]{0:T(256)(128)(2,1)}, u32[]{:S(2)}) copy-start(bf16[32]{0:T(256)(128)(2,1)} %param.43) | copy-start | bytes 196
  86.8 98.8 %copy-start.26 = (s32[4,32]{1,0:T(4,128)S(1)}, s32[4,32]{1,0:T(4,128)}, u32[]{:S(2)}) copy-start(s32[4,32]{1,0:T(4,128)} %param.27) | copy-start | bytes 1540
  86.8 99.9 %copy-start.18 = (bf16[4608]{0:T(1024)(128)(2,1)S(1)}, bf16[4608]{0:T(1024)(128)(2,1)}, u32[]{:S(2)}) copy-start(bf16[4608]{0:T(1024)(128)(2,1)} %param.37) | copy-start | bytes 27652
  338.5 101.3 %copy-start.6 = (f32[144,1152]{1,0:T(8,128)S(1)}, f32[144,1152]{1,0:T(8,128)}, u32[]{:S(2)}) copy-start(f32[144,1152]{1,0:T(8,128)} %get-tuple-element.105) | copy-start | bytes 1990660
  441.8 5.0 copy-start.16
  441.8 5.2 %copy-start.17 = (f32[3,1152]{1,0:T(4,128)S(1)}, f32[3,1152]{1,0:T(4,128)}, u32[]{:S(2)}) copy-start(f32[3,1152]{1,0:T(4,128)} %get-tuple-element.88) | copy-start | bytes 41476
  441.8 5.2 %copy-start.15 = (f32[4,1,1152]{2,1,0:T(1,128)S(1)}, f32[4,1,1152]{2,1,0:T(1,128)}, u32[]{:S(2)}) copy-start(f32[4,1,1152]{2,1,0:T(1,128)} %get-tuple-element.89) | copy-start | bytes 55300
  441.8 6.0 %copy-start.12 = (bf16[32,48,128]{2,1,0:T(8,128)(2,1)S(1)}, bf16[32,48,128]{2,1,0:T(8,128)(2,1)}, u32[]{:S(2)}) copy-start(bf16[32,48,128]{2,1,0:T(8,128)(2,1)} %get-tuple-element.91) | copy-start | bytes 1179652
  444.9 4.5 copy-start.4
  449.5 46.5 %copy-start.8 = (f32[144,768]{1,0:T(8,128)S(1)}, f32[144,768]{1,0:T(8,128)}, u32[]{:S(2)}) copy-start(f32[144,768]{1,0:T(8,128)} %get-tuple-element.99) | copy-start | bytes 1327108
  496.0 4.3 copy-start.2
  497.2 5.1 copy-start.14
  497.2 6.3 %copy-start.28 = (f32[1,128]{1,0:T(1,128)S(1)}, f32[1,128]{1,0:T(1,128)}, u32[]{:S(2)}) copy-start(f32[1,128]{1,0:T(1,128)} %get-tuple-element.107) | copy-start | bytes 1540
  504.6 5.4 %copy-start.1 = (bf16[1152,32]{0,1:T(8,128)(2,1)S(1)}, bf16[1152,32]{0,1:T(8,128)(2,1)}, u32[]{:S(2)}) copy-start(bf16[1152,32]{0,1:T(8,128)(2,1)} %param.42) | copy-start | bytes 221188
  504.6 4.9 copy-start.25
  (5 other events, 13.8 us)

commit v5 on v4

--- a/solution.py
+++ b/solution.py
@@ -525,58 +525,6 @@
         return [pltpu.VMEM((2, rows, width), dtype), pltpu.SemaphoreType.DMA((2,))]
 
 
-def prologue_kernel(
-    shard_ref, cond_ref, ada_ref, ada_bias_ref, g_ref, conds_ref, mods_ref, mod_local, cond_sems, mod_sems, *sems, planes, slots
-):
-    place = Place(planes)
-    weights = Gather(place, shard_ref, g_ref, *sems)
-    conds = Exchange(place, cond_ref, conds_ref, cond_sems, True)
-    mods = Exchange(place, mod_local, mods_ref, mod_sems, False)
-    conds.greet()
-    weights.run("begin")
-    conds.start()
-    mod_local[...] = jnp.zeros_like(mod_local)
-    parts = weights.parts()
-    for part in parts[1:4]:
-        weights.run(part)
-    conds.arrive()
-    devices, rows, lanes = conds_ref.shape
-    d, width = ada_ref.shape
-    every = conds_ref[...].reshape(devices * rows, lanes)
-    columns = ada_bias_ref[...]
-    for j in range(d // lanes):
-        piece = dg(every, ada_ref[j * lanes : (j + 1) * lanes, :], NN).reshape(devices, rows, width)
-        columns = columns + piece[:, slots * j : slots * (j + 1)]
-    mod_local[:, :slots, :width] = columns.astype(BF)
-    mods.start()
-    for part in parts[4:-1]:
-        weights.run(part)
-    mods.arrive()
-    conds.end()
-    mods.end()
-    weights.run("end")
-
-
-def prologue_call(shard, cond, ada, ada_bias, planes, slots):
-    devices = 8 * planes
-    lanes = up_to(ada.shape[1], 128)
-    return pl.pallas_call(
-        functools.partial(prologue_kernel, planes=planes, slots=slots),
-        out_shape=(
-            shape((4, planes, 2) + shard.shape, BF),
-            shape((devices,) + cond.shape, BF),
-            shape((devices, 16, lanes), BF),
-        ),
-        in_specs=[ANY_SPEC, VMEM_SPEC, VMEM_SPEC, VMEM_SPEC],
-        out_specs=(ANY_SPEC, VMEM_SPEC, VMEM_SPEC),
-        scratch_shapes=[pltpu.VMEM((devices, 16, lanes), BF)]
-        + [Exchange.scratch(planes)] * 2
-        + Gather.scratch(planes),
-        compiler_params=params(collective_id=1),
-        name="weights_and_modulation",
-    )(shard, cond, ada, ada_bias)
-
-
 def head_window(h, hd, width):
     a = pl.multiple_of(jnp.minimum((h * hd) // 128, (width - WINDOW) // 128) * 128, 128)
     lane = lax.broadcasted_iota(jnp.int32, (1, WINDOW), 1) + a
@@ -589,17 +537,28 @@
 
 def forward_kernel(
     off_ref,
+    single_ref,
     gate_ref,
-    mod_ref,
-    vec_ref,
     keep_ref,
+    cond_ref,
+    ada_ref,
+    ada_bias_ref,
+    qkv_shard_ref,
+    proj_shard_ref,
+    up_t_ref,
+    down_t_ref,
+    query_bias_ref,
+    value_bias_ref,
+    proj_bias_ref,
+    down_bias_ref,
+    router_ref,
     tokens_ref,
     cot_ref,
-    g_ref,
-    up_ref,
-    down_ref,
     lse_ref,
     tg_ref,
+    conds_ref,
+    table_ref,
+    vec_ref,
     n1_ref,
     qkv_ref,
     w_ref,
@@ -613,7 +572,13 @@
     g_up_ref,
     g_down_ref,
     lse_sc,
+    shard_ref,
+    up_ref,
+    down_ref,
     g_s,
+    mod_local,
+    mods_s,
+    flat_s,
     tok_s,
     w_s,
     wp_s,
@@ -632,6 +597,8 @@
     n2_sems,
     gm_slots,
     gm_sems,
+    cond_sems,
+    mod_sems,
     *gather_sems,
     heads,
     blk,
@@ -642,18 +609,31 @@
     nb = t // blk
     c = hd**-0.5 * LOG2E
     place = Place(planes)
-    place.barrier()
-    half = len(gather_sems) // 2
+    weights = Gather(place, shard_ref, g_s, *gather_sems[:6])
     gathers = [
-        Gather(place, up_ref, g_up_ref, *gather_sems[:half]),
-        Gather(place, down_ref, g_down_ref, *gather_sems[half:]),
+        Gather(place, up_ref, g_up_ref, *gather_sems[6:12]),
+        Gather(place, down_ref, g_down_ref, *gather_sems[12:]),
     ]
-    parts = gathers[0].parts()
-    for g in gathers:
-        g.run("begin")
-    groups = spread_out(
-        [functools.partial(g.run, part) for part in parts[1:-1] for g in gathers], 2 * nb + heads
-    )
+    conds = Exchange(place, cond_ref, conds_ref, cond_sems, True)
+    mods = Exchange(place, mod_local, mods_s, mod_sems, False)
+    rows = proj_shard_ref.shape[0]
+    for b in range(3):
+        shard_ref[b * rows : (b + 1) * rows, :] = qkv_shard_ref[:, b * d : (b + 1) * d]
+    shard_ref[3 * rows : 4 * rows, :] = proj_shard_ref[...]
+    conds.greet()
+    weights.run("begin")
+    conds.start()
+    for src, dst in ((up_t_ref, up_ref), (down_t_ref, down_ref)):
+        natural = src[...].T
+        quarter = natural.shape[0] // 4
+        dst[:quarter, :] = jnp.concatenate(
+            [natural[k * quarter : (k + 1) * quarter] for k in range(4)], axis=1
+        )
+    vec_ref[...] = jnp.zeros_like(vec_ref)
+    for i, ref in enumerate(
+        (query_bias_ref, value_bias_ref, proj_bias_ref, down_bias_ref, router_ref)
+    ):
+        vec_ref[i : i + 1, :] = ref[...].astype(F32).reshape(1, d)
 
     def run_group(i):
         for step in groups[i]:
@@ -663,7 +643,6 @@
         name: pltpu.make_async_copy(src, dst, sems.at[i])
         for i, (name, src, dst) in enumerate(
             (
-                ("g", g_ref, g_s),
                 ("tok", tokens_ref, tok_s),
                 ("w", w_s, w_ref),
                 ("wp", wp_s, wp_ref),
@@ -680,18 +659,54 @@
             cot_ref.at[pl.ds(i * blk, blk)], cot_s.at[i % 2], cot_sems.at[i % 2]
         )
 
-    moves["g"].start()
     moves["tok"].start()
     for i in range(2):
         cot_copy(i).start()
-    devices = g_s.shape[0]
+    parts = weights.parts()
+    rest = [(g, part) for part in parts[1:-1] for g in gathers]
+    mod_local[...] = jnp.zeros_like(mod_local)
+    for part in parts[1:4]:
+        weights.run(part)
+    conds.arrive()
+    devices, rows, lanes = conds_ref.shape
+    width = ada_ref.shape[0]
+    slots = table_ref.shape[0]
+    every = conds_ref[...].reshape(devices * rows, lanes)
+    columns = ada_bias_ref[...]
+    for j in range(d // lanes):
+        piece = dg(every, ada_ref[:, j * lanes : (j + 1) * lanes], NT).reshape(devices, rows, width)
+        columns = columns + piece[:, slots * j : slots * (j + 1)]
+    mod_local[:, :slots, :width] = columns.astype(BF)
+    mods.start()
+    middle = 9
+    for part in parts[4:middle]:
+        weights.run(part)
+    for g in gathers:
+        g.run("begin")
+    late = parts[middle:-1]
+    for part in late[: len(late) // 2]:
+        weights.run(part)
+    for g, part in rest[:4]:
+        g.run(part)
+    for part in late[len(late) // 2 :]:
+        weights.run(part)
+    groups = spread_out([functools.partial(g.run, part) for g, part in rest[4:]], 2 * nb + heads)
+    mods.arrive()
+    for i in range(devices):
+        flat_s[:slots, i * width : (i + 1) * width] = mods_s[i, :slots, :width].astype(F32)
+    single = single_ref[0]
+    flat = flat_s[:slots, :]
+    flat = flat * (1.0 - single) + flat[:1] * single
+    for k in range(6):
+        table_ref[:, k, :] = flat[:, k * d : (k + 1) * d]
+    weights.run("end")
     r = d // devices
-    moves["g"].wait()
     for i in range(devices):
+        at = (i // (2 * planes), i // 2 % planes, i % 2)
         rows = slice(i * r, (i + 1) * r)
         for b in range(3):
-            w_s[rows, b * d : (b + 1) * d] = g_s[i, b * r : (b + 1) * r, :]
-        wp_s[rows, :] = g_s[i, 3 * r : 4 * r, :]
+            w_s[rows, b * d : (b + 1) * d] = g_s[at + (slice(b * r, (b + 1) * r),)]
+        wp_s[rows, :] = g_s[at + (slice(3 * r, 4 * r),)]
     moves["w"].start()
     moves["wp"].start()
     moves["tok"].wait()
@@ -700,7 +715,7 @@
         return vec_ref[i : i + 1, :]
 
     def mod(i, k):
-        return mod_ref[i, k : k + 1, :]
+        return table_ref[i, k : k + 1, :]
 
     bias = jnp.concatenate(
         [vector(QUERY_BIAS), jnp.zeros((1, d), F32), vector(VALUE_BIAS)], axis=1
@@ -776,17 +791,29 @@
         stream.end()
     for name in ("w", "wp", "n1", "qkv", "att", "gated"):
         moves[name].wait()
-
-
-def forward_call(off, gate_rows, mods, vecs, keep, tokens, cot, g, up, down, heads, blk, planes):
+    conds.end()
+    mods.end()
+
+
+def forward_call(
+    off, single, gate_rows, keep, cond, ada_t, ada_bias, qkv_w, proj_w, up_t, down_t, vectors, tokens, cot, heads, blk, planes
+):
     t, d = tokens.shape
-    gathered = shape((4, planes, 2) + up.shape, BF)
+    devices = 8 * planes
+    slots = t // blk
+    lanes = up_to(ada_t.shape[0], 128)
+    shard = (up_to(4 * proj_w.shape[0], 16), d)
+    unit = (up_to(up_t.shape[1] // 4, 16), d)
+    gathered = shape((4, planes, 2) + unit, BF)
     dma = pltpu.SemaphoreType.DMA
     return pl.pallas_call(
         functools.partial(forward_kernel, heads=heads, blk=blk, planes=planes),
         out_shape=(
             shape((heads, t)),
             shape((t, 1)),
+            shape((devices,) + cond.shape, BF),
+            shape((slots, 6, d)),
+            shape((8, d)),
             shape((d, t), BF),
             shape((t, 3 * d), BF),
             shape((d, 3 * d), BF),
@@ -800,11 +827,17 @@
             gathered,
             gathered,
         ),
-        in_specs=[SMEM_SPEC] + [VMEM_SPEC] * 4 + [ANY_SPEC] * 5,
-        out_specs=(VMEM_SPEC,) * 2 + (ANY_SPEC,) * 12,
+        in_specs=[SMEM_SPEC] * 2 + [VMEM_SPEC] * 14 + [ANY_SPEC] * 2,
+        out_specs=(VMEM_SPEC,) * 5 + (ANY_SPEC,) * 12,
         scratch_shapes=[
             pltpu.VMEM((t, 128), F32),
-            pltpu.VMEM(g.shape, BF),
+            pltpu.VMEM(shard, BF),
+            pltpu.VMEM(unit, BF),
+            pltpu.VMEM(unit, BF),
+            pltpu.VMEM((4, planes, 2) + shard, BF),
+            pltpu.VMEM((devices, 16, lanes), BF),
+            pltpu.VMEM((devices, 16, lanes), BF),
+            pltpu.VMEM((up_to(slots, 8), 6 * d), F32),
             pltpu.VMEM((t, d), F32),
             pltpu.VMEM((d, 3 * d), BF),
             pltpu.VMEM((d, d), BF),
@@ -814,14 +847,17 @@
             pltpu.VMEM((t, d), BF),
             pltpu.VMEM((2, blk, d), F32),
             dma((2,)),
-            dma((8,)),
+            dma((7,)),
         ]
         + Stream.scratch(blk, d, F32) * 2
         + Stream.scratch(blk, d, BF) * 2
-        + Gather.scratch(planes) * 2,
-        compiler_params=params(62, collective_id=2),
-        name="attention_and_middle_forward",
-    )(off, gate_rows, mods, vecs, keep, tokens, cot, g, up, down)
+        + [Exchange.scratch(planes)] * 2
+        + Gather.scratch(planes) * 3,
+        compiler_params=params(63, collective_id=2),
+        name="forward",
+    )(
+        off, single, gate_rows, keep, cond, ada_t, ada_bias, qkv_w, proj_w, up_t, down_t, *vectors, tokens, cot
+    )
 
 
 def backward_kernel(
@@ -1328,18 +1364,27 @@
     sums_ref,
     logits_ref,
     conds_ref,
+    up1_ref,
+    up2_ref,
+    down1_ref,
+    down2_ref,
+    done_ref,
     part_ref,
     dqkv_ref,
     w_ref,
     tokens_ref,
     ga_ref,
-    out_ref,
+    qkv_grad_ref,
+    proj_grad_ref,
     sum_ref,
     ada_ref,
     ada_bias_ref,
     router_ref,
     logit_ref,
+    up_ref,
+    down_ref,
     grad_ref,
+    conds_s,
     all_sums,
     own_mods,
     all_mods,
@@ -1418,17 +1463,30 @@
     def products():
         mods.arrive()
         logits.arrive()
-        devices, rows, _ = conds_ref.shape
-        conds = conds_ref[...].reshape(devices * rows, d)
+        devices, rows, _ = conds_s.shape
+        conds = conds_s[...].reshape(devices * rows, d)
         got = all_mods[...].reshape(devices * rows, -1)
         columns = ada_bias_ref.shape[1]
-        ada_ref[...] = dg(conds, got, TN)[:, :columns]
+        ada_ref[...] = dg(got, conds, TN)[:columns]
         ada_bias_ref[...] = col_sum(got.astype(F32))[:, :columns]
         got = all_logits[...].reshape(devices * rows, -1)
         router_ref[...] = lax.dot_general(
-            conds.astype(F32), got, TN, precision=HIGHEST, preferred_element_type=F32
+            got, conds.astype(F32), TN, precision=HIGHEST, preferred_element_type=F32
         )
         logit_ref[...] = col_sum(got)
+
+    def local_work():
+        lanes = conds_ref.shape[2]
+        conds_s[...] = jnp.zeros_like(conds_s)
+        for j in range(d // lanes):
+            rows = slice(nb * j, nb * (j + 1))
+            conds_s[:, :nb, j * lanes : (j + 1) * lanes] = conds_ref[:, rows, :]
+        piece = up_ref.shape[0]
+        quarter = up_ref.shape[1] // 4
+        for a, b, to in ((up1_ref, up2_ref, up_ref), (down1_ref, down2_ref, down_ref)):
+            both = a[...] + b[...]
+            rows = [both[:quarter, k * piece : (k + 1) * piece] for k in range(4)]
+            to[...] = jnp.concatenate(rows, axis=0).T
 
     parts = [functools.partial(sums.run, part) for part in sums.parts()[1:-1]]
     rest = steps[3:]
@@ -1438,7 +1496,9 @@
         [functools.partial(block, i) for i in range(1, nb - 1)],
         rest[:1],
         [functools.partial(block, nb - 1), exchange],
-        rest[1:],
+        rest[1:2],
+        [local_work],
+        rest[2:],
     ]
     work = [do for group in work for do in group]
     for do, group in zip(work, spread_out(parts, len(work))):
@@ -1448,33 +1508,48 @@
     products()
     sums.run("end")
     sum_ref[...] = jnp.sum(all_sums[...].reshape((8 * planes,) + sum_ref.shape), axis=0)
-    out_ref[...] = chain.total()
+    last = chain.total()
+    r = proj_grad_ref.shape[0]
+    ready = done_ref.shape[1]
+    for b in range(4):
+        rows = slice(b * r, (b + 1) * r)
+        to, start = (qkv_grad_ref, b * d) if b < 3 else (proj_grad_ref, 0)
+        to[:, start : start + ready] = done_ref[rows, :]
+        to[:, start + ready : start + d] = last[rows]
     out.end()
     mods.end()
     logits.end()
 
 
-def final_call(single, table, mods, sums, logits, conds, part, dqkv, w, tokens, ga, mod_width, planes, blk):
+def final_call(
+    single, table, mods, sums, logits, conds, pairs, done, part, dqkv, w, tokens, ga, mod_width, hidden, planes, blk
+):
     rows, width = part.shape[3:]
     t, d = tokens.shape
     devices = 8 * planes
     spread = (4, planes, 2)
-    blocks = (devices, conds.shape[1], up_to(mod_width, 128))
+    padded = logits.shape[0]
+    blocks = (devices, padded, up_to(mod_width, 128))
+    piece = shape((d // 4, hidden))
     dma = pltpu.SemaphoreType.DMA
     return pl.pallas_call(
         functools.partial(final_kernel, planes=planes, blk=blk),
         out_shape=(
-            shape((rows, width)),
+            shape((d // devices, 3 * d)),
+            shape((d // devices, d)),
             shape(sums.shape),
-            shape((d, mod_width)),
+            shape((mod_width, d)),
             shape((1, mod_width)),
-            shape((d, logits.shape[1])),
+            shape((logits.shape[1], d)),
             shape((1, logits.shape[1])),
+            piece,
+            piece,
             shape((t, d)),
         ),
-        in_specs=[SMEM_SPEC] + [VMEM_SPEC] * 5 + [ANY_SPEC] * 5,
-        out_specs=(VMEM_SPEC,) * 6 + (ANY_SPEC,),
+        in_specs=[SMEM_SPEC] + [VMEM_SPEC] * 10 + [ANY_SPEC] * 5,
+        out_specs=(VMEM_SPEC,) * 9 + (ANY_SPEC,),
         scratch_shapes=[
+            pltpu.VMEM((devices, padded, d), BF),
             pltpu.VMEM(spread + sums.shape, F32),
             pltpu.VMEM(blocks, BF),
             pltpu.VMEM(blocks, BF),
@@ -1492,7 +1567,7 @@
         + Scatter.scratch(planes, rows, width),
         compiler_params=params(collective_id=4),
         name="last_sums",
-    )(single, table, mods, sums, logits, conds, part, dqkv, w, tokens, ga)
+    )(single, table, mods, sums, logits, conds, *pairs, done, part, dqkv, w, tokens, ga)
 
 
 def on_device(
@@ -1541,30 +1616,11 @@
         return jnp.where(single, jnp.where(first, total, 0.0), blocks)
 
     devices = 8 * planes
-    def pack_rows(*blocks):
-        return pad_rows(jnp.concatenate(blocks, axis=0))
-
-    def pack_piece(weight):
-        rows, cols = weight.shape
-        return pad_rows(weight.reshape(4, rows // 4, cols).transpose(1, 0, 2).reshape(rows // 4, d))
-
-    def unpack_piece(piece, rows):
-        cols = d // 4
-        return piece[: rows // 4].reshape(rows // 4, 4, cols).transpose(1, 0, 2).reshape(rows, cols)
-
     silu_cond = jax.nn.silu(conditioning.astype(F32)).astype(BF)
-    shard = pack_rows(qkv_weight[:, :d], qkv_weight[:, d : 2 * d], qkv_weight[:, 2 * d :], proj_weight)
     conds_pad = pad_rows(silu_cond.reshape(slots, -1, 128).transpose(1, 0, 2).reshape(-1, 128))
-    g_attn, conds, mod_columns = prologue_call(
-        shard, conds_pad, ada_weight, ada_bias.astype(F32)[None], planes, slots
-    )
     mod_width = ada_bias.shape[0]
-    every_cond = conds[:, : slots * d // 128].reshape(devices, -1, slots, 128).transpose(0, 2, 1, 3)
-    every_cond = jnp.pad(
-        every_cond.reshape(devices, slots, d), ((0, 0), (0, up_to(slots, 16) - slots), (0, 0))
-    )
-    modulation = mod_columns[:, :slots, :mod_width].transpose(1, 0, 2).reshape(slots, 6, d)
-    table = per_block(modulation.astype(F32))
+    alone = jnp.where(single, 1.0, 0.0).astype(F32).reshape(1)
+
     def router(weight, bias, mask):
         gate = jax.nn.sigmoid(dg(silu_cond, weight, NN) + bias.astype(F32))
         mask = mask.astype(F32)
@@ -1576,19 +1632,39 @@
     chan_rows = jnp.repeat(per_block(chan_gate), unit, axis=1)
     keep = (1.0 - skip_mask.astype(F32))[:, None]
 
-    vecs = jnp.concatenate([query_bias, value_bias, proj_bias, fc2_bias, token_router])
-    vecs = vecs.astype(F32).reshape(5, d)
-    lse, tg, n1t, qkv, full_qkv, full_proj, att, gated, attn, after, n2, gm, g_up, g_down = forward_call(
-        off,
-        head_rows,
+    (
+        lse,
+        tg,
+        conds,
         table,
         vecs,
+        n1t,
+        qkv,
+        full_qkv,
+        full_proj,
+        att,
+        gated,
+        attn,
+        after,
+        n2,
+        gm,
+        g_up,
+        g_down,
+    ) = forward_call(
+        off,
+        alone,
+        head_rows,
         keep,
+        conds_pad,
+        ada_weight.T,
+        ada_bias.astype(F32)[None],
+        qkv_weight,
+        proj_weight,
+        fc1_weight.T,
+        fc2_weight.T,
+        (query_bias, value_bias, proj_bias, fc2_bias, token_router),
         tokens,
         cotangent,
-        g_attn.reshape((devices,) + shard.shape),
-        pack_piece(fc1_weight),
-        pack_piece(fc2_weight),
         heads,
         blk,
         planes,
@@ -1628,24 +1704,36 @@
     vector = jnp.concatenate([qkv_sums[0], qkv_sums[2], sums[1], gb1, sums[2], sums[0]])
     length = vector.shape[0]
     vector = jnp.pad(vector, (0, up_to(length, 1024) - length)).reshape(-1, 128)
-    g_last, small, grad_ada_weight, grad_ada_bias, router_grads, logit_sums, grad_tokens = final_call(
-        jnp.where(single, 1.0, 0.0).astype(F32).reshape(1),
+    (
+        g_qkv,
+        g_proj,
+        small,
+        grad_ada_t,
+        grad_ada_bias,
+        router_t,
+        logit_sums,
+        g_up_t,
+        g_down_t,
+        grad_tokens,
+    ) = final_call(
+        alone,
         table,
         mods,
         vector,
         logits,
-        every_cond,
+        conds,
+        (g_up, o_up, g_down, o_down),
+        g_done,
         part,
         dqkv,
         full_qkv,
         tokens,
         ga,
         mod_width,
+        fc1_weight.shape[0],
         planes,
         blk,
     )
-    g_attn = jnp.concatenate([g_done, g_last], axis=1)
-    g_attn = g_attn[: 4 * (d // devices)].reshape(4, d // devices, d)
     small = small.reshape(-1)[:length]
     grad_ada_bias = grad_ada_bias[0]
     logit_sums = logit_sums[0]
@@ -1654,20 +1742,20 @@
     return (
         output,
         grad_tokens,
-        grad_ada_weight,
+        grad_ada_t.T,
         grad_ada_bias,
-        g_attn[:3].transpose(1, 0, 2).reshape(d // devices, 3 * d),
+        g_qkv,
         g_query,
         g_value,
-        g_attn[3],
+        g_proj,
         g_proj_bias,
-        unpack_piece(g_up + o_up, fc1_weight.shape[0]),
+        g_up_t.T,
         g_b1,
-        unpack_piece(g_down + o_down, fc2_weight.shape[0]),
+        g_down_t.T,
         g_b2,
-        router_grads[:, :heads],
+        router_t[:heads].T,
         logit_sums[:heads],
-        router_grads[:, heads : heads + groups],
+        router_t[heads : heads + groups].T,
         logit_sums[heads : heads + groups],
         g_router,
     )

time: 518 us -> 494 us (0.954)
  local copies, waits for them, and re-layouts: 32.9 us -> 24 us
  Pallas kernels: 465 us -> 458 us
    pallas_call x1, Pallas kernels: 98.8 us -> 169 us  [forward_call(): pl.pallas_call(functools.partial(forward_kernel, heads=heads, blk=blk, pl...]
    pallas_call x1 -> x0, Pallas kernels: 67.7 us -> none  [prologue_call(): pl.pallas_call(functools.partial(prologue_kernel, planes=planes, slots=sl...]
    pallas_call x1, Pallas kernels: 123 us -> 114 us  [mlp_call(): pl.pallas_call(functools.partial(mlp_kernel, blk=blk, planes=planes), gri...]
    unnamed x80 -> x42, local copies, waits for them, and re-layouts: 15.5 us -> 9.79 us
where the time goes in v5:
time: 494 us; the launch traced here: 491 us
  Pallas kernels  458 us (93%)
  local copies, waits for them, and re-layouts  24 us (5%)
  other arithmetic  5.53 us (1%)
    pallas_call x1, Pallas kernels, forward_call(): pl.pallas_call(functools.partial(forward_kernel, heads=heads, blk=blk, pl...  169 us
    pallas_call x1, Pallas kernels, mlp_call(): pl.pallas_call(functools.partial(mlp_kernel, blk=blk, planes=planes), gri...  114 us
    pallas_call x1, Pallas kernels, backward_call(): pl.pallas_call(functools.partial(backward_kernel, heads=heads, blk=blk, p...  99.9 us
    pallas_call x1, Pallas kernels, final_call(): pl.pallas_call(functools.partial(final_kernel, planes=planes, blk=blk), o...  47.1 us
    pallas_call x1, Pallas kernels, middle_back_call(): pl.pallas_call(functools.partial(middle_back_kernel, heads=heads), grid=(...  27.8 us

profile of v5, /device:TPU:0, one launch (start us, length us, event | category | flops | bytes accessed | tf_op | source)
XLA Modules:
  0.0 490.6 jit_solution(9649219561804324116)
XLA Ops:
  0.7 0.8 fusion.10
  2.1 0.9 convert_multiply_fusion.2
  3.7 0.7 broadcast_in_dim_reshape.3.gate_ref.head_ref
  5.1 0.7 convert_subtract_fusion
  5.8 1.0 copy.48.keep_ref
  6.8 1.2 broadcast_in_dim.93
  8.1 169.1 %forward.1 = (f32[16,1024]{1,0:T(8,128)}, f32[1024,1]{1,0:T(8,128)}, bf16[32,48,128]{2,1,0:T(8,128)(2,1)}, f32[4,6,1152]{2,1,0:T(8,128)}, f32[8,1152]{1,0:T(8,12...) custom-call(f32[1]{0:T(128)} %bitcast.1.off_ref, ...), custom_call_target="tpu_custom_call" | custom-call | tf_op jit(solution)/shard_map/forward/pallas_call | solution.py:809
  178.9 114.1 %feed_forward.1 = (f32[1024,1152]{1,0:T(8,128)}, f32[1024,1152]{1,0:T(8,128)}, f32[4,1,1152]{2,1,0:T(1,128)}, f32[4,4,1152]{2,1,0:T(4,128)}, f32[144,1152]{1,0:T...) custom-call(bf16[1024,1152]{1,0:T(8,128)(2,1)} %get-tuple-element.66.n2_r, ...), custom_call_target="tpu_custom_call" | custom-call | tf_op jit(solution)/shard_map/feed_forward/pallas_call | solution.py:1210
  293.1 27.8 %middle_backward.1 = (f32[1024,1152]{1,0:T(8,128)}, f32[1024,1152]{1,0:T(8,128)}, bf16[1024,1152]{1,0:T(8,128)(2,1)}, f32[16,1024]{1,0:T(8,128)}, bf16[1152,1152...) custom-call(f32[1024,1152]{1,0:T(8,128)} %get-tuple-element.70.mlp_ref, ...), custom_call_target="tpu_custom_call" | custom-call | tf_op jit(solution)/shard_map/middle_backward/pallas_call | solution.py:1331
  320.8 1.0 reshape.100.mods_ref
  323.7 99.9 %attention_backward.1 = (bf16[1024,3456]{1,0:T(8,128)(2,1)}, f32[3,1,1152]{2,1,0:T(1,128)}, f32[144,1152]{1,0:T(8,128)}, f32[144,1152]{1,0:T(8,128)}, f32[144,76...) custom-call(f32[1]{0:T(128)} %bitcast.1.off_ref, bf16[1024,3456]{1,0:T(8,128)(2,1)} %get-tuple-element.82.qkv_ref, ...), custom_call_target="tpu_custom_call" | custom-call | tf_op jit(solution)/shard_map/attention_backward/pallas_call | solution.py:1021
  423.6 0.8 reduce.6
  425.3 47.1 %last_sums.1 = (f32[36,3456]{1,0:T(8,128)}, f32[36,1152]{1,0:T(8,128)}, f32[88,128]{1,0:T(8,128)}, f32[216,1152]{1,0:T(8,128)}, f32[1,216]{1,0:T(1,128)}, /*inde...) custom-call(f32[1]{0:T(128)} %bitcast.2.single_ref, ...), custom_call_target="tpu_custom_call" | custom-call | tf_op jit(solution)/shard_map/last_sums/pallas_call | solution.py:1535
  472.4 1.6 slice_bitcast_fusion
  474.0 1.5 slice_bitcast_fusion.1
  475.6 1.4 slice_bitcast_fusion.3
  477.0 1.3 slice_bitcast_fusion.2
  478.3 1.2 slice_bitcast_fusion.8
  479.5 1.1 slice_bitcast_fusion.9
  480.6 5.0 %copy.68 = f32[1024,1152]{1,0:T(8,128)} copy(f32[1024,1152]{1,0:T(8,128)} %get-tuple-element.149) | data formatting | bytes 9437184
  485.6 0.9 copy.69
  487.1 0.8 copy.71
  488.6 0.9 copy.73
  489.5 0.9 copy.74
  (78 shorter events, 7.0 us)
Async XLA Ops:
  0.7 176.6 %copy-start = (bf16[1152,32]{0,1:T(8,128)(2,1)S(1)}, bf16[1152,32]{0,1:T(8,128)(2,1)}, u32[]{:S(2)}) copy-start(bf16[1152,32]{0,1:T(8,128)(2,1)} %param.42) | copy-start | bytes 221188
  8.1 169.1 %copy-start.14 = (bf16[32]{0:T(256)(128)(2,1)S(1)}, bf16[32]{0:T(256)(128)(2,1)}, u32[]{:S(2)}) copy-start(bf16[32]{0:T(256)(128)(2,1)} %param.43) | copy-start | bytes 196
  8.1 169.2 %copy-start.13 = (s32[4,32]{1,0:T(4,128)S(1)}, s32[4,32]{1,0:T(4,128)}, u32[]{:S(2)}) copy-start(s32[4,32]{1,0:T(4,128)} %param.27) | copy-start | bytes 1540
  8.1 170.2 %copy-start.11 = (bf16[4608]{0:T(1024)(128)(2,1)S(1)}, bf16[4608]{0:T(1024)(128)(2,1)}, u32[]{:S(2)}) copy-start(bf16[4608]{0:T(1024)(128)(2,1)} %param.37) | copy-start | bytes 27652
  293.1 29.3 %copy-start.7 = (f32[4,4,1152]{2,1,0:T(4,128)S(1)}, f32[4,4,1152]{2,1,0:T(4,128)}, u32[]{:S(2)}) copy-start(f32[4,4,1152]{2,1,0:T(4,128)} %get-tuple-element.93) | copy-start | bytes 221188
  321.8 101.8 %copy-start.5 = (f32[4,8,1152]{2,1,0:T(8,128)}, f32[4,8,1152]{2,1,0:T(8,128)S(1)}, u32[]{:S(2)}) copy-start(f32[4,8,1152]{2,1,0:T(8,128)S(1)} %reshape.100.mods_ref) | copy-start | bytes 442372
  323.7 100.8 %copy-start.10 = (f32[3,1152]{1,0:T(4,128)S(1)}, f32[3,1152]{1,0:T(4,128)}, u32[]{:S(2)}) copy-start(f32[3,1152]{1,0:T(4,128)} %get-tuple-element.91) | copy-start | bytes 41476
  323.7 100.9 %copy-start.9 = (f32[4,1,1152]{2,1,0:T(1,128)S(1)}, f32[4,1,1152]{2,1,0:T(1,128)}, u32[]{:S(2)}) copy-start(f32[4,1,1152]{2,1,0:T(1,128)} %get-tuple-element.92) | copy-start | bytes 55300
  480.6 5.0 %copy-start.2 = (f32[216,1152]{1,0:T(8,128)S(1)}, f32[216,1152]{1,0:T(8,128)}, u32[]{:S(2)}) copy-start(f32[216,1152]{1,0:T(8,128)} %get-tuple-element.105) | copy-start | bytes 2985988
  480.6 6.0 %copy-start.12 = (f32[1,216]{1,0:T(1,128)S(1)}, f32[1,216]{1,0:T(1,128)}, u32[]{:S(2)}) copy-start(f32[1,216]{1,0:T(1,128)} %get-tuple-element.106) | copy-start | bytes 2596
  480.6 6.5 %copy-start.6 = (f32[36,3456]{1,0:T(8,128)S(1)}, f32[36,3456]{1,0:T(8,128)}, u32[]{:S(2)}) copy-start(f32[36,3456]{1,0:T(8,128)} %get-tuple-element.152) | copy-start | bytes 1492996
  480.6 7.3 %copy-start.8 = (f32[36,1152]{1,0:T(8,128)S(1)}, f32[36,1152]{1,0:T(8,128)}, u32[]{:S(2)}) copy-start(f32[36,1152]{1,0:T(8,128)} %get-tuple-element.155) | copy-start | bytes 497668
  480.6 8.0 %copy-start.4 = (f32[288,576]{1,0:T(8,128)S(1)}, f32[288,576]{1,0:T(8,128)}, u32[]{:S(2)}) copy-start(f32[288,576]{1,0:T(8,128)} %get-tuple-element.110) | copy-start | bytes 1990660
  480.6 9.7 %copy-start.1 = (bf16[1152,32]{0,1:T(8,128)(2,1)S(1)}, bf16[1152,32]{0,1:T(8,128)(2,1)}, u32[]{:S(2)}) copy-start(bf16[1152,32]{0,1:T(8,128)(2,1)} %param.42) | copy-start | bytes 221188
  485.6 3.9 copy-start.3

commit v6 on v5

--- a/solution.py
+++ b/solution.py
@@ -116,28 +116,20 @@
     def dev(self, n, z, c):
         return (n, z * 2 + c)
 
-    def barrier(self, every_plane=False):
+    def greet(self):
         sem = pltpu.get_barrier_semaphore()
 
-        def greet(n, z, c):
+        def signal(n, z, c):
             pl.semaphore_signal(sem, inc=1, device_id=self.dev(n, z, c), device_id_type=MESH)
 
-        greet(self.xn, self.z, self.c)
-        greet(self.yn, self.z, self.c)
-        greet(self.n, self.z, 1 - self.c)
-        if every_plane:
-            for k in range(1, self.planes):
-                greet(self.n, lax.rem(self.z + k, self.planes), self.c)
-            pl.semaphore_wait(sem, self.planes + 2)
-            return
-        for step in (-1, 1):
-
-            @pl.when(self.has(step))
-            def _(step=step):
-                greet(self.n, self.z + step, self.c)
-
-        ends = jnp.where(self.z > 0, 1, 0) + jnp.where(self.z < self.planes - 1, 1, 0)
-        pl.semaphore_wait(sem, 3 + ends)
+        signal(self.xn, self.z, self.c)
+        signal(self.yn, self.z, self.c)
+        signal(self.n, self.z, 1 - self.c)
+        for k in range(1, self.planes):
+            signal(self.n, lax.rem(self.z + k, self.planes), self.c)
+
+    def meet(self):
+        pl.semaphore_wait(pltpu.get_barrier_semaphore(), self.planes + 2)
 
     def has(self, step):
         return self.z + step >= 0 if step < 0 else self.z + step < self.planes
@@ -464,7 +456,9 @@
             return carry
 
         lax.fori_loop(1, self.total, signal, 0)
-        pl.semaphore_wait(sem, self.total - 1)
+
+    def meet(self):
+        pl.semaphore_wait(pltpu.get_barrier_semaphore(), self.total - 1)
 
     def copy(self, i):
         other = lax.rem(self.me + i, self.total)
@@ -616,11 +610,12 @@
     ]
     conds = Exchange(place, cond_ref, conds_ref, cond_sems, True)
     mods = Exchange(place, mod_local, mods_s, mod_sems, False)
+    conds.greet()
     rows = proj_shard_ref.shape[0]
     for b in range(3):
         shard_ref[b * rows : (b + 1) * rows, :] = qkv_shard_ref[:, b * d : (b + 1) * d]
     shard_ref[3 * rows : 4 * rows, :] = proj_shard_ref[...]
-    conds.greet()
+    conds.meet()
     weights.run("begin")
     conds.start()
     for src, dst in ((up_t_ref, up_ref), (down_t_ref, down_ref)):
@@ -690,7 +685,24 @@
         g.run(part)
     for part in late[len(late) // 2 :]:
         weights.run(part)
-    groups = spread_out([functools.partial(g.run, part) for g, part in rest[4:]], 2 * nb + heads)
+    at_end = (place.z == 0) | (place.z == planes - 1)
+    count = 2 * nb + heads
+
+    def only(cond, items):
+        def run():
+            @pl.when(cond)
+            def _():
+                for g, part in items:
+                    g.run(part)
+
+        return [run] if items else []
+
+    only(at_end, rest[4:8])[0]()
+    ends = spread_out(rest[8:], count - 2) + [[]] * 2
+    inner = [[]] * 2 + spread_out(rest[4:], count - 2)
+    groups = [
+        only(at_end, ends[i]) + only(jnp.logical_not(at_end), inner[i]) for i in range(count)
+    ]
     mods.arrive()
     for i in range(devices):
         flat_s[:slots, i * width : (i + 1) * width] = mods_s[i, :slots, :width].astype(F32)
@@ -895,7 +907,7 @@
     r = d // devices
     first = planes // 2
     place = Place(planes)
-    place.barrier(True)
+    place.greet()
     slots, rest = rest[: cuts - 1], rest[cuts - 1 :]
     each = 10
     js = list(range(first, planes))
@@ -920,6 +932,8 @@
     ]
     up_steps = scatter_steps(ups)
     chain_steps = [scatter_steps([chain], planes) for chain in chains]
+    kt_sc[...] = qkv_ref[:, d : 2 * d].T
+    place.meet()
     up_steps[0]()
     ends = [-(-width * (m + 1) // hd) for m in range(cuts)]
     queues = [[] for _ in range(heads + 1)]
@@ -935,7 +949,6 @@
         place_steps(steps, ends[m], min(ends[m] + 4 - m, heads), min(ends[m] + 7, heads))
 
     off = off_ref[0]
-    kt_sc[...] = qkv_ref[:, d : 2 * d].T
 
     def body(h, carry, start, end):
         a, mask = head_window(h, hd, d)
@@ -1131,7 +1144,7 @@
     def _():
         for copy in loads(0):
             copy.start()
-        place.barrier(True)
+        place.greet()
         mlp_ref[...] = jnp.zeros_like(mlp_ref)
         gn2_ref[...] = jnp.zeros_like(gn2_ref)
 
@@ -1147,6 +1160,7 @@
         for copy in loads(j + 1):
             copy.start()
 
+    pl.when(j == 0)(place.meet)
     at_steps(early)
     w1 = w1_s[...]
     w2 = w2_s[...]
@@ -1376,10 +1390,16 @@
     ga_ref,
     qkv_grad_ref,
     proj_grad_ref,
-    sum_ref,
+    query_ref,
+    value_ref,
+    proj_ref,
+    b1_ref,
+    b2_ref,
+    token_ref,
     ada_ref,
     ada_bias_ref,
-    router_ref,
+    head_ref,
+    chan_ref,
     logit_ref,
     up_ref,
     down_ref,
@@ -1423,15 +1443,16 @@
             for k, (src, dst) in enumerate(((dqkv_ref, dq_s), (tokens_ref, tok_s), (ga_ref, ga_s)))
         ]
 
+    mods.greet()
     w_load.start()
     for copy in loads(0) + loads(1):
         copy.start()
-    mods.greet()
+    own_mods[...] = jnp.zeros_like(own_mods)
+    mods.meet()
     steps = scatter_steps([chain], planes)
     steps[0]()
     sums.run("begin")
     logits.start()
-    own_mods[...] = jnp.zeros_like(own_mods)
     out = Stream(out_slots, out_sems, grad_ref)
     tables = []
 
@@ -1470,9 +1491,12 @@
         ada_ref[...] = dg(got, conds, TN)[:columns]
         ada_bias_ref[...] = col_sum(got.astype(F32))[:, :columns]
         got = all_logits[...].reshape(devices * rows, -1)
-        router_ref[...] = lax.dot_general(
+        router = lax.dot_general(
             got, conds.astype(F32), TN, precision=HIGHEST, preferred_element_type=F32
         )
+        heads = head_ref.shape[0]
+        head_ref[...] = router[:heads]
+        chan_ref[...] = router[heads : heads + chan_ref.shape[0]]
         logit_ref[...] = col_sum(got)
 
     def local_work():
@@ -1507,7 +1531,12 @@
             part()
     products()
     sums.run("end")
-    sum_ref[...] = jnp.sum(all_sums[...].reshape((8 * planes,) + sum_ref.shape), axis=0)
+    total = jnp.sum(all_sums[...].reshape((8 * planes,) + sums_ref.shape), axis=0)
+    start = 0
+    for to in (query_ref, value_ref, proj_ref, b1_ref, b2_ref, token_ref):
+        stop = start + to.shape[0]
+        to[...] = total[start:stop]
+        start = stop
     last = chain.total()
     r = proj_grad_ref.shape[0]
     ready = done_ref.shape[1]
@@ -1522,7 +1551,7 @@
 
 
 def final_call(
-    single, table, mods, sums, logits, conds, pairs, done, part, dqkv, w, tokens, ga, mod_width, hidden, planes, blk
+    single, table, mods, sums, logits, conds, pairs, done, part, dqkv, w, tokens, ga, mod_width, hidden, ff, heads, groups, planes, blk
 ):
     rows, width = part.shape[3:]
     t, d = tokens.shape
@@ -1537,17 +1566,23 @@
         out_shape=(
             shape((d // devices, 3 * d)),
             shape((d // devices, d)),
-            shape(sums.shape),
+            shape((d // 128, 128)),
+            shape((d // 128, 128)),
+            shape((d // 128, 128)),
+            shape((ff // 128, 128)),
+            shape((d // 128, 128)),
+            shape((d // 128, 128)),
             shape((mod_width, d)),
             shape((1, mod_width)),
-            shape((logits.shape[1], d)),
+            shape((heads, d)),
+            shape((groups, d)),
             shape((1, logits.shape[1])),
             piece,
             piece,
             shape((t, d)),
         ),
         in_specs=[SMEM_SPEC] + [VMEM_SPEC] * 10 + [ANY_SPEC] * 5,
-        out_specs=(VMEM_SPEC,) * 9 + (ANY_SPEC,),
+        out_specs=(VMEM_SPEC,) * 15 + (ANY_SPEC,),
         scratch_shapes=[
             pltpu.VMEM((devices, padded, d), BF),
             pltpu.VMEM(spread + sums.shape, F32),
@@ -1707,10 +1742,16 @@
     (
         g_qkv,
         g_proj,
-        small,
+        g_query,
+        g_value,
+        g_proj_bias,
+        g_b1,
+        g_b2,
+        g_router,
         grad_ada_t,
         grad_ada_bias,
-        router_t,
+        head_t,
+        chan_t,
         logit_sums,
         g_up_t,
         g_down_t,
@@ -1731,14 +1772,17 @@
         ga,
         mod_width,
         fc1_weight.shape[0],
+        hidden,
+        heads,
+        groups,
         planes,
         blk,
     )
-    small = small.reshape(-1)[:length]
     grad_ada_bias = grad_ada_bias[0]
     logit_sums = logit_sums[0]
-    ends = [d, 2 * d, 3 * d, 3 * d + hidden, 4 * d + hidden]
-    g_query, g_value, g_proj_bias, g_b1, g_b2, g_router = jnp.split(small, ends)
+    g_query, g_value, g_proj_bias, g_b1, g_b2, g_router = [
+        x.reshape(-1) for x in (g_query, g_value, g_proj_bias, g_b1, g_b2, g_router)
+    ]
     return (
         output,
         grad_tokens,
@@ -1753,9 +1797,9 @@
         g_b1,
         g_down_t.T,
         g_b2,
-        router_t[:heads].T,
+        head_t.T,
         logit_sums[:heads],
-        router_t[heads : heads + groups].T,
+        chan_t.T,
         logit_sums[heads : heads + groups],
         g_router,
     )

time: 494 us -> 494 us (level)
    unnamed x42 -> x66, local copies, waits for them, and re-layouts: 9.79 us -> 14.7 us
where the time goes in v6:
time: 494 us; the launch traced here: 487 us
  Pallas kernels  455 us (92%)
  local copies, waits for them, and re-layouts  23.3 us (5%)
  other arithmetic  5.53 us (1%)
    pallas_call x1, Pallas kernels, forward_call(): pl.pallas_call(functools.partial(forward_kernel, heads=heads, blk=blk, pl...  167 us
    pallas_call x1, Pallas kernels, mlp_call(): pl.pallas_call(functools.partial(mlp_kernel, blk=blk, planes=planes), gri...  113 us
    pallas_call x1, Pallas kernels, backward_call(): pl.pallas_call(functools.partial(backward_kernel, heads=heads, blk=blk, p...  99.7 us
    pallas_call x1, Pallas kernels, final_call(): pl.pallas_call(functools.partial(final_kernel, planes=planes, blk=blk), o...  47.3 us
    pallas_call x1, Pallas kernels, middle_back_call(): pl.pallas_call(functools.partial(middle_back_kernel, heads=heads), grid=(...  27.8 us
    unnamed x66, local copies, waits for them, and re-layouts  14.7 us

profile of v6, /device:TPU:0, one launch (start us, length us, event | category | flops | bytes accessed | tf_op | source)
XLA Modules:
  0.0 487.3 jit_solution(14179363544212306312)
XLA Ops:
  0.7 0.8 fusion.10
  1.4 0.7 convert_element_type.32
  2.1 0.9 convert_multiply_fusion.2
  3.7 0.7 broadcast_in_dim_reshape.3.gate_ref.head_ref
  5.1 0.7 convert_subtract_fusion
  5.8 1.0 copy.48.keep_ref
  6.8 1.2 broadcast_in_dim.93
  8.1 167.2 %forward.1 = (f32[16,1024]{1,0:T(8,128)}, f32[1024,1]{1,0:T(8,128)}, bf16[32,48,128]{2,1,0:T(8,128)(2,1)}, f32[4,6,1152]{2,1,0:T(8,128)}, f32[8,1152]{1,0:T(8,12...) custom-call(f32[1]{0:T(128)} %bitcast.1.off_ref, ...), custom_call_target="tpu_custom_call" | custom-call | tf_op jit(solution)/shard_map/forward/pallas_call | solution.py:821
  177.0 113.3 %feed_forward.1 = (f32[1024,1152]{1,0:T(8,128)}, f32[1024,1152]{1,0:T(8,128)}, f32[4,1,1152]{2,1,0:T(1,128)}, f32[4,4,1152]{2,1,0:T(4,128)}, f32[144,1152]{1,0:T...) custom-call(bf16[1024,1152]{1,0:T(8,128)(2,1)} %get-tuple-element.72.n2_r, ...), custom_call_target="tpu_custom_call" | custom-call | tf_op jit(solution)/shard_map/feed_forward/pallas_call | solution.py:1224
  290.3 27.8 %middle_backward.1 = (f32[1024,1152]{1,0:T(8,128)}, f32[1024,1152]{1,0:T(8,128)}, bf16[1024,1152]{1,0:T(8,128)(2,1)}, f32[16,1024]{1,0:T(8,128)}, bf16[1152,1152...) custom-call(f32[1024,1152]{1,0:T(8,128)} %get-tuple-element.76.mlp_ref, ...), custom_call_target="tpu_custom_call" | custom-call | tf_op jit(solution)/shard_map/middle_backward/pallas_call | solution.py:1345
  318.1 1.0 reshape.110.mods_ref
  320.2 0.7 select_maximum_fusion.logits_ref
  320.9 99.7 %attention_backward.1 = (bf16[1024,3456]{1,0:T(8,128)(2,1)}, f32[3,1,1152]{2,1,0:T(1,128)}, f32[144,1152]{1,0:T(8,128)}, f32[144,1152]{1,0:T(8,128)}, f32[144,76...) custom-call(f32[1]{0:T(128)} %bitcast.1.off_ref, bf16[1024,3456]{1,0:T(8,128)(2,1)} %get-tuple-element.88.qkv_ref, ...), custom_call_target="tpu_custom_call" | custom-call | tf_op jit(solution)/shard_map/attention_backward/pallas_call | solution.py:1034
  420.6 0.8 reduce.6
  422.4 47.3 %last_sums.1 = (f32[36,3456]{1,0:T(8,128)}, f32[36,1152]{1,0:T(8,128)}, f32[9,128]{1,0:T(8,128)}, f32[9,128]{1,0:T(8,128)}, f32[9,128]{1,0:T(8,128)}, /*index=5*...) custom-call(f32[1]{0:T(128)} %bitcast.2.single_ref, ...), custom_call_target="tpu_custom_call" | custom-call | tf_op jit(solution)/shard_map/last_sums/pallas_call | solution.py:1564
  469.6 1.3 slice_bitcast_fusion
  470.9 1.2 slice_bitcast_fusion.1
  472.1 5.0 %copy.76 = f32[1024,1152]{1,0:T(8,128)} copy(f32[1024,1152]{1,0:T(8,128)} %get-tuple-element.156) | data formatting | bytes 9437184
  477.1 1.0 copy.77
  478.7 0.8 copy.79
  480.7 0.7 copy.82
  481.9 0.9 copy.84
  483.4 0.9 copy.86
  485.5 0.7 copy.89
  (98 shorter events, 9.3 us)
Async XLA Ops:
  0.7 174.6 %copy-start = (bf16[1152,32]{0,1:T(8,128)(2,1)S(1)}, bf16[1152,32]{0,1:T(8,128)(2,1)}, u32[]{:S(2)}) copy-start(bf16[1152,32]{0,1:T(8,128)(2,1)} %param.42) | copy-start | bytes 221188
  8.1 167.2 %copy-start.22 = (bf16[32]{0:T(256)(128)(2,1)S(1)}, bf16[32]{0:T(256)(128)(2,1)}, u32[]{:S(2)}) copy-start(bf16[32]{0:T(256)(128)(2,1)} %param.43) | copy-start | bytes 196
  8.1 167.2 %copy-start.21 = (s32[4,32]{1,0:T(4,128)S(1)}, s32[4,32]{1,0:T(4,128)}, u32[]{:S(2)}) copy-start(s32[4,32]{1,0:T(4,128)} %param.27) | copy-start | bytes 1540
  8.1 168.3 %copy-start.14 = (bf16[4608]{0:T(1024)(128)(2,1)S(1)}, bf16[4608]{0:T(1024)(128)(2,1)}, u32[]{:S(2)}) copy-start(bf16[4608]{0:T(1024)(128)(2,1)} %param.37) | copy-start | bytes 27652
  290.3 29.3 %copy-start.7 = (f32[4,4,1152]{2,1,0:T(4,128)S(1)}, f32[4,4,1152]{2,1,0:T(4,128)}, u32[]{:S(2)}) copy-start(f32[4,4,1152]{2,1,0:T(4,128)} %get-tuple-element.99) | copy-start | bytes 221188
  319.1 101.6 %copy-start.5 = (f32[4,8,1152]{2,1,0:T(8,128)}, f32[4,8,1152]{2,1,0:T(8,128)S(1)}, u32[]{:S(2)}) copy-start(f32[4,8,1152]{2,1,0:T(8,128)S(1)} %reshape.110.mods_ref) | copy-start | bytes 442372
  320.9 100.6 %copy-start.13 = (f32[3,1152]{1,0:T(4,128)S(1)}, f32[3,1152]{1,0:T(4,128)}, u32[]{:S(2)}) copy-start(f32[3,1152]{1,0:T(4,128)} %get-tuple-element.97) | copy-start | bytes 41476
  320.9 100.7 %copy-start.12 = (f32[4,1,1152]{2,1,0:T(1,128)S(1)}, f32[4,1,1152]{2,1,0:T(1,128)}, u32[]{:S(2)}) copy-start(f32[4,1,1152]{2,1,0:T(1,128)} %get-tuple-element.98) | copy-start | bytes 55300
  472.0 5.0 %copy-start.2 = (f32[216,1152]{1,0:T(8,128)S(1)}, f32[216,1152]{1,0:T(8,128)}, u32[]{:S(2)}) copy-start(f32[216,1152]{1,0:T(8,128)} %get-tuple-element.111) | copy-start | bytes 2985988
  472.1 6.0 %copy-start.20 = (f32[1,216]{1,0:T(1,128)S(1)}, f32[1,216]{1,0:T(1,128)}, u32[]{:S(2)}) copy-start(f32[1,216]{1,0:T(1,128)} %get-tuple-element.112) | copy-start | bytes 2596
  472.1 6.6 %copy-start.6 = (f32[36,3456]{1,0:T(8,128)S(1)}, f32[36,3456]{1,0:T(8,128)}, u32[]{:S(2)}) copy-start(f32[36,3456]{1,0:T(8,128)} %get-tuple-element.159) | copy-start | bytes 1492996
  472.1 7.4 %copy-start.19 = (f32[9,128]{1,0:T(8,128)S(1)}, f32[9,128]{1,0:T(8,128)}, u32[]{:S(2)}) copy-start(f32[9,128]{1,0:T(8,128)} %get-tuple-element.114) | copy-start | bytes 13828
  472.1 8.0 %copy-start.18 = (f32[9,128]{1,0:T(8,128)S(1)}, f32[9,128]{1,0:T(8,128)}, u32[]{:S(2)}) copy-start(f32[9,128]{1,0:T(8,128)} %get-tuple-element.115) | copy-start | bytes 13828
  472.1 8.6 %copy-start.8 = (f32[36,1152]{1,0:T(8,128)S(1)}, f32[36,1152]{1,0:T(8,128)}, u32[]{:S(2)}) copy-start(f32[36,1152]{1,0:T(8,128)} %get-tuple-element.162) | copy-start | bytes 497668
  472.1 9.3 %copy-start.17 = (f32[9,128]{1,0:T(8,128)S(1)}, f32[9,128]{1,0:T(8,128)}, u32[]{:S(2)}) copy-start(f32[9,128]{1,0:T(8,128)} %get-tuple-element.117) | copy-start | bytes 13828
  472.1 9.9 %copy-start.4 = (f32[288,576]{1,0:T(8,128)S(1)}, f32[288,576]{1,0:T(8,128)}, u32[]{:S(2)}) copy-start(f32[288,576]{1,0:T(8,128)} %get-tuple-element.118) | copy-start | bytes 1990660
  472.1 14.7 %copy-start.1 = (bf16[1152,32]{0,1:T(8,128)(2,1)S(1)}, bf16[1152,32]{0,1:T(8,128)(2,1)}, u32[]{:S(2)}) copy-start(bf16[1152,32]{0,1:T(8,128)(2,1)} %param.42) | copy-start | bytes 221188
  477.1 5.7 %copy-start.11 = (f32[36,128]{1,0:T(8,128)S(1)}, f32[36,128]{1,0:T(8,128)}, u32[]{:S(2)}) copy-start(f32[36,128]{1,0:T(8,128)} %get-tuple-element.119) | copy-start | bytes 55300
  477.1 6.3 %copy-start.3 = (f32[288,576]{1,0:T(8,128)S(1)}, f32[288,576]{1,0:T(8,128)}, u32[]{:S(2)}) copy-start(f32[288,576]{1,0:T(8,128)} %get-tuple-element.120) | copy-start | bytes 1990660
  477.1 7.2 %copy-start.16 = (f32[9,128]{1,0:T(8,128)S(1)}, f32[9,128]{1,0:T(8,128)}, u32[]{:S(2)}) copy-start(f32[9,128]{1,0:T(8,128)} %get-tuple-element.121) | copy-start | bytes 13828
  477.1 7.8 %copy-start.10 = (f32[16,1152]{1,0:T(8,128)S(1)}, f32[16,1152]{1,0:T(8,128)}, u32[]{:S(2)}) copy-start(f32[16,1152]{1,0:T(8,128)} %get-tuple-element.122) | copy-start | bytes 221188
  477.1 8.4 %copy-start.9 = (f32[32,1152]{1,0:T(8,128)S(1)}, f32[32,1152]{1,0:T(8,128)}, u32[]{:S(2)}) copy-start(f32[32,1152]{1,0:T(8,128)} %get-tuple-element.124) | copy-start | bytes 442372
  477.1 9.1 %copy-start.15 = (f32[9,128]{1,0:T(8,128)S(1)}, f32[9,128]{1,0:T(8,128)}, u32[]{:S(2)}) copy-start(f32[9,128]{1,0:T(8,128)} %get-tuple-element.125) | copy-start | bytes 13828
